TPU v7x, 256 devices: a whole 4x4x8 slice. The times are simulated.
256 devices in a mesh: dp: 16 (over y, x), seq: 2 (over core), tensor: 8 (over z).
Axes of the slice: x: 4, y: 4, z: 8, core: 2. Of those that a mesh axis runs over, the one named last changes fastest.
Arguments:
- query_in: bfloat16 [16, 1024, 4096], P('dp', 'seq', 'tensor'), may hold values from -96 to 96
- key_in: bfloat16 [16, 1024, 4096], P('dp', 'seq', 'tensor'), may hold values from -4 to 4
- value_in: bfloat16 [16, 1024, 4096], P('dp', 'seq', 'tensor'), may hold values from -12 to 12
- attn_grad: bfloat16 [16, 1024, 4096], P('dp', 'seq', 'tensor'), may hold values from -6 to 6
- out_grad: bfloat16 [16, 1024, 4096], P('dp', 'seq', 'tensor'), may hold values from -1600 to 1600
- carried_error: float32 [16, 16, 256, 4096], P('dp', 'seq', None, 'tensor'), may hold values from -12 to 12
- lengths: int32 [16, 4], P('dp'), may hold values from 1 to 512, 1024 in all within a row
Outputs:
- d_queries: bfloat16 [16, 1024, 4096], P('dp', 'seq', 'tensor')
- d_keys: bfloat16 [16, 1024, 4096], P('dp', 'seq', 'tensor')
- d_values: bfloat16 [16, 1024, 4096], P('dp', 'seq', 'tensor')
- level_sums: float32 [16, 256, 4096], P('seq', 'dp', 'tensor')
- block_scale: float32 [16, 4096], P('seq', 'tensor')
Inputs may be any that keep to these rules, and one draw needn't show every extreme that they name: Each row holds 4 image lengths that sum to 1024; one of them is exactly 512.
All inputs are finite; a program needn't handle non-finite values.
Results may differ from a plain program's by a relative error of at most 0.03.
Values may be sent and summed in bfloat16 or wider, within the bound.
No kernel may reach another device: no remote copies, remote signals or barrier semaphores. Data moves between devices by JAX's collectives and lax.ppermute only.
A program may use at most 64 MiB of HBM per device.

v0:
```python
import math

import jax
import jax.numpy as jnp
from jax import lax
from jax.sharding import PartitionSpec as P

HEAD_DIM = 128


NEG_FILL = -1e30


def rounded(values):
    return lax.optimization_barrier(values.astype(jnp.bfloat16)).astype(jnp.float32)


def image_index(length_row, row_count):
    image_ends = jnp.cumsum(length_row)
    positions = jnp.arange(row_count, dtype=jnp.int32)
    return jnp.sum(
        (positions[:, None] >= image_ends[None, :]).astype(jnp.int32), axis=1, dtype=jnp.int32
    )


def attend_block(
    query_rows,
    grad_rows,
    query_ids,
    key_rows,
    value_rows,
    key_ids,
    part_rows,
    key_terms,
    value_terms,
):
    row_count, head_count, head_depth = query_rows.shape
    key_count = key_rows.shape[0]
    key_width = min(512, key_count)
    key_blocks = key_count // key_width
    inverse = 1.0 / math.sqrt(head_depth)
    lowest = query_ids[0]
    highest = query_ids[row_count - 1]
    part_count = row_count // part_rows

    def pieces(block_index):
        first_key = block_index * key_width
        key_part = lax.dynamic_slice_in_dim(key_rows, first_key, key_width, 0)
        value_part = lax.dynamic_slice_in_dim(value_rows, first_key, key_width, 0)
        id_part = lax.dynamic_slice_in_dim(key_ids, first_key, key_width, 0)
        scores = (
            jnp.einsum("qhd,khd->hqk", query_rows, key_part, preferred_element_type=jnp.float32)
            * inverse
        )
        inside = (query_ids[:, None] == id_part[None, :])[None, :, :]
        return (key_part, value_part, scores, inside)

    def touches(block_index):
        first_key = block_index * key_width
        return jnp.logical_and(
            key_ids[first_key + key_width - 1] >= lowest, key_ids[first_key] <= highest
        )

    def first_pass(block_index, running):

        def first_update(pair_state):
            peak_now, total_sum = pair_state
            scores, inside = pieces(block_index)[2:]
            block_peak = jnp.max(jnp.where(inside, scores, NEG_FILL), axis=2)
            new_peak = jnp.maximum(peak_now, block_peak)
            added = jnp.sum(jnp.where(inside, jnp.exp(scores - new_peak[:, :, None]), 0.0), axis=2)
            return (new_peak, total_sum * jnp.exp(peak_now - new_peak) + added)

        return lax.cond(touches(block_index), first_update, lambda pair_state: pair_state, running)

    start_state = (
        jnp.full((head_count, row_count), NEG_FILL, jnp.float32),
        jnp.zeros((head_count, row_count), jnp.float32),
    )
    peak_now, total_sum = lax.fori_loop(0, key_blocks, first_pass, start_state)
    log_total = peak_now + jnp.log(total_sum)

    def second_pass(block_index, summed):

        def second_update(partial_value):
            value_part, scores, inside = pieces(block_index)[1:]
            prob_bf = jnp.where(inside, jnp.exp(scores - log_total[:, :, None]), 0.0).astype(
                jnp.bfloat16
            )
            return partial_value + jnp.einsum(
                "hqk,khd->qhd", prob_bf, value_part, preferred_element_type=jnp.float32
            )

        return lax.cond(
            touches(block_index), second_update, lambda partial_value: partial_value, summed
        )

    attended = lax.fori_loop(
        0, key_blocks, second_pass, jnp.zeros((row_count, head_count, head_depth), jnp.float32)
    ).astype(jnp.bfloat16)
    row_delta = jnp.sum(grad_rows.astype(jnp.float32) * attended.astype(jnp.float32), axis=2).T

    def third_pass(block_index, grads_state):

        def third_update(inner_state):
            query_grad, key_sums, value_sums = inner_state
            key_part, value_part, scores, inside = pieces(block_index)
            weights = jnp.where(inside, jnp.exp(scores - log_total[:, :, None]), 0.0)
            prob_bf = weights.astype(jnp.bfloat16)
            grad_probs = jnp.einsum(
                "qhd,khd->hqk", grad_rows, value_part, preferred_element_type=jnp.float32
            )
            grad_scores = (weights * (grad_probs - row_delta[:, :, None]) * inverse).astype(
                jnp.bfloat16
            )
            query_grad = query_grad + jnp.einsum(
                "hqk,khd->qhd", grad_scores, key_part, preferred_element_type=jnp.float32
            )
            split_scores = grad_scores.reshape(head_count, part_count, part_rows, key_width)
            split_probs = prob_bf.reshape(head_count, part_count, part_rows, key_width)
            split_queries = query_rows.reshape(part_count, part_rows, head_count, head_depth)
            split_grads = grad_rows.reshape(part_count, part_rows, head_count, head_depth)
            key_piece = jnp.sum(
                rounded(
                    jnp.einsum(
                        "hsqk,sqhd->skhd",
                        split_scores,
                        split_queries,
                        preferred_element_type=jnp.float32,
                    )
                ),
                axis=0,
            )
            value_piece = jnp.sum(
                rounded(
                    jnp.einsum(
                        "hsqk,sqhd->skhd",
                        split_probs,
                        split_grads,
                        preferred_element_type=jnp.float32,
                    )
                ),
                axis=0,
            )
            first_key = block_index * key_width
            key_sums = lax.dynamic_update_slice_in_dim(
                key_sums,
                lax.dynamic_slice_in_dim(key_sums, first_key, key_width, 0) + key_piece,
                first_key,
                0,
            )
            value_sums = lax.dynamic_update_slice_in_dim(
                value_sums,
                lax.dynamic_slice_in_dim(value_sums, first_key, key_width, 0) + value_piece,
                first_key,
                0,
            )
            return (query_grad, key_sums, value_sums)

        return lax.cond(
            touches(block_index), third_update, lambda inner_state: inner_state, grads_state
        )

    start_grads = (
        jnp.zeros((row_count, head_count, head_depth), jnp.float32),
        key_terms,
        value_terms,
    )
    query_grad, key_terms, value_terms = lax.fori_loop(0, key_blocks, third_pass, start_grads)
    return (attended, query_grad, key_terms, value_terms)


def body(query_in, key_in, value_in, attn_grad, out_grad, carried_error, lengths):
    row_count = query_in.shape[1]
    head_depth = HEAD_DIM
    head_count = query_in.shape[2] // head_depth
    seq_count = lax.axis_size("seq")
    row_length = row_count * seq_count
    all_ids = image_index(lengths[0], row_length)
    cube_shape = (row_count, head_count, head_depth)
    query_cube = query_in[0].reshape(cube_shape)
    key_cube = key_in[0].reshape(cube_shape)
    value_cube = value_in[0].reshape(cube_shape)
    grad_cube = attn_grad[0].reshape(cube_shape)
    row_keys, row_values = (
        lax.all_gather(key_cube, "seq", axis=0, tiled=True),
        lax.all_gather(value_cube, "seq", axis=0, tiled=True),
    )
    own_ids = lax.dynamic_slice_in_dim(all_ids, lax.axis_index("seq") * row_count, row_count, 0)
    empty_terms = jnp.zeros((row_length, head_count, head_depth), jnp.float32)
    attended, query_grad, key_terms, value_terms = attend_block(
        query_cube,
        grad_cube,
        own_ids,
        row_keys,
        row_values,
        all_ids,
        row_count,
        empty_terms,
        empty_terms,
    )
    key_grad, value_grad = (
        lax.psum_scatter(
            key_terms.astype(jnp.bfloat16), "seq", scatter_dimension=0, tiled=True
        ).astype(jnp.float32),
        lax.psum_scatter(
            value_terms.astype(jnp.bfloat16), "seq", scatter_dimension=0, tiled=True
        ).astype(jnp.float32),
    )
    query_grad = query_grad.astype(jnp.bfloat16)
    key_grad = key_grad.astype(jnp.bfloat16)
    value_grad = value_grad.astype(jnp.bfloat16)
    flat_width = head_count * head_depth
    attend_flat = attended.reshape(row_count, flat_width)
    full_grad = lax.all_gather(out_grad[0], "tensor", axis=1, tiled=True)
    block_dev = carried_error.shape[1]
    block_size = carried_error.shape[2]
    weight_grad = lax.psum_scatter(
        rounded(
            lax.dot_general(
                full_grad, attend_flat, (((0,), (0,)), ((), ())), preferred_element_type=jnp.float32
            )
        ).astype(jnp.bfloat16),
        "seq",
        scatter_dimension=0,
        tiled=True,
    ).astype(jnp.float32)
    corrected = weight_grad.reshape(block_dev, block_size, flat_width) + carried_error[0]
    block_peaks = lax.pmax(jnp.max(jnp.abs(corrected), axis=1), "dp")
    block_scale = (block_peaks + 1e-06) / 7.0
    levels = rounded(corrected / block_scale[:, None, :])
    level_sums = lax.psum_scatter(
        levels.astype(jnp.bfloat16), "dp", scatter_dimension=1, tiled=True
    ).astype(jnp.float32)
    out_shape = (1, row_count, flat_width)
    return (
        query_grad.reshape(out_shape),
        key_grad.reshape(out_shape),
        value_grad.reshape(out_shape),
        level_sums,
        block_scale,
    )


def solution(mesh):
    in_specs = (
        P("dp", "seq", "tensor"),
        P("dp", "seq", "tensor"),
        P("dp", "seq", "tensor"),
        P("dp", "seq", "tensor"),
        P("dp", "seq", "tensor"),
        P("dp", "seq", None, "tensor"),
        P("dp", None),
    )
    out_specs = (
        P("dp", "seq", "tensor"),
        P("dp", "seq", "tensor"),
        P("dp", "seq", "tensor"),
        P("seq", "dp", "tensor"),
        P("seq", "tensor"),
    )
    return jax.shard_map(body, mesh=mesh, in_specs=in_specs, out_specs=out_specs, check_vma=False)
```

profile of v0, /device:TPU:2, one launch (start us, length us, event | category | flops | bytes accessed | tf_op | source)
XLA Modules:
  0.0 319.9 jit_solution(12545661453598773802)
XLA Ops:
  7.2 2.1 copy.52
  9.4 2.0 copy.56
  15.6 12.1 %all-gather.5.cloned.1.call-done = bf16[1024,4,128]{0,2,1:T(8,128)(2,1)} async-done(((bf16[512,4,128]{0,2,1:T(8,128)(2,1)}), bf16[1024,4,128]{0,2,1:T(8,128)(2,1)}) %all-gather.5.cloned.1.call-update) | async-done | bytes 1048592 | tf_op jit(solution)/shard_map/all_gather | solution.py:186
  27.7 1.6 copy.60
  29.4 10.9 %while.60 = (s32[]{:T(128)}, f32[4,512]{1,0:T(4,128)S(1)}, f32[4,512]{1,0:T(4,128)S(1)}, s32[1024]{0:T(1024)S(1)}, s32[]{:T(128)}, /*index=5*/s32[]{:T(128)}, s3...) while((s32[]{:T(128)}, f32[4,512]{1,0:T(4,128)S(1)}, ...), condition=%wide.region_7.8_spmd, body=%wide.region_2.7_spmd.sunk | while | flops 276041728 | bytes 10338745 | solution.py:80
  32.6 2.2 conditional.6
  38.1 2.2 conditional.6
  40.3 5.5 %all-gather.7.cloned.1.call-done = bf16[1024,4,128]{0,2,1:T(8,128)(2,1)} async-done(((bf16[512,4,128]{0,2,1:T(8,128)(2,1)}), bf16[1024,4,128]{0,2,1:T(8,128)(2,1)}) %all-gather.7.cloned.1.call-update) | async-done | bytes 1048592 | tf_op jit(solution)/shard_map/all_gather | solution.py:187
  45.9 11.9 %while.61 = (s32[]{:T(128)}, f32[512,4,128]{0,2,1:T(8,128)S(1)}, s32[1024]{0:T(1024)S(1)}, s32[]{:T(128)}, s32[]{:T(128)}, /*index=5*/bf16[1024,4,128]{0,2,1:T(8...) while((s32[]{:T(128)}, f32[512,4,128]{0,2,1:T(8,128)S(1)}, ...), condition=%wide.region_11.12_spmd, body=%wide.region_8.11_spmd.sunk | while | flops 541589504 | bytes 4212133 | solution.py:98
  49.1 2.7 conditional.7
  49.5 2.4 fusion.10
  55.1 2.7 conditional.7
  55.4 2.4 fusion.10
  58.7 45.0 %all-gather.9.cloned.1.call-done = bf16[1,512,4096]{2,1,0:T(8,128)(2,1)} async-done(((bf16[1,512,512]{2,1,0:T(8,128)(2,1)}), bf16[1,512,4096]{2,1,0:T(8,128)(2,1)}) %all-gather.9.cloned.1.call-update) | async-done | bytes 4194320 | tf_op jit(solution)/shard_map/all_gather | solution.py:215
  103.7 6.7 %fusion.48 = bf16[4096,512]{0,1:T(8,128)(2,1)} fusion(bf16[512,512]{0,1:T(8,128)(2,1)} %bitcast.120, bf16[1,512,4096]{2,1,0:T(8,128)(2,1)} %all-gather.9.cloned.1.call-done), kind=kOutput, calls=%fused_computation.55 | convolution fusion | flops 2149580800 | bytes 8912896 | tf_op jit(solution)/shard_map/dot_general | solution.py:220
  111.7 2.3 copy.62
  117.0 30.1 %while.62 = (s32[]{:T(128)}, f32[512,4,128]{0,2,1:T(8,128)S(1)}, f32[1024,4,128]{2,0,1:T(8,128)}, f32[1024,4,128]{2,0,1:T(8,128)}, s32[1024]{0:T(1024)S(1)}, /*i...) while((s32[]{:T(128)}, f32[512,4,128]{0,2,1:T(8,128)S(1)}, ...), condition=%wide.region_16.17_spmd, body=%wide.region_13.16_spmd.sunk | while | flops 1355808768 | bytes 44335792 | solution.py:169
  120.2 11.9 %conditional.8 = ((f32[512,4,128]{0,2,1:T(8,128)S(1)}, f32[1024,4,128]{2,0,1:T(8,128)}, f32[1024,4,128]{2,0,1:T(8,128)})) conditional(s32[]{:T(128)} %convert_element_type.160, (f32[512,4,128]{0,2,1:T(8,128)S(1)}, f32[1024,4,128]{2,0,1:T(8,128)}, f32[1024,4,128]{2,0,1:T(8,128)}) %tuple.184, (s32[]{:T(128)}, bf16[1024,4,128]{2,0,1:T(8,128)(2,1)S(1)}, ...), branch_computations={%region_14.14_spmd, %region_15.15_spmd} | conditional | flops 1355808768 | bytes 44335312 | solution.py:160
  121.5 2.0 reshape.151
  129.0 3.1 fusion.35
  135.4 11.7 %conditional.8 = ((f32[512,4,128]{0,2,1:T(8,128)S(1)}, f32[1024,4,128]{2,0,1:T(8,128)}, f32[1024,4,128]{2,0,1:T(8,128)})) conditional(s32[]{:T(128)} %convert_element_type.160, (f32[512,4,128]{0,2,1:T(8,128)S(1)}, f32[1024,4,128]{2,0,1:T(8,128)}, f32[1024,4,128]{2,0,1:T(8,128)}) %tuple.184, (s32[]{:T(128)}, bf16[1024,4,128]{2,0,1:T(8,128)(2,1)S(1)}, ...), branch_computations={%region_14.14_spmd, %region_15.15_spmd} | conditional | flops 1355808768 | bytes 44335312 | solution.py:160
  136.6 2.0 reshape.151
  141.0 1.6 fusion.19
  144.0 3.1 fusion.35
  147.1 2.7 convert_element_type.122
  149.9 2.8 convert_element_type.121
  152.8 4.2 %copy.72 = f32[2048,512]{1,0:T(8,128)} copy(bf16[2048,512]{0,1:T(8,128)(2,1)} %reduce-scatter.9.cloned.1.call-done) | data formatting | bytes 6291456 | tf_op jit(solution)/shard_map/reshape | solution.py:228
  157.0 4.8 %abs_reduce_fusion = f32[8,512]{1,0:T(8,128)S(1)} fusion(f32[1,8,256,512]{3,2,1,0:T(8,128)} %param.24, f32[2048,512]{1,0:T(8,128)} %copy.72), kind=kLoop, calls=%fused_computation.59 | loop fusion | flops 3141632 | bytes 8404992 | tf_op jit(solution)/shard_map/reduce_max | solution.py:229
  161.7 66.7 %pmax.7 = f32[8,512]{1,0:T(8,128)S(1)} all-reduce(f32[8,512]{1,0:T(8,128)S(1)} %abs_reduce_fusion), channel_id=1, replica_groups=mesh['dp'=16,'seq'=2,'tensor'=8] {'dp'}, use_global_device_ids=true, to_apply=%region_21.22 | all-reduce | flops 4096 | bytes 32768 | tf_op jit(solution)/shard_map/pmax | solution.py:229
  228.4 5.9 %divide_convert_fusion = bf16[8,256,512]{2,1,0:T(8,128)(2,1)} fusion(f32[8,512]{1,0:T(8,128)S(1)} %add_multiply_fusion, f32[1,8,256,512]{3,2,1,0:T(8,128)} %param.24, f32[2048,512]{1,0:T(8,128)} %copy.72), kind=kLoop, calls=%fused_computation.58 | loop fusion | flops 3145728 | bytes 10502144 | tf_op jit(solution)/shard_map/convert_element_type | solution.py:15
  240.3 71.1 %reduce-scatter.11.cloned.1.call-done = bf16[8,16,512]{2,1,0:T(8,128)(2,1)} async-done(((bf16[8,256,512]{2,1,0:T(8,128)(2,1)}), bf16[8,16,512]{2,1,0:T(8,128)(2,1)}) %reduce-scatter.11.cloned.1.call-update) | async-done | bytes 131088 | tf_op jit(solution)/shard_map/reduce_scatter | solution.py:232
  311.4 1.6 convert_element_type.126
  (101 shorter events, 36.0 us)
Async XLA Ops:
  7.2 7.5 %copy-start.1 = (bf16[1,512,512]{2,1,0:T(8,128)(2,1)S(1)}, bf16[1,512,512]{2,1,0:T(8,128)(2,1)}, u32[]{:S(2)}) copy-start(bf16[1,512,512]{2,1,0:T(8,128)(2,1)} %param.22) | copy-start | bytes 1572868
  7.2 20.6 %all-gather.5.cloned.1.call-start = ((), (), s32[]{:S(2)}) async-start(), calls=%async_computation.4 | async-start | bytes 1572864 | tf_op jit(solution)/shard_map/all_gather | solution.py:186
  9.3 36.5 %all-gather.7.cloned.1.call-start = ((), (), s32[]{:S(2)}) async-start(), calls=%async_computation.5 | async-start | bytes 1572864 | tf_op jit(solution)/shard_map/all_gather | solution.py:187
  11.5 92.3 %all-gather.9.cloned.1.call-start = ((), (), s32[]{:S(2)}) async-start(), calls=%async_computation.10 | async-start | bytes 4718592 | tf_op jit(solution)/shard_map/all_gather | solution.py:215
  12.2 140.6 %reduce-scatter.9.cloned.1.call-start = ((), (), s32[]{:S(2)}) async-start(), calls=%async_computation.8 | async-start | bytes 6291456 | tf_op jit(solution)/shard_map/reduce_scatter | solution.py:218
  110.4 125.0 %reduce-scatter.7.cloned.1.call-start = ((), (), s32[]{:S(2)}) async-start(), calls=%async_computation.7 | async-start | bytes 1572864 | tf_op jit(solution)/shard_map/reduce_scatter | solution.py:206
  110.6 6.4 %copy-start = (bf16[1,512,512]{2,1,0:T(8,128)(2,1)S(1)}, bf16[1,512,512]{2,1,0:T(8,128)(2,1)}, u32[]{:S(2)}) copy-start(bf16[1,512,512]{2,1,0:T(8,128)(2,1)} %param.19) | copy-start | bytes 1572868
  123.4 1.2 copy-start.3
  124.6 1.3 copy-start.4
  124.6 1.4 copy-start.5
  126.0 1.6 copy-start.2
  138.6 1.0 copy-start.3
  139.6 1.2 copy-start.4
  139.6 1.4 copy-start.5
  141.0 1.6 copy-start.2
  149.8 88.0 %reduce-scatter.5.cloned.1.call-start = ((), (), s32[]{:S(2)}) async-start(), calls=%async_computation.6 | async-start | bytes 1572864 | tf_op jit(solution)/shard_map/reduce_scatter | solution.py:203
  152.7 158.7 %reduce-scatter.11.cloned.1.call-start = ((), (), s32[]{:S(2)}) async-start(), calls=%async_computation.9 | async-start | bytes 2228224 | tf_op jit(solution)/shard_map/reduce_scatter | solution.py:232
  228.4 5.9 %copy-start.6 = (f32[8,512]{1,0:T(8,128)}, f32[8,512]{1,0:T(8,128)S(1)}, u32[]{:S(2)}) copy-start(f32[8,512]{1,0:T(8,128)S(1)} %add_multiply_fusion) | copy-start | bytes 49156
Sparse Core Ops, SparseCore 0:
  10.4 17.3 all-gather.4
  30.1 15.6 all-gather.6
  47.6 56.1 all-gather.8
  110.5 16.0 reduce-scatter.8
  150.0 11.2 reduce-scatter.6
  163.6 15.1 reduce-scatter.4
  234.5 76.9 reduce-scatter.10
where the time goes:
time: 321 us; the launch traced here: 320 us
  waiting for transfers between devices  135 us (42%)
  blocking collectives  66.7 us (21%)
  local copies, waits for them, and re-layouts  36.2 us (11%)
  other arithmetic  29.2 us (9%)
  matrix products  22.4 us (7%)
  loops' own time  16.1 us (5%)
  between operations  14.3 us (4%)
    reduce_scatter x1, waiting for transfers between devices, body(): lax.psum_scatter(levels.astype(jnp.bfloat16), 'dp', scatter_dimension=1,...  71.1 us
    pmax x1, blocking collectives, body(): block_peaks = lax.pmax(jnp.max(jnp.abs(corrected), axis=1), 'dp')  66.7 us
    all_gather x1, waiting for transfers between devices, body(): full_grad = lax.all_gather(out_grad[0], 'tensor', axis=1, tiled=True)  45 us
    all_gather x1, waiting for transfers between devices, body(): lax.all_gather(key_cube, 'seq', axis=0, tiled=True)  12.1 us
    dot_general x1, matrix products, body(): lax.dot_general(full_grad, attend_flat, (((0,), (0,)), ((), ())), preferr...  6.65 us
  transfers between devices with their start and end apart: 7, of which 4 were waited for; matrix products, arithmetic and copies ran while one was open for 24% of the time, Pallas kernels for 0%

commit v1 on v0

v1 whole, which is shorter than its diff:
```python
import functools
import math

import jax
import jax.numpy as jnp
from jax import lax
from jax.experimental import pallas as pl
from jax.experimental.pallas import tpu as pltpu
from jax.sharding import PartitionSpec as P

HEAD_DIM = 128
NEG_FILL = -1e30
F32 = jnp.float32
BF16 = jnp.bfloat16
VMEM_LIMIT = 48 * 2**20


def dot_on(a, b, a_dim, b_dim):
    return lax.dot_general(a, b, (((a_dim,), (b_dim,)), ((), ())), preferred_element_type=F32)


def attention_kernel(
    lengths_ref, place_ref, q_ref, ko_ref, kp_ref, vo_ref, vp_ref, g_ref,
    att_ref, dq_ref, dko_ref, dkp_ref, dvo_ref, dvp_ref,
    ids_ref, dk_acc, dv_acc, *, tile,
):
    rows = q_ref.shape[0]
    inverse = 1.0 / math.sqrt(HEAD_DIM)
    to_exp2 = inverse * math.log2(math.e)
    own = place_ref[0] * rows
    other = rows - own

    def ids(positions):
        found = jnp.zeros(positions.shape, jnp.int32)
        end = jnp.int32(0)
        for image in range(4):
            end = end + lengths_ref[image]
            found = found + (positions >= end).astype(jnp.int32)
        return found

    @pl.when(pl.program_id(0) == 0)
    def _():
        positions = lax.broadcasted_iota(jnp.int32, (rows, 128), 0)
        ids_ref[:rows, :] = ids(positions + own)
        ids_ref[rows:, :] = ids(positions + other)

    k = jnp.concatenate([ko_ref[...], kp_ref[...]], 0)
    v = jnp.concatenate([vo_ref[...], vp_ref[...]], 0)
    k_t, v_t = k.T, v.T
    for i in range(rows // tile):
        part = slice(i * tile, (i + 1) * tile)
        q, g = q_ref[part, :], g_ref[part, :]
        query_ids = ids(lax.broadcasted_iota(jnp.int32, (8, tile), 1) + (own + i * tile))[:1]
        key_ids = jnp.concatenate([ids_ref[...]] * (tile // 128), 1)
        scores = jnp.where(key_ids == query_ids, dot_on(k, q, 1, 1) * to_exp2, NEG_FILL)
        peak = jnp.max(scores, axis=0, keepdims=True)
        raised = jnp.exp2(scores - peak)
        weights = raised * (1.0 / jnp.sum(raised, axis=0, keepdims=True))
        prob = weights.astype(BF16)
        att_t = dot_on(v_t, prob, 1, 0).astype(BF16).astype(F32)
        att_ref[part, :] = att_t.T.astype(BF16)
        delta = jnp.sum(g.astype(F32).T * att_t, axis=0, keepdims=True)
        grad_probs = dot_on(v, g, 1, 1)
        grad_scores = (weights * ((grad_probs - delta) * inverse)).astype(BF16)
        dq_ref[part, :] = dot_on(k_t, grad_scores, 1, 0).T.astype(BF16)
        dk = dot_on(grad_scores, q, 1, 0)
        dv = dot_on(prob, g, 1, 0)
        if i == 0:
            dk_acc[...] = dk
            dv_acc[...] = dv
        else:
            dk_acc[...] += dk
            dv_acc[...] += dv
    dko_ref[...] = dk_acc[:rows].astype(BF16)
    dkp_ref[...] = dk_acc[rows:].astype(BF16)
    dvo_ref[...] = dv_acc[:rows].astype(BF16)
    dvp_ref[...] = dv_acc[rows:].astype(BF16)


def attention(lengths, place, q, ko, kp, vo, vp, g):
    rows, width = q.shape
    heads = width // HEAD_DIM
    spec = pl.BlockSpec((rows, HEAD_DIM), lambda i, *_: (0, i))
    return pl.pallas_call(
        functools.partial(attention_kernel, tile=256),
        grid_spec=pltpu.PrefetchScalarGridSpec(
            num_scalar_prefetch=2,
            grid=(heads,),
            in_specs=[spec] * 6,
            out_specs=[spec] * 6,
            scratch_shapes=[
                pltpu.VMEM((2 * rows, 128), jnp.int32),
                pltpu.VMEM((2 * rows, HEAD_DIM), F32),
                pltpu.VMEM((2 * rows, HEAD_DIM), F32),
            ],
        ),
        out_shape=[jax.ShapeDtypeStruct((rows, width), BF16)] * 6,
        compiler_params=pltpu.CompilerParams(vmem_limit_bytes=VMEM_LIMIT),
        cost_estimate=pl.CostEstimate(
            flops=24 * rows * rows * width,
            bytes_accessed=24 * rows * width,
            transcendentals=2 * rows * rows * heads,
        ),
        name="attention",
    )(lengths, place, q, ko, kp, vo, vp, g)


def weight_kernel(place_ref, own_ref, recv_ref, att_ref, att_peer_ref, carried_ref, *refs, dp_count):
    *peak_refs, out_ref, peak_ref = refs
    step = pl.program_id(0)
    corrected = (
        dot_on(own_ref[...], att_ref[...], 0, 0)
        + dot_on(recv_ref[...], att_peer_ref[...], 0, 0)
        + carried_ref[0]
    )
    share = corrected.shape[0] // dp_count
    peak_ref[pl.ds(step, 1), :] = jnp.max(jnp.abs(corrected), axis=0, keepdims=True)
    rounded = corrected.astype(BF16)
    place = pl.ds(pl.multiple_of(step * share, share), share)
    for dest in range(dp_count):
        out_ref[dest, place, :] = rounded[dest * share : (dest + 1) * share]
    if peak_refs:

        @pl.when(step == 1)
        def _():
            peaks = jnp.concatenate([peak_ref[...]] + [ref[...] for ref in peak_refs], 0)
            high = peaks.astype(BF16).astype(F32)
            both = jnp.concatenate([high, peaks - high], 0).astype(BF16)
            for dest in range(dp_count):
                out_ref[dest, 2 * share :, :] = both


def weight_block(place, own, recv, att, att_peer, carried, peaks, dp_count):
    rows, width = att.shape
    block = carried.shape[1]
    share = block // dp_count
    out_rows = 2 * share + (16 if peaks else 0)
    whole = lambda i, *_: (0, 0)
    half = lambda i, *_: (0, i)
    return pl.pallas_call(
        functools.partial(weight_kernel, dp_count=dp_count),
        grid_spec=pltpu.PrefetchScalarGridSpec(
            num_scalar_prefetch=1,
            grid=(2,),
            in_specs=[
                pl.BlockSpec((rows, block), half),
                pl.BlockSpec((rows, block), half),
                pl.BlockSpec((rows, width), whole),
                pl.BlockSpec((rows, width), whole),
                pl.BlockSpec((1, block, width), lambda i, ref: (2 * ref[0] + i, 0, 0)),
            ]
            + [pl.BlockSpec((2, width), whole) for _ in peaks],
            out_specs=[
                pl.BlockSpec((dp_count, out_rows, width), lambda i, *_: (0, 0, 0)),
                pl.BlockSpec((2, width), whole),
            ],
        ),
        out_shape=[
            jax.ShapeDtypeStruct((dp_count, out_rows, width), BF16),
            jax.ShapeDtypeStruct((2, width), F32),
        ],
        compiler_params=pltpu.CompilerParams(vmem_limit_bytes=VMEM_LIMIT),
        cost_estimate=pl.CostEstimate(
            flops=8 * rows * block * width, bytes_accessed=16 * rows * width, transcendentals=0
        ),
        name="weight_block",
    )(place, own, recv, att, att_peer, carried, *peaks)


def finish_kernel(place_ref, last_ref, *refs):
    *sum_refs, levels_ref, scale_ref = refs
    share = levels_ref.shape[1]
    pairs = len(sum_refs) + 1
    head = 2 * share
    peaks = jnp.max(
        last_ref[:, head : head + 8, :].astype(F32) + last_ref[:, head + 8 : head + 16, :].astype(F32),
        axis=0,
    )
    scale = (peaks + 1e-6) / 7.0
    for pair in range(pairs):
        if pair == 0:
            total = jnp.sum(last_ref[:, :head, :].astype(F32), axis=0)
        else:
            total = sum_refs[pair - 1][...]
        for half in range(2):
            block = 2 * place_ref[pair] + half
            row = scale[2 * pair + half : 2 * pair + half + 1]
            scale_ref[pl.ds(block, 1), :] = row
            levels_ref[block] = total[half * share : (half + 1) * share] / row


def finish(places, last, sums):
    width = last.shape[2]
    share = sums[0].shape[0] // 2
    blocks = 2 * (len(sums) + 1)
    return pl.pallas_call(
        finish_kernel,
        in_specs=[pl.BlockSpec(memory_space=pltpu.SMEM)]
        + [pl.BlockSpec(memory_space=pltpu.VMEM)] * (1 + len(sums)),
        out_specs=[pl.BlockSpec(memory_space=pltpu.VMEM)] * 2,
        out_shape=[
            jax.ShapeDtypeStruct((blocks, share, width), F32),
            jax.ShapeDtypeStruct((blocks, width), F32),
        ],
        compiler_params=pltpu.CompilerParams(vmem_limit_bytes=VMEM_LIMIT),
        name="finish",
    )(places, last, *sums)


def body(query_in, key_in, value_in, attn_grad, out_grad, carried_error, lengths):
    dp_count = lax.axis_size("dp")
    z_count = lax.axis_size("tensor")
    seq = lax.axis_index("seq")
    z = lax.axis_index("tensor")
    up = [(i, (i + 1) % z_count) for i in range(z_count)]
    down = [(i, (i - 1) % z_count) for i in range(z_count)]
    swap = [(0, 1), (1, 0)]

    def peer(array):
        return lax.ppermute(array, "seq", swap)

    own = out_grad[0]
    half = own.shape[0] // 2
    from_down, from_up = [own], [own]
    for _ in range(3):
        from_down.append(lax.ppermute(from_down[-1], "tensor", up))
        from_up.append(lax.ppermute(from_up[-1], "tensor", down))
    farthest = jnp.concatenate(
        [
            lax.ppermute(from_down[3][:half], "tensor", up),
            lax.ppermute(from_up[3][half:], "tensor", down),
        ],
        0,
    )
    key_peer, value_peer = peer(key_in[0]), peer(value_in[0])
    seq_place = jnp.reshape(seq, (1,)).astype(jnp.int32)
    att, dq, dk_own, dk_peer, dv_own, dv_peer = attention(
        lengths[0], seq_place, query_in[0], key_in[0], key_peer, value_in[0], value_peer, attn_grad[0]
    )
    att_peer = peer(att)
    d_keys = (dk_own.astype(F32) + peer(dk_peer).astype(F32)).astype(BF16)
    d_values = (dv_own.astype(F32) + peer(dv_peer).astype(F32)).astype(BF16)

    offsets = jnp.mod(z - jnp.arange(4, dtype=jnp.int32), z_count)
    places = jnp.mod(offsets, 4)
    pairs = {
        2: (from_down[2], from_up[2]),
        1: (from_down[1], from_up[3]),
        3: (from_down[3], from_up[1]),
        0: (own, farthest),
    }
    sums, peaks = {}, {}
    for pair, (near, far) in pairs.items():
        keep_near = (offsets[pair] // 4) == seq
        mine = jnp.where(keep_near, near, far)
        recv = peer(jnp.where(keep_near, far, near))
        known = [peaks[i] for i in (1, 2, 3)] if pair == 0 else []
        terms, peaks[pair] = weight_block(
            places[pair : pair + 1], mine, recv, att, att_peer, carried_error[0], known, dp_count
        )
        shared = lax.all_to_all(terms, "dp", 0, 0, tiled=True)
        sums[pair] = shared if pair == 0 else jnp.sum(shared.astype(F32), axis=0)
    level_sums, block_scale = finish(places, sums[0], [sums[i] for i in (1, 2, 3)])
    return dq[None], d_keys[None], d_values[None], level_sums, block_scale


def solution(mesh):
    tokens = P("dp", "seq", "tensor")
    in_specs = (tokens,) * 5 + (P("dp", "seq", None, "tensor"), P("dp", None))
    out_specs = (tokens,) * 3 + (P("seq", "dp", "tensor"), P("seq", "tensor"))
    return jax.shard_map(body, mesh=mesh, in_specs=in_specs, out_specs=out_specs, check_vma=False)
```

time: 321 us -> 148 us (0.46)
  waiting for transfers between devices: 135 us -> 33.6 us
  blocking collectives: 66.7 us -> 0 us
  starting transfers between devices: 0.46 us -> 42.1 us
  Pallas kernels: 0 us -> 28.7 us
  matrix products: 22.4 us -> 0 us
  local copies, waits for them, and re-layouts: 36.2 us -> 14.6 us
  loops' own time: 16.1 us -> 0 us
  other arithmetic: 29.2 us -> 15.5 us
    reduce_scatter x4 -> x0, waiting for transfers between devices: 71.1 us -> none  [the longest x1 71.1 us: body(): lax.psum_scatter(levels.astype(jnp.bfloat16), 'dp', scatter_dimension=1,...]
    pmax x1 -> x0, blocking collectives: 66.7 us -> none  [body(): block_peaks = lax.pmax(jnp.max(jnp.abs(corrected), axis=1), 'dp')]
    all_gather x3 -> x0, waiting for transfers between devices: 62.6 us -> none  [the longest x1 45 us: body(): full_grad = lax.all_gather(out_grad[0], 'tensor', axis=1, tiled=True)]
    pallas_call x0 -> x6, Pallas kernels: none -> 28.7 us  [the longest x1 15.3 us: attention(): pl.pallas_call(functools.partial(attention_kernel, tile=256), grid_spec=p...]
    all_to_all x0 -> x4, starting transfers between devices: none -> 25 us  [body(): shared = lax.all_to_all(terms, 'dp', 0, 0, tiled=True)]
    dot_general x15 -> x0, matrix products: 22.4 us -> none  [the longest x1 6.65 us: body(): lax.dot_general(full_grad, attend_flat, (((0,), (0,)), ((), ())), preferr...]
    ppermute x0 -> x17, waiting for transfers between devices: none -> 19.9 us  [the longest x3 19.9 us: body(): from_down.append(lax.ppermute(from_down[-1], 'tensor', up))]
    ppermute x0 -> x17, starting transfers between devices: none -> 17.1 us  [the longest x3 10.6 us: body(): from_up.append(lax.ppermute(from_up[-1], 'tensor', down))]
  transfers between devices with their start and end apart: 7 -> 21, of which waited for: 4 -> 5; matrix products, arithmetic and copies ran while one was open for 24% -> 15% of each run, Pallas kernels for 0% -> 19%
where the time goes in v1:
time: 148 us; the launch traced here: 146 us
  starting transfers between devices  42.1 us (28%)
  waiting for transfers between devices  33.6 us (23%)
  Pallas kernels  28.7 us (19%)
  other arithmetic  15.5 us (10%)
  local copies, waits for them, and re-layouts  14.6 us (10%)
  between operations  11.5 us (8%)
    all_to_all x4, starting transfers between devices, body(): shared = lax.all_to_all(terms, 'dp', 0, 0, tiled=True)  25 us
    ppermute x3, waiting for transfers between devices, body(): from_down.append(lax.ppermute(from_down[-1], 'tensor', up))  19.9 us
    pallas_call x1, Pallas kernels, attention(): pl.pallas_call(functools.partial(attention_kernel, tile=256), grid_spec=p...  15.3 us
    all_to_all x4, waiting for transfers between devices, body(): shared = lax.all_to_all(terms, 'dp', 0, 0, tiled=True)  13.7 us
    pallas_call x4, Pallas kernels, weight_block(): pl.pallas_call(functools.partial(weight_kernel, dp_count=dp_count), grid_...  12 us
    ppermute x3, starting transfers between devices, body(): from_up.append(lax.ppermute(from_up[-1], 'tensor', down))  10.6 us
    unnamed x25, local copies, waits for them, and re-layouts  9.76 us
    select_n x4, other arithmetic, body(): recv = peer(jnp.where(keep_near, far, near))  8.11 us
  transfers between devices with their start and end apart: 21, of which 5 were waited for; matrix products, arithmetic and copies ran while one was open for 15% of the time, Pallas kernels for 19%

profile of v1, /device:TPU:2, one launch (start us, length us, event | category | flops | bytes accessed | tf_op | source)
XLA Modules:
  0.0 146.1 jit_solution(18414889407025078608)
XLA Ops:
  0.6 2.0 %collective-permute-start.4 = (bf16[512,512]{1,0:T(8,128)(2,1)}, bf16[512,512]{1,0:T(8,128)(2,1)S(1)}, u32[]{:S(2)}, u32[]{:S(2)}) collective-permute-start(bf16[512,512]{1,0:T(8,128)(2,1)} %bitcast.30), channel_id=1, source_target_pairs={{0,1},{1,2},{2,3},{3,4},{4,5},{5,6},{6,7},{7,0},{8,9},{9,10},{10,1... | collective-permute-start | bytes 1572872 | tf_op jit(solution)/shard_map/ppermute | solution.py:226
  2.6 4.0 %collective-permute-start.8 = (bf16[512,512]{1,0:T(8,128)(2,1)}, bf16[512,512]{1,0:T(8,128)(2,1)S(1)}, u32[]{:S(2)}, u32[]{:S(2)}) collective-permute-start(bf16[512,512]{1,0:T(8,128)(2,1)} %bitcast.31), channel_id=1, source_target_pairs={{0,7},{1,0},{2,1},{3,2},{4,3},{5,4},{6,5},{7,6},{8,15},{9,8},{10,9... | collective-permute-start | bytes 1572872 | tf_op jit(solution)/shard_map/ppermute | solution.py:227
  6.7 12.0 %collective-permute-done.4 = bf16[512,512]{1,0:T(8,128)(2,1)S(1)} collective-permute-done((bf16[512,512]{1,0:T(8,128)(2,1)}, bf16[512,512]{1,0:T(8,128)(2,1)S(1)}, u32[]{:S(2)}, u32[]{:S(2)}) %collective-permute-start.4) | collective-permute-done | bytes 524320 | tf_op jit(solution)/shard_map/ppermute | solution.py:226
  18.7 3.3 %collective-permute-start.9 = (bf16[512,512]{1,0:T(8,128)(2,1)S(1)}, bf16[512,512]{1,0:T(8,128)(2,1)}, u32[]{:S(2)}, u32[]{:S(2)}) collective-permute-start(bf16[512,512]{1,0:T(8,128)(2,1)S(1)} %collective-permute-done.8), channel_id=1, source_target_pairs={{0,7},{1,0},{2,1},{3,2},{4,3},{5,4},{6,5},{7,6},{8,15},{9,8},{10,9... | collective-permute-start | bytes 1572872 | tf_op jit(solution)/shard_map/ppermute | solution.py:227
  25.3 7.8 %collective-permute-done.5 = bf16[512,512]{1,0:T(8,128)(2,1)} collective-permute-done((bf16[512,512]{1,0:T(8,128)(2,1)S(1)}, bf16[512,512]{1,0:T(8,128)(2,1)}, u32[]{:S(2)}, u32[]{:S(2)}) %collective-permute-start.5) | collective-permute-done | bytes 524320 | tf_op jit(solution)/shard_map/ppermute | solution.py:226
  34.2 1.0 copy-done.4
  35.2 1.0 copy-done.5
  38.0 15.3 %attention.1 = (bf16[512,512]{1,0:T(8,128)(2,1)S(1)}, bf16[512,512]{1,0:T(8,128)(2,1)}, bf16[512,512]{1,0:T(8,128)(2,1)S(1)}, bf16[512,512]{1,0:T(8,128)(2,1)S(1...) custom-call(s32[4]{0:T(128)S(1)} %bitcast.25, s32[1]{0:T(128)} %bitcast.1.place_ref, ...), custom_call_target="tpu_custom_call" | custom-call | flops 3221225472 | bytes 6291456 | tf_op jit(solution)/shard_map/attention/pallas_call | solution.py:84
  54.9 2.1 %broadcast_select_fusion.2 = (bf16[512,512]{1,0:T(8,128)(2,1)}, bf16[512,512]{1,0:T(8,128)(2,1)S(1)}) fusion(bf16[512,512]{1,0:T(8,128)(2,1)} %collective-permute-done.9, bf16[512,512]{1,0:T(8,128)(2,1)} %collective-permute-done.5, pred[]{:T(512)S(6)} %eq.17), kind=kLoop, calls=%fused_computation.9 | loop fusion | flops 524288 | bytes 2097153 | tf_op jit(solution)/shard_map/jit(_where)/select_n | solution.py:256
  60.0 3.3 %collective-permute-start.10 = (bf16[512,512]{1,0:T(8,128)(2,1)}, bf16[512,512]{1,0:T(8,128)(2,1)}, u32[]{:S(2)}, u32[]{:S(2)}) collective-permute-start(bf16[512,512]{1,0:T(8,128)(2,1)} %collective-permute-done.9), channel_id=1, source_target_pairs={{0,7},{1,0},{2,1},{3,2},{4,3},{5,4},{6,5},{7,6},{8,15},{9,8},{10,9... | collective-permute-start | bytes 1572872 | tf_op jit(solution)/shard_map/ppermute | solution.py:227
  63.3 2.1 %broadcast_select_fusion = (bf16[512,512]{1,0:T(8,128)(2,1)}, bf16[512,512]{1,0:T(8,128)(2,1)S(1)}) fusion(bf16[512,512]{1,0:T(8,128)(2,1)} %copy-done.11, bf16[512,512]{1,0:T(8,128)(2,1)} %collective-permute-done.6, pred[]{:T(512)S(6)} %eq.18), kind=kLoop, calls=%fused_computation.7 | loop fusion | flops 524288 | bytes 2097153 | tf_op jit(solution)/shard_map/jit(_where)/select_n | solution.py:256
  66.0 2.8 %weight_block.5 = (bf16[16,32,512]{2,1,0:T(8,128)(2,1)S(1)}, f32[2,512]{1,0:T(2,128)S(1)}) custom-call(s32[1]{0:T(128)} %get-tuple-element.48.place_ref, bf16[512,512]{1,0:T(8,128)(2,1)S(1)} %get-tuple-element.38.own_ref, bf16[512,512]{1,0:T(8,128)(2,1)} %collective-permute-done.15.recv_ref, bf16[512,512]{1,0:T(8,128)(2,1)S(1)} %get-tuple-element.25.att_ref, ...), custom_call_target="tpu_custom_call" | custom-call | flops 536870912 | bytes 4194304 | tf_op jit(solution)/shard_map/weight_block/pallas_call | solution.py:140
  69.7 7.5 %all-to-all-start.2 = ((bf16[16,32,512]{2,1,0:T(8,128)(2,1)}), bf16[16,32,512]{2,1,0:T(8,128)(2,1)}, u32[]{:S(2)}, u32[]{:S(2)}) async-start(bf16[16,32,512]{2,1,0:T(8,128)(2,1)} %copy-done), calls=%async_computation.2 | async-start | bytes 1048576 | tf_op jit(solution)/shard_map/all_to_all | solution.py:261
  83.9 1.7 %slice.41 = bf16[256,512]{1,0:T(8,128)(2,1)} slice(bf16[512,512]{1,0:T(8,128)(2,1)} %collective-permute-done.10), slice={[256:512], [0:512]} | slice | bytes 524288 | tf_op jit(solution)/shard_map/slice | solution.py:231
  85.6 3.2 %collective-permute-start.11 = (bf16[256,512]{1,0:T(8,128)(2,1)}, bf16[256,512]{1,0:T(8,128)(2,1)}, u32[]{:S(2)}, u32[]{:S(2)}) collective-permute-start(bf16[256,512]{1,0:T(8,128)(2,1)} %slice.41), channel_id=1, source_target_pairs={{0,7},{1,0},{2,1},{3,2},{4,3},{5,4},{6,5},{7,6},{8,15},{9,8},{10,9... | collective-permute-start | bytes 786440 | tf_op jit(solution)/shard_map/ppermute | solution.py:231
  88.8 2.1 %broadcast_select_fusion.4 = (bf16[512,512]{1,0:T(8,128)(2,1)}, bf16[512,512]{1,0:T(8,128)(2,1)S(1)}) fusion(bf16[512,512]{1,0:T(8,128)(2,1)} %collective-permute-done.10, bf16[512,512]{1,0:T(8,128)(2,1)} %copy-done.10, pred[]{:T(512)S(6)} %eq.16), kind=kLoop, calls=%fused_computation.11 | loop fusion | flops 524288 | bytes 2097153 | tf_op jit(solution)/shard_map/jit(_where)/select_n | solution.py:256
  90.9 2.8 %weight_block.6 = (bf16[16,32,512]{2,1,0:T(8,128)(2,1)S(1)}, f32[2,512]{1,0:T(2,128)S(1)}) custom-call(s32[1]{0:T(128)} %get-tuple-element.47.place_ref, bf16[512,512]{1,0:T(8,128)(2,1)S(1)} %get-tuple-element.36.own_ref, bf16[512,512]{1,0:T(8,128)(2,1)} %collective-permute-done.16.recv_ref, bf16[512,512]{1,0:T(8,128)(2,1)S(1)} %get-tuple-element.25.att_ref, ...), custom_call_target="tpu_custom_call" | custom-call | flops 536870912 | bytes 4194304 | tf_op jit(solution)/shard_map/weight_block/pallas_call | solution.py:140
  94.5 7.2 %all-to-all-start.3 = ((bf16[16,32,512]{2,1,0:T(8,128)(2,1)}), bf16[16,32,512]{2,1,0:T(8,128)(2,1)}, u32[]{:S(2)}, u32[]{:S(2)}) async-start(bf16[16,32,512]{2,1,0:T(8,128)(2,1)} %copy-done.1), calls=%async_computation.3 | async-start | bytes 1048576 | tf_op jit(solution)/shard_map/all_to_all | solution.py:261
  103.7 1.9 %broadcast_select_fusion.6 = (bf16[512,512]{1,0:T(8,128)(2,1)}, bf16[512,512]{1,0:T(8,128)(2,1)S(1)}) fusion(bf16[512,512]{1,0:T(8,128)(2,1)S(1)} %constant_dynamic-update-slice_fusion, pred[]{:T(512)S(6)} %eq.15, bf16[1,512,512]{2,1,0:T(8,128)(2,1)} %param.11), kind=kLoop, calls=%fused_computation.13 | loop fusion | flops 524288 | bytes 2097153 | tf_op jit(solution)/shard_map/jit(_where)/select_n | solution.py:256
  106.1 2.7 %weight_block.4 = (bf16[16,32,512]{2,1,0:T(8,128)(2,1)S(1)}, f32[2,512]{1,0:T(2,128)S(1)}) custom-call(s32[1]{0:T(128)} %get-tuple-element.49.place_ref, bf16[512,512]{1,0:T(8,128)(2,1)S(1)} %get-tuple-element.40.own_ref, bf16[512,512]{1,0:T(8,128)(2,1)} %collective-permute-done.14.recv_ref, bf16[512,512]{1,0:T(8,128)(2,1)S(1)} %get-tuple-element.25.att_ref, ...), custom_call_target="tpu_custom_call" | custom-call | flops 536870912 | bytes 4194304 | tf_op jit(solution)/shard_map/weight_block/pallas_call | solution.py:140
  109.6 3.0 %all-to-all-done.3 = bf16[16,32,512]{2,1,0:T(8,128)(2,1)} async-done(((bf16[16,32,512]{2,1,0:T(8,128)(2,1)}), bf16[16,32,512]{2,1,0:T(8,128)(2,1)}, u32[]{:S(2)}, u32[]{:S(2)}) %all-to-all-start.3) | async-done | bytes 524320 | tf_op jit(solution)/shard_map/all_to_all | solution.py:261
  112.7 5.4 %all-to-all-start.1 = ((bf16[16,32,512]{2,1,0:T(8,128)(2,1)}), bf16[16,32,512]{2,1,0:T(8,128)(2,1)}, u32[]{:S(2)}, u32[]{:S(2)}) async-start(bf16[16,32,512]{2,1,0:T(8,128)(2,1)} %copy-done.2), calls=%async_computation.1 | async-start | bytes 1048576 | tf_op jit(solution)/shard_map/all_to_all | solution.py:261
  118.1 3.7 %weight_block.7 = (bf16[16,48,512]{2,1,0:T(8,128)(2,1)}, f32[2,512]{1,0:T(2,128)}) custom-call(s32[1]{0:T(128)} %get-tuple-element.50.place_ref, bf16[512,512]{1,0:T(8,128)(2,1)S(1)} %get-tuple-element.42.own_ref, bf16[512,512]{1,0:T(8,128)(2,1)} %collective-permute-done.12.recv_ref, bf16[512,512]{1,0:T(8,128)(2,1)S(1)} %get-tuple-element.25.att_ref, ...), custom_call_target="tpu_custom_call" | custom-call | flops 536870912 | bytes 4194304 | tf_op jit(solution)/shard_map/weight_block/pallas_call | solution.py:140
  121.8 6.2 %all-to-all-done.1 = bf16[16,32,512]{2,1,0:T(8,128)(2,1)} async-done(((bf16[16,32,512]{2,1,0:T(8,128)(2,1)}), bf16[16,32,512]{2,1,0:T(8,128)(2,1)}, u32[]{:S(2)}, u32[]{:S(2)}) %all-to-all-start.1) | async-done | bytes 524320 | tf_op jit(solution)/shard_map/all_to_all | solution.py:261
  128.0 4.9 %all-to-all-start = ((bf16[16,48,512]{2,1,0:T(8,128)(2,1)}), bf16[16,48,512]{2,1,0:T(8,128)(2,1)S(1)}, u32[]{:S(2)}, u32[]{:S(2)}) async-start(bf16[16,48,512]{2,1,0:T(8,128)(2,1)} %get-tuple-element.29), calls=%async_computation | async-start | bytes 1572864 | tf_op jit(solution)/shard_map/all_to_all | solution.py:261
  132.9 2.0 %fusion.1 = bf16[1,512,512]{2,1,0:T(8,128)(2,1)} fusion(bf16[512,512]{1,0:T(8,128)(2,1)} %collective-permute-done.3, bf16[512,512]{1,0:T(8,128)(2,1)S(1)} %get-tuple-element.23), kind=kLoop, calls=%fused_computation.6 | loop fusion | flops 1048576 | bytes 1572864 | tf_op jit(solution)/shard_map/broadcast_in_dim | solution.py:264
  134.9 2.0 %fusion = bf16[1,512,512]{2,1,0:T(8,128)(2,1)} fusion(bf16[512,512]{1,0:T(8,128)(2,1)} %collective-permute-done.2, bf16[512,512]{1,0:T(8,128)(2,1)S(1)} %get-tuple-element.21), kind=kLoop, calls=%fused_computation.5 | loop fusion | flops 1048576 | bytes 1572864 | tf_op jit(solution)/shard_map/broadcast_in_dim | solution.py:264
  136.9 1.1 convert_reduce_fusion.1.refs_1_
  138.0 1.1 convert_reduce_fusion.refs_2_
  139.2 1.1 convert_reduce_fusion.2.refs_0_
  140.3 4.4 %all-to-all-done.last_ref = bf16[16,48,512]{2,1,0:T(8,128)(2,1)S(1)} async-done(((bf16[16,48,512]{2,1,0:T(8,128)(2,1)}), bf16[16,48,512]{2,1,0:T(8,128)(2,1)S(1)}, u32[]{:S(2)}, u32[]{:S(2)}) %all-to-all-start) | async-done | bytes 786464 | tf_op jit(solution)/shard_map/all_to_all | solution.py:261
  144.7 1.4 finish.1
  (56 shorter events, 12.2 us)
Async XLA Ops:
  0.6 18.1 %collective-permute-start.4 = (bf16[512,512]{1,0:T(8,128)(2,1)}, bf16[512,512]{1,0:T(8,128)(2,1)S(1)}, u32[]{:S(2)}, u32[]{:S(2)}) collective-permute-start(bf16[512,512]{1,0:T(8,128)(2,1)} %bitcast.30), channel_id=1, source_target_pairs={{0,1},{1,2},{2,3},{3,4},{4,5},{5,6},{6,7},{7,0},{8,9},{9,10},{10,1... | collective-permute-start | bytes 1572872 | tf_op jit(solution)/shard_map/ppermute | solution.py:226
  2.6 16.1 %collective-permute-start.8 = (bf16[512,512]{1,0:T(8,128)(2,1)}, bf16[512,512]{1,0:T(8,128)(2,1)S(1)}, u32[]{:S(2)}, u32[]{:S(2)}) collective-permute-start(bf16[512,512]{1,0:T(8,128)(2,1)} %bitcast.31), channel_id=1, source_target_pairs={{0,7},{1,0},{2,1},{3,2},{4,3},{5,4},{6,5},{7,6},{8,15},{9,8},{10,9... | collective-permute-start | bytes 1572872 | tf_op jit(solution)/shard_map/ppermute | solution.py:227
  6.7 26.5 %collective-permute-start = (bf16[512,512]{1,0:T(8,128)(2,1)}, bf16[512,512]{1,0:T(8,128)(2,1)S(1)}, u32[]{:S(2)}, u32[]{:S(2)}) collective-permute-start(bf16[512,512]{1,0:T(8,128)(2,1)} %bitcast.20), channel_id=1, source_target_pairs={{0,8},{8,0},{1,9},{9,1},{2,10},{10,2},{3,11},{11,3},{4,12},{12,4},... | collective-permute-start | bytes 1572872 | tf_op jit(solution)/shard_map/ppermute | solution.py:220
  18.7 14.4 %copy-start.10 = (bf16[512,512]{1,0:T(8,128)(2,1)}, bf16[512,512]{1,0:T(8,128)(2,1)S(1)}, u32[]{:S(2)}) copy-start(bf16[512,512]{1,0:T(8,128)(2,1)S(1)} %collective-permute-done.4) | copy-start | bytes 1572868
  18.7 14.4 %collective-permute-start.5 = (bf16[512,512]{1,0:T(8,128)(2,1)S(1)}, bf16[512,512]{1,0:T(8,128)(2,1)}, u32[]{:S(2)}, u32[]{:S(2)}) collective-permute-start(bf16[512,512]{1,0:T(8,128)(2,1)S(1)} %collective-permute-done.4), channel_id=1, source_target_pairs={{0,1},{1,2},{2,3},{3,4},{4,5},{5,6},{6,7},{7,0},{8,9},{9,10},{10,1... | collective-permute-start | bytes 1572872 | tf_op jit(solution)/shard_map/ppermute | solution.py:226
  18.7 14.4 %collective-permute-start.1 = (bf16[512,512]{1,0:T(8,128)(2,1)}, bf16[512,512]{1,0:T(8,128)(2,1)S(1)}, u32[]{:S(2)}, u32[]{:S(2)}) collective-permute-start(bf16[512,512]{1,0:T(8,128)(2,1)} %bitcast.22), channel_id=1, source_target_pairs={{0,8},{8,0},{1,9},{9,1},{2,10},{10,2},{3,11},{11,3},{4,12},{12,4},... | collective-permute-start | bytes 1572872 | tf_op jit(solution)/shard_map/ppermute | solution.py:220
  18.7 34.5 %copy-start.11 = (bf16[512,512]{1,0:T(8,128)(2,1)}, bf16[512,512]{1,0:T(8,128)(2,1)S(1)}, u32[]{:S(2)}) copy-start(bf16[512,512]{1,0:T(8,128)(2,1)S(1)} %collective-permute-done.8) | copy-start | bytes 1572868
  18.7 36.1 %collective-permute-start.9 = (bf16[512,512]{1,0:T(8,128)(2,1)S(1)}, bf16[512,512]{1,0:T(8,128)(2,1)}, u32[]{:S(2)}, u32[]{:S(2)}) collective-permute-start(bf16[512,512]{1,0:T(8,128)(2,1)S(1)} %collective-permute-done.8), channel_id=1, source_target_pairs={{0,7},{1,0},{2,1},{3,2},{4,3},{5,4},{6,5},{7,6},{8,15},{9,8},{10,9... | collective-permute-start | bytes 1572872 | tf_op jit(solution)/shard_map/ppermute | solution.py:227
  33.1 30.2 %collective-permute-start.6 = (bf16[512,512]{1,0:T(8,128)(2,1)}, bf16[512,512]{1,0:T(8,128)(2,1)}, u32[]{:S(2)}, u32[]{:S(2)}) collective-permute-start(bf16[512,512]{1,0:T(8,128)(2,1)} %collective-permute-done.5), channel_id=1, source_target_pairs={{0,1},{1,2},{2,3},{3,4},{4,5},{5,6},{6,7},{7,0},{8,9},{9,10},{10,1... | collective-permute-start | bytes 1572872 | tf_op jit(solution)/shard_map/ppermute | solution.py:226
  33.2 1.0 copy-start.3
  34.2 1.0 copy-start.4
  35.2 1.0 copy-start.5
  36.3 1.0 copy-start.6
  53.3 0.8 copy-start.7
  54.1 0.8 copy-start.8
  54.9 11.2 %collective-permute-start.13 = (bf16[512,512]{1,0:T(8,128)(2,1)S(1)}, bf16[512,512]{1,0:T(8,128)(2,1)S(1)}, u32[]{:S(2)}, u32[]{:S(2)}) collective-permute-start(bf16[512,512]{1,0:T(8,128)(2,1)S(1)} %get-tuple-element.25.att_ref), channel_id=1, source_target_pairs={{0,8},{8,0},{1,9},{9,1},{2,10},{10,2},{3,11},{11,3},{4,12},{12,4},... | collective-permute-start | bytes 1572872 | tf_op jit(solution)/shard_map/ppermute | solution.py:220
  56.9 9.1 %collective-permute-start.15 = (bf16[512,512]{1,0:T(8,128)(2,1)}, bf16[512,512]{1,0:T(8,128)(2,1)}, u32[]{:S(2)}, u32[]{:S(2)}) collective-permute-start(bf16[512,512]{1,0:T(8,128)(2,1)} %get-tuple-element.37), channel_id=1, source_target_pairs={{0,8},{8,0},{1,9},{9,1},{2,10},{10,2},{3,11},{11,3},{4,12},{12,4},... | collective-permute-start | bytes 1572872 | tf_op jit(solution)/shard_map/ppermute | solution.py:220
  60.0 23.9 %collective-permute-start.10 = (bf16[512,512]{1,0:T(8,128)(2,1)}, bf16[512,512]{1,0:T(8,128)(2,1)}, u32[]{:S(2)}, u32[]{:S(2)}) collective-permute-start(bf16[512,512]{1,0:T(8,128)(2,1)} %collective-permute-done.9), channel_id=1, source_target_pairs={{0,7},{1,0},{2,1},{3,2},{4,3},{5,4},{6,5},{7,6},{8,15},{9,8},{10,9... | collective-permute-start | bytes 1572872 | tf_op jit(solution)/shard_map/ppermute | solution.py:227
  65.4 25.5 %collective-permute-start.16 = (bf16[512,512]{1,0:T(8,128)(2,1)}, bf16[512,512]{1,0:T(8,128)(2,1)}, u32[]{:S(2)}, u32[]{:S(2)}) collective-permute-start(bf16[512,512]{1,0:T(8,128)(2,1)} %get-tuple-element.35), channel_id=1, source_target_pairs={{0,8},{8,0},{1,9},{9,1},{2,10},{10,2},{3,11},{11,3},{4,12},{12,4},... | collective-permute-start | bytes 1572872 | tf_op jit(solution)/shard_map/ppermute | solution.py:220
  68.9 0.8 copy-start
  69.7 24.8 %all-to-all-start.2 = ((bf16[16,32,512]{2,1,0:T(8,128)(2,1)}), bf16[16,32,512]{2,1,0:T(8,128)(2,1)}, u32[]{:S(2)}, u32[]{:S(2)}) async-start(bf16[16,32,512]{2,1,0:T(8,128)(2,1)} %copy-done), calls=%async_computation.2 | async-start | bytes 1048576 | tf_op jit(solution)/shard_map/all_to_all | solution.py:261
  83.6 18.1 %collective-permute-start.7 = (bf16[256,512]{1,0:T(8,128)(2,1)S(1)}, bf16[256,512]{1,0:T(8,128)(2,1)}, u32[]{:S(2)}, u32[]{:S(2)}) collective-permute-start(bf16[256,512]{1,0:T(8,128)(2,1)S(1)} %slice.40), channel_id=1, source_target_pairs={{0,1},{1,2},{2,3},{3,4},{4,5},{5,6},{6,7},{7,0},{8,9},{9,10},{10,1... | collective-permute-start | bytes 786440 | tf_op jit(solution)/shard_map/ppermute | solution.py:230
  85.6 17.1 %collective-permute-start.11 = (bf16[256,512]{1,0:T(8,128)(2,1)}, bf16[256,512]{1,0:T(8,128)(2,1)}, u32[]{:S(2)}, u32[]{:S(2)}) collective-permute-start(bf16[256,512]{1,0:T(8,128)(2,1)} %slice.41), channel_id=1, source_target_pairs={{0,7},{1,0},{2,1},{3,2},{4,3},{5,4},{6,5},{7,6},{8,15},{9,8},{10,9... | collective-permute-start | bytes 786440 | tf_op jit(solution)/shard_map/ppermute | solution.py:231
  90.9 15.2 %collective-permute-start.14 = (bf16[512,512]{1,0:T(8,128)(2,1)}, bf16[512,512]{1,0:T(8,128)(2,1)}, u32[]{:S(2)}, u32[]{:S(2)}) collective-permute-start(bf16[512,512]{1,0:T(8,128)(2,1)} %get-tuple-element.39), channel_id=1, source_target_pairs={{0,8},{8,0},{1,9},{9,1},{2,10},{10,2},{3,11},{11,3},{4,12},{12,4},... | collective-permute-start | bytes 1572872 | tf_op jit(solution)/shard_map/ppermute | solution.py:220
  93.7 0.8 copy-start.1
  94.5 18.2 %all-to-all-start.3 = ((bf16[16,32,512]{2,1,0:T(8,128)(2,1)}), bf16[16,32,512]{2,1,0:T(8,128)(2,1)}, u32[]{:S(2)}, u32[]{:S(2)}) async-start(bf16[16,32,512]{2,1,0:T(8,128)(2,1)} %copy-done.1), calls=%async_computation.3 | async-start | bytes 1048576 | tf_op jit(solution)/shard_map/all_to_all | solution.py:261
  105.6 12.5 %collective-permute-start.12 = (bf16[512,512]{1,0:T(8,128)(2,1)}, bf16[512,512]{1,0:T(8,128)(2,1)}, u32[]{:S(2)}, u32[]{:S(2)}) collective-permute-start(bf16[512,512]{1,0:T(8,128)(2,1)} %get-tuple-element.41), channel_id=1, source_target_pairs={{0,8},{8,0},{1,9},{9,1},{2,10},{10,2},{3,11},{11,3},{4,12},{12,4},... | collective-permute-start | bytes 1572872 | tf_op jit(solution)/shard_map/ppermute | solution.py:220
  105.6 27.3 %collective-permute-start.3 = (bf16[512,512]{1,0:T(8,128)(2,1)}, bf16[512,512]{1,0:T(8,128)(2,1)}, u32[]{:S(2)}, u32[]{:S(2)}) collective-permute-start(bf16[512,512]{1,0:T(8,128)(2,1)} %copy-done.8), channel_id=1, source_target_pairs={{0,8},{8,0},{1,9},{9,1},{2,10},{10,2},{3,11},{11,3},{4,12},{12,4},... | collective-permute-start | bytes 1572872 | tf_op jit(solution)/shard_map/ppermute | solution.py:220
  108.8 0.8 copy-start.2
  112.7 15.4 %all-to-all-start.1 = ((bf16[16,32,512]{2,1,0:T(8,128)(2,1)}), bf16[16,32,512]{2,1,0:T(8,128)(2,1)}, u32[]{:S(2)}, u32[]{:S(2)}) async-start(bf16[16,32,512]{2,1,0:T(8,128)(2,1)} %copy-done.2), calls=%async_computation.1 | async-start | bytes 1048576 | tf_op jit(solution)/shard_map/all_to_all | solution.py:261
  118.1 16.8 %collective-permute-start.2 = (bf16[512,512]{1,0:T(8,128)(2,1)}, bf16[512,512]{1,0:T(8,128)(2,1)}, u32[]{:S(2)}, u32[]{:S(2)}) collective-permute-start(bf16[512,512]{1,0:T(8,128)(2,1)} %copy-done.7), channel_id=1, source_target_pairs={{0,8},{8,0},{1,9},{9,1},{2,10},{10,2},{3,11},{11,3},{4,12},{12,4},... | collective-permute-start | bytes 1572872 | tf_op jit(solution)/shard_map/ppermute | solution.py:220
  128.0 16.7 %all-to-all-start = ((bf16[16,48,512]{2,1,0:T(8,128)(2,1)}), bf16[16,48,512]{2,1,0:T(8,128)(2,1)S(1)}, u32[]{:S(2)}, u32[]{:S(2)}) async-start(bf16[16,48,512]{2,1,0:T(8,128)(2,1)} %get-tuple-element.29), calls=%async_computation | async-start | bytes 1572864 | tf_op jit(solution)/shard_map/all_to_all | solution.py:261
  (1 other events, 0.7 us)

commit v2 on v1

v2 whole, which is shorter than its diff:
```python
import functools
import math

import jax
import jax.numpy as jnp
from jax import lax
from jax.experimental import pallas as pl
from jax.experimental.pallas import tpu as pltpu
from jax.sharding import PartitionSpec as P

HEAD_DIM = 128
NEG_FILL = -1e30
F32 = jnp.float32
BF16 = jnp.bfloat16
MIB = 2**20
TOKEN = jax.ShapeDtypeStruct((8, 128), F32)
TOKEN_SPEC = pl.BlockSpec((8, 128), lambda i, *_: (0, 0))


def dot_on(a, b, a_dim, b_dim):
    return lax.dot_general(a, b, (((a_dim,), (b_dim,)), ((), ())), preferred_element_type=F32)


def attention_kernel(
    place_ref, kp_ref, vp_ref, q_hbm, ko_hbm, vo_hbm, g_hbm, *refs, tile, first, count
):
    att_ref, dq_ref, dko_ref, dkp_ref, dvo_ref, dvp_ref, token_ref = refs[-12:-5]
    ids_ref, dk_acc, dv_acc, held_ref, sems = refs[-5:]
    token_ref[...] = jnp.zeros_like(token_ref)
    rows = kp_ref.shape[0]
    head = pl.program_id(0)

    def fetch(step, source, index):
        column = pl.ds((first + step) * HEAD_DIM, HEAD_DIM)
        return pltpu.make_async_copy(
            source.at[:, column], held_ref.at[step, index], sems.at[step, index]
        )

    sources = (ko_hbm, q_hbm, vo_hbm, g_hbm)

    @pl.when(head == 0)
    def _():
        for step in range(count):
            for index, source in enumerate(sources):
                fetch(step, source, index).start()
    inverse = 1.0 / math.sqrt(HEAD_DIM)
    to_exp2 = inverse * math.log2(math.e)
    own = place_ref[0] * rows
    other = rows - own

    def ids(positions):
        found = jnp.zeros(positions.shape, jnp.int32)
        end = jnp.int32(0)
        for image in range(4):
            end = end + place_ref[2 + image]
            found = found + (positions >= end).astype(jnp.int32)
        return found

    @pl.when(head == 0)
    def _():
        positions = lax.broadcasted_iota(jnp.int32, (rows, 128), 0)
        ids_ref[:rows, :] = ids(positions + own)
        ids_ref[rows:, :] = ids(positions + other)

    for step in range(count):

        @pl.when(head == step)
        def _():
            for index, source in enumerate(sources):
                fetch(step, source, index).wait()

    ko_ref, q_ref, vo_ref, g_ref = (held_ref.at[head, index] for index in range(4))
    k = jnp.concatenate([ko_ref[...], kp_ref[...]], 0)
    v = jnp.concatenate([vo_ref[...], vp_ref[...]], 0)
    k_t, v_t = k.T, v.T
    for i in range(rows // tile):
        part = slice(i * tile, (i + 1) * tile)
        q, g = q_ref[part, :], g_ref[part, :]
        query_ids = ids(lax.broadcasted_iota(jnp.int32, (8, tile), 1) + (own + i * tile))[:1]
        key_ids = jnp.concatenate([ids_ref[...]] * (tile // 128), 1)
        scores = jnp.where(key_ids == query_ids, dot_on(k, q, 1, 1) * to_exp2, NEG_FILL)
        peak = jnp.max(scores, axis=0, keepdims=True)
        raised = jnp.exp2(scores - peak)
        weights = raised * (1.0 / jnp.sum(raised, axis=0, keepdims=True))
        prob = weights.astype(BF16)
        att_t = dot_on(v_t, prob, 1, 0).astype(BF16).astype(F32)
        att_ref[part, :] = att_t.T.astype(BF16)
        delta = jnp.sum(g.astype(F32).T * att_t, axis=0, keepdims=True)
        grad_probs = dot_on(v, g, 1, 1)
        grad_scores = (weights * ((grad_probs - delta) * inverse)).astype(BF16)
        dq_ref[part, :] = dot_on(k_t, grad_scores, 1, 0).T.astype(BF16)
        dk = dot_on(grad_scores, q, 1, 0)
        dv = dot_on(prob, g, 1, 0)
        if i == 0:
            dk_acc[...] = dk
            dv_acc[...] = dv
        else:
            dk_acc[...] += dk
            dv_acc[...] += dv
    dko_ref[...] = dk_acc[:rows].astype(BF16)
    dkp_ref[...] = dk_acc[rows:].astype(BF16)
    dvo_ref[...] = dv_acc[:rows].astype(BF16)
    dvp_ref[...] = dv_acc[rows:].astype(BF16)


def cost(microseconds):
    return pl.CostEstimate(
        flops=int(microseconds * 1.15e9), bytes_accessed=0, transcendentals=0
    )


def attention(place, q, ko, kp, vo, vp, g, first, count, held, after):
    rows, width = q.shape
    spec = pl.BlockSpec((rows, HEAD_DIM), lambda i, *_: (0, i + first))
    return pl.pallas_call(
        functools.partial(attention_kernel, tile=256, first=first, count=count),
        grid_spec=pltpu.PrefetchScalarGridSpec(
            num_scalar_prefetch=1,
            grid=(count,),
            in_specs=[spec] * 2
            + [pl.BlockSpec(memory_space=pltpu.HBM)] * 4
            + [pl.BlockSpec(memory_space=pl.ANY)] * (len(held) + len(after)),
            out_specs=[spec] * 6 + [TOKEN_SPEC],
            scratch_shapes=[
                pltpu.VMEM((2 * rows, 128), jnp.int32),
                pltpu.VMEM((2 * rows, HEAD_DIM), F32),
                pltpu.VMEM((2 * rows, HEAD_DIM), F32),
                pltpu.VMEM((count, 4, rows, HEAD_DIM), BF16),
                pltpu.SemaphoreType.DMA((count, 4)),
            ],
        ),
        out_shape=[jax.ShapeDtypeStruct((rows, width), BF16)] * 6 + [TOKEN],
        input_output_aliases={7 + i: i for i in range(len(held))},
        compiler_params=pltpu.CompilerParams(vmem_limit_bytes=24 * MIB),
        cost_estimate=cost(0.2),
        name="attention",
    )(place, kp, vp, q, ko, vo, g, *held, *after)


def gate_kernel(*refs):
    pass


def gate(arrays, after):
    anywhere = pl.BlockSpec(memory_space=pl.ANY)
    return pl.pallas_call(
        gate_kernel,
        in_specs=[anywhere] * (len(arrays) + len(after)),
        out_specs=[anywhere] * len(arrays),
        out_shape=[jax.ShapeDtypeStruct(a.shape, a.dtype) for a in arrays],
        input_output_aliases={i: i for i in range(len(arrays))},
        compiler_params=pltpu.CompilerParams(vmem_limit_bytes=2 * MIB),
        cost_estimate=cost(0.0001),
        name="gate",
    )(*arrays, *after)


def half_kernel(whole_ref, half_ref, *, start):
    half_ref[...] = whole_ref[pl.ds(start, half_ref.shape[0]), :]


def half_of(array, second):
    rows, width = array.shape
    whole = pl.BlockSpec(memory_space=pltpu.VMEM)
    return pl.pallas_call(
        functools.partial(half_kernel, start=rows // 2 * second),
        in_specs=[whole],
        out_specs=whole,
        out_shape=jax.ShapeDtypeStruct((rows // 2, width), array.dtype),
        compiler_params=pltpu.CompilerParams(vmem_limit_bytes=4 * MIB),
        cost_estimate=cost(0.0001),
        name="half_of",
    )(array)


def origin(place_ref, pair, chips):
    return lax.rem(place_ref[1] + (chips - pair), chips)


def owns(place_ref, pair, chips):
    return (lax.div(origin(place_ref, pair, chips), chips // 2) == place_ref[0]).astype(jnp.int32)


def spot(place_ref, pair, chips):
    return lax.rem(origin(place_ref, pair, chips), chips // 2)


def pick_kernel(place_ref, near_ref, *refs, pair, chips, count):
    far_refs, out_ref = refs[:count], refs[-1]
    keep = owns(place_ref, pair, chips) == 1
    rows = near_ref.shape[0] // len(far_refs)
    for index, far_ref in enumerate(far_refs):
        part = slice(index * rows, (index + 1) * rows)
        out_ref[part, :] = jnp.where(keep, far_ref[...], near_ref[part, :])


def pick_other(place, near, far, pair, chips, after):
    rows, width = near.shape
    whole = pl.BlockSpec(memory_space=pltpu.VMEM)
    return pl.pallas_call(
        functools.partial(pick_kernel, pair=pair, chips=chips, count=len(far)),
        in_specs=[pl.BlockSpec(memory_space=pltpu.SMEM)]
        + [whole] * (1 + len(far))
        + [pl.BlockSpec(memory_space=pl.ANY)] * len(after),
        out_specs=whole,
        out_shape=jax.ShapeDtypeStruct((rows, width), near.dtype),
        compiler_params=pltpu.CompilerParams(vmem_limit_bytes=8 * MIB),
        cost_estimate=cost(0.0001),
        name="pick_other",
    )(place, near, *far, *after)


def weight_kernel(place_ref, *refs, pairs, pieces, chips, dp_count, after):
    near, refs = refs[: len(pairs)], refs[len(pairs) :]
    recv, refs = refs[: len(pairs)], refs[len(pairs) :]
    far, refs = refs[: len(pairs) * pieces], refs[len(pairs) * pieces :]
    atts, carried_hbm = refs[:2], refs[2]
    *known_refs, out_ref, peak_ref, carried_ref, sems = refs[3 + after :]
    step = pl.program_id(0)

    def fetch(index):
        block = 2 * spot(place_ref, pairs[index // 2], chips) + index % 2
        return pltpu.make_async_copy(carried_hbm.at[block], carried_ref.at[index], sems.at[index])

    @pl.when(step == 0)
    def _():
        for index in range(2 * len(pairs)):
            fetch(index).start()

    rows = near[0].shape[0]

    def chunk(side, part, piece):
        found = None
        for index, pair in enumerate(pairs):
            if side:
                value = recv[index][part, :]
            else:
                keep = owns(place_ref, pair, chips) == 1
                value = jnp.where(keep, near[index][part, :], far[index * pieces + piece][...])
            found = value if index == 0 else jnp.where(step < 2 * index, found, value)
        return found

    corrected = None
    for side in range(2):
        for piece in range(pieces):
            part = slice(piece * rows // pieces, (piece + 1) * rows // pieces)
            product = dot_on(chunk(side, part, piece), atts[side][part, :], 0, 0)
            corrected = product if corrected is None else corrected + product
    for index in range(2 * len(pairs)):

        @pl.when(step == index)
        def _():
            fetch(index).wait()

    corrected = corrected + carried_ref[step]
    share = corrected.shape[0] // dp_count
    peak_ref[pl.ds(step, 1), :] = jnp.max(jnp.abs(corrected), axis=0, keepdims=True)
    rounded = corrected.astype(BF16)
    place = pl.ds(pl.multiple_of(step * share, share), share)
    for dest in range(dp_count):
        out_ref[dest, place, :] = rounded[dest * share : (dest + 1) * share]
    if known_refs:

        @pl.when(step == 2 * len(pairs) - 1)
        def _():
            peaks = jnp.concatenate([peak_ref[...]] + [ref[...] for ref in known_refs], 0)
            high = peaks.astype(BF16).astype(F32)
            both = jnp.concatenate([high, peaks - high], 0).astype(BF16)
            for dest in range(dp_count):
                out_ref[dest, 2 * len(pairs) * share :, :] = both


def weight_block(
    place, near, far, recv, att, carried, known, pairs, chips, dp_count, after
):
    rows, width = att[0].shape
    block = carried.shape[1]
    share = block // dp_count
    count = len(pairs)
    pieces = len(far[0])
    out_rows = 2 * count * share + (16 if known else 0)
    whole = lambda i, *_: (0, 0)

    def column(index, wanted):
        def find(i, ref):
            return 0, jnp.clip(i - 2 * index, 0, 1) * wanted(owns(ref, pairs[index], chips))

        return find

    near_specs = [pl.BlockSpec((rows, block), column(n, lambda own: own)) for n in range(count)]
    recv_specs = [pl.BlockSpec((rows, block), column(n, lambda own: 1)) for n in range(count)]
    far_specs = [
        pl.BlockSpec((rows // pieces, block), column(n, lambda own: 1 - own))
        for n in range(count)
        for _ in range(pieces)
    ]
    return pl.pallas_call(
        functools.partial(
            weight_kernel,
            pairs=pairs,
            pieces=pieces,
            chips=chips,
            dp_count=dp_count,
            after=len(after),
        ),
        grid_spec=pltpu.PrefetchScalarGridSpec(
            num_scalar_prefetch=1,
            grid=(2 * count,),
            in_specs=near_specs
            + recv_specs
            + far_specs
            + [pl.BlockSpec((rows, width), whole)] * 2
            + [pl.BlockSpec(memory_space=pltpu.HBM)]
            + [pl.BlockSpec(memory_space=pl.ANY)] * len(after)
            + [pl.BlockSpec(array.shape, whole) for array in known],
            out_specs=[
                pl.BlockSpec((dp_count, out_rows, width), lambda i, *_: (0, 0, 0)),
                pl.BlockSpec((2 * count, width), whole),
            ],
            scratch_shapes=[
                pltpu.VMEM((2 * count, block, width), F32),
                pltpu.SemaphoreType.DMA((2 * count,)),
            ],
        ),
        out_shape=[
            jax.ShapeDtypeStruct((dp_count, out_rows, width), BF16),
            jax.ShapeDtypeStruct((2 * count, width), F32),
        ],
        compiler_params=pltpu.CompilerParams(vmem_limit_bytes=28 * MIB),
        cost_estimate=cost(0.0001),
        name="weight_block",
    )(place, *near, *recv, *[p for f in far for p in f], *att, carried, *after, *known)


def add_kernel(a_ref, b_ref, c_ref, d_ref, first_ref, second_ref):
    first_ref[...] = (a_ref[...].astype(F32) + b_ref[...].astype(F32)).astype(BF16)
    second_ref[...] = (c_ref[...].astype(F32) + d_ref[...].astype(F32)).astype(BF16)


def add_pairs(a, b, c, d):
    rows, width = a.shape
    spec = pl.BlockSpec((rows // 4, width), lambda i: (i, 0))
    return pl.pallas_call(
        add_kernel,
        grid=(4,),
        in_specs=[spec] * 4,
        out_specs=[spec] * 2,
        out_shape=[jax.ShapeDtypeStruct((rows, width), BF16)] * 2,
        compiler_params=pltpu.CompilerParams(vmem_limit_bytes=8 * MIB),
        cost_estimate=cost(0.0001),
        name="add_pairs",
    )(a, b, c, d)


def finish_kernel(place_ref, last_ref, sides_ref, middle_ref, levels_ref, scale_ref, *, chips):
    share = levels_ref.shape[1]
    head = 2 * share
    peaks = jnp.max(
        last_ref[:, head : head + 8, :].astype(F32) + last_ref[:, head + 8 : head + 16, :].astype(F32),
        axis=0,
    )
    scale = (peaks + 1e-6) / 7.0
    for index, pair in enumerate((0, 1, 3, 2)):
        for half in range(2):
            block = 2 * spot(place_ref, pair, chips) + half
            row = scale[2 * index + half : 2 * index + half + 1]
            scale_ref[pl.ds(block, 1), :] = row
            terms_ref = (last_ref, sides_ref, sides_ref, middle_ref)[index]
            start = ((pair == 3) * 2 + half) * share
            terms = terms_ref[pl.ds(start, share), :] if index else jnp.sum(
                terms_ref[:, start : start + share, :].astype(F32), axis=0
            )
            levels_ref[block] = terms / row


def finish(place, last, sides, middle, share, chips):
    width = last.shape[2]
    vmem = pl.BlockSpec(memory_space=pltpu.VMEM)
    return pl.pallas_call(
        functools.partial(finish_kernel, chips=chips),
        in_specs=[pl.BlockSpec(memory_space=pltpu.SMEM)] + [vmem] * 3,
        out_specs=[vmem] * 2,
        out_shape=[
            jax.ShapeDtypeStruct((8, share, width), F32),
            jax.ShapeDtypeStruct((8, width), F32),
        ],
        compiler_params=pltpu.CompilerParams(vmem_limit_bytes=12 * MIB),
        cost_estimate=cost(0.0001),
        name="finish",
    )(place, last, sides, middle)


def body(query_in, key_in, value_in, attn_grad, out_grad, carried_error, lengths):
    dp_count = lax.axis_size("dp")
    z_count = lax.axis_size("tensor")
    seq = lax.axis_index("seq")
    z = lax.axis_index("tensor")
    up = [(i, (i + 1) % z_count) for i in range(z_count)]
    down = [(i, (i - 1) % z_count) for i in range(z_count)]
    swap = [(0, 1), (1, 0)]

    def peer(array):
        return lax.ppermute(array, "seq", swap)

    own = out_grad[0]
    place = jnp.concatenate([jnp.stack([seq, z]).astype(jnp.int32), lengths[0]])
    heads = own.shape[1] // HEAD_DIM

    def send_up(array):
        return lax.ppermute(array, "tensor", up)

    def send_down(array):
        return lax.ppermute(array, "tensor", down)

    def stay(array):
        return pltpu.with_memory_space_constraint(array, pltpu.HBM)

    from_down, from_up = {1: send_up(own)}, {1: send_down(own)}
    tokens = (
        stay(query_in[0]),
        stay(key_in[0]),
        peer(key_in[0]),
        stay(value_in[0]),
        peer(value_in[0]),
        stay(attn_grad[0]),
    )
    carried = stay(carried_error[0])
    *held, token = attention(place, *tokens, 0, heads // 2, [], [])
    (from_down[1],) = gate([from_down[1]], [token])
    from_down[2] = send_up(from_down[1])
    (from_up[1],) = gate([from_up[1]], [token])
    from_up[2] = send_down(from_up[1])
    att, dq, dk_own, dk_peer, dv_own, dv_peer, token = attention(
        place, *tokens, heads // 2, heads // 2, held, [from_down[1], from_up[1]]
    )
    from_down[2], att = gate([from_down[2], att], [token])
    from_down[3] = send_up(from_down[2])
    (from_up[2],) = gate([from_up[2]], [token])
    from_up[3] = send_down(from_up[2])
    atts = (att, peer(att))
    share = carried.shape[1] // dp_count

    def swapped(pair, near, far, after=()):
        return peer(pick_other(place, near, far, pair, z_count, after))

    def weigh(pairs, near, far, recv, known=(), after=()):
        return weight_block(
            place, near, far, recv, atts, carried, known, pairs, z_count, dp_count, after
        )

    def exchange(array):
        return lax.all_to_all(array, "dp", 0, 0, tiled=True)

    recv2 = swapped(2, from_down[2], [from_up[2]])
    terms, peaks2 = weigh((2,), [from_down[2]], [[from_up[2]]], [recv2])
    middle = jnp.sum(exchange(terms).astype(F32), axis=0)
    (from_down[3],) = gate([from_down[3]], [peaks2])
    farthest = [send_up(half_of(from_down[3], 0))]
    (from_up[3],) = gate([from_up[3]], [peaks2])
    farthest.append(send_down(half_of(from_up[3], 1)))
    recv1 = swapped(1, from_down[1], [from_up[3]])
    recv3 = swapped(3, from_down[3], [from_up[1]])
    terms, peaks13 = weigh(
        (1, 3),
        [from_down[1], from_down[3]],
        [[from_up[3]], [from_up[1]]],
        [recv1, recv3],
    )
    *farthest, terms = gate([*farthest, terms], [peaks13, middle])
    sides = exchange(terms)
    recv0 = swapped(0, own, farthest)
    terms, _ = weigh((0,), [own], [farthest], [recv0], (peaks13, peaks2))
    last = exchange(terms)
    d_keys, d_values = add_pairs(dk_own, peer(dk_peer), dv_own, peer(dv_peer))
    level_sums, block_scale = finish(
        place,
        last,
        jnp.sum(sides.astype(F32), axis=0),
        middle,
        share,
        z_count,
    )
    return dq[None], d_keys[None], d_values[None], level_sums, block_scale


def solution(mesh):
    tokens = P("dp", "seq", "tensor")
    in_specs = (tokens,) * 5 + (P("dp", "seq", None, "tensor"), P("dp", None))
    out_specs = (tokens,) * 3 + (P("seq", "dp", "tensor"), P("seq", "tensor"))
    return jax.shard_map(body, mesh=mesh, in_specs=in_specs, out_specs=out_specs, check_vma=False)
```

time: 148 us -> 109 us (0.74)
  other arithmetic: 15.5 us -> 3.23 us
  Pallas kernels: 28.7 us -> 40.3 us
  local copies, waits for them, and re-layouts: 14.6 us -> 3.7 us
  between operations: 11.5 us -> 0.89 us
  waiting for transfers between devices: 33.6 us -> 24 us
  starting transfers between devices: 42.1 us -> 36.5 us
    ppermute x8, waiting for transfers between devices: 19.9 us -> 5.49 us  [the longest x4 5.48 us: send_up(): return lax.ppermute(array, 'tensor', up)]
    pallas_call x6 -> x20, Pallas kernels: 28.7 us -> 40.3 us  [the longest x2 18.1 us: attention(): pl.pallas_call(functools.partial(attention_kernel, tile=256, first=first,...]
    select_n x5 -> x0, other arithmetic: 8.12 us -> none  [the longest x4 8.11 us: body(): recv = peer(jnp.where(keep_near, far, near))]
    all_to_all x4 -> x3, starting transfers between devices: 25 us -> 18.6 us  [exchange(): return lax.all_to_all(array, 'dp', 0, 0, tiled=True)]
    unnamed x25 -> x20, local copies, waits for them, and re-layouts: 9.76 us -> 3.7 us
    ppermute x9, waiting for transfers between devices: 0.02 us -> 4.27 us  [peer(): return lax.ppermute(array, 'seq', swap)]
    broadcast_in_dim x2 -> x0, other arithmetic: 4.01 us -> none  [body(): return (dq[None], d_keys[None], d_values[None], level_sums, block_scale)]
    slice x4 -> x0, local copies, waits for them, and re-layouts: 3.9 us -> none  [the longest x1 1.67 us: body(): from_up[3][half:]]
  transfers between devices with their start and end apart: 21 -> 20, of which waited for: 5 -> 9; matrix products, arithmetic and copies ran while one was open for 15% -> 3% of each run, Pallas kernels for 19% -> 36%
where the time goes in v2:
time: 109 us
  Pallas kernels  40.3 us (37%)
  starting transfers between devices  36.5 us (33%)
  waiting for transfers between devices  24 us (22%)
  local copies, waits for them, and re-layouts  3.7 us (3%)
  other arithmetic  3.23 us (3%)
    all_to_all x3, starting transfers between devices, exchange(): return lax.all_to_all(array, 'dp', 0, 0, tiled=True)  18.6 us
    pallas_call x2, Pallas kernels, attention(): pl.pallas_call(functools.partial(attention_kernel, tile=256, first=first,...  18.1 us
    all_to_all x3, waiting for transfers between devices, exchange(): return lax.all_to_all(array, 'dp', 0, 0, tiled=True)  14.2 us
    ppermute x4, starting transfers between devices, send_down(): return lax.ppermute(array, 'tensor', down)  13.2 us
    pallas_call x3, Pallas kernels, weight_block(): pl.pallas_call(functools.partial(weight_kernel, pairs=pairs, pieces=piece...  12.7 us
    ppermute x4, waiting for transfers between devices, send_up(): return lax.ppermute(array, 'tensor', up)  5.48 us
    pallas_call x4, Pallas kernels, pick_other(): pl.pallas_call(functools.partial(pick_kernel, pair=pair, chips=chips, cou...  5.07 us
    ppermute x9, waiting for transfers between devices, peer(): return lax.ppermute(array, 'seq', swap)  4.27 us
  transfers between devices with their start and end apart: 20, of which 9 were waited for; matrix products, arithmetic and copies ran while one was open for 3% of the time, Pallas kernels for 36%

profile of v2, /device:TPU:2, one launch (start us, length us, event | category | flops | bytes accessed | tf_op | source)
XLA Modules:
  0.0 108.5 jit_solution(14996701990255646094)
XLA Ops:
  1.2 1.9 %collective-permute-start.2 = (bf16[512,512]{1,0:T(8,128)(2,1)}, bf16[512,512]{1,0:T(8,128)(2,1)S(1)}, u32[]{:S(2)}, u32[]{:S(2)}) collective-permute-start(bf16[512,512]{1,0:T(8,128)(2,1)} %bitcast.12), channel_id=1, source_target_pairs={{0,1},{1,2},{2,3},{3,4},{4,5},{5,6},{6,7},{7,0},{8,9},{9,10},{10,1... | collective-permute-start | bytes 1572872 | tf_op jit(solution)/shard_map/ppermute | solution.py:410
  3.1 3.9 %collective-permute-start.3 = (bf16[512,512]{1,0:T(8,128)(2,1)}, bf16[512,512]{1,0:T(8,128)(2,1)S(1)}, u32[]{:S(2)}, u32[]{:S(2)}) collective-permute-start(bf16[512,512]{1,0:T(8,128)(2,1)} %bitcast.13), channel_id=1, source_target_pairs={{0,7},{1,0},{2,1},{3,2},{4,3},{5,4},{6,5},{7,6},{8,15},{9,8},{10,9... | collective-permute-start | bytes 1572872 | tf_op jit(solution)/shard_map/ppermute | solution.py:413
  7.8 9.1 %attention.2 = (bf16[512,512]{1,0:T(8,128)(2,1)S(1)}, bf16[512,512]{1,0:T(8,128)(2,1)}, bf16[512,512]{1,0:T(8,128)(2,1)S(1)}, bf16[512,512]{1,0:T(8,128)(2,1)S(1...) custom-call(s32[6]{0:T(128)S(1)} %pad_add_fusion.place_ref, ...), custom_call_target="tpu_custom_call" | custom-call | flops 230000000 | tf_op jit(solution)/shard_map/attention/pallas_call | solution.py:115
  16.9 2.6 %collective-permute-done.2.refs_0_ = bf16[512,512]{1,0:T(8,128)(2,1)S(1)} collective-permute-done((bf16[512,512]{1,0:T(8,128)(2,1)}, bf16[512,512]{1,0:T(8,128)(2,1)S(1)}, u32[]{:S(2)}, u32[]{:S(2)}) %collective-permute-start.2) | collective-permute-done | bytes 524320 | tf_op jit(solution)/shard_map/ppermute | solution.py:410
  19.5 3.2 %collective-permute-start.8 = (bf16[512,512]{1,0:T(8,128)(2,1)S(1)}, bf16[512,512]{1,0:T(8,128)(2,1)}, u32[]{:S(2)}, u32[]{:S(2)}) collective-permute-start(bf16[512,512]{1,0:T(8,128)(2,1)S(1)} %gate.8.refs_7_.refs_0_.refs_5_), channel_id=1, source_target_pairs={{0,7},{1,0},{2,1},{3,2},{4,3},{5,4},{6,5},{7,6},{8,15},{9,8},{10,9... | collective-permute-start | bytes 1572872 | tf_op jit(solution)/shard_map/ppermute | solution.py:413
  22.7 9.1 %attention.3 = (bf16[512,512]{1,0:T(8,128)(2,1)S(1)}, bf16[512,512]{1,0:T(8,128)(2,1)}, bf16[512,512]{1,0:T(8,128)(2,1)S(1)}, bf16[512,512]{1,0:T(8,128)(2,1)S(1...) custom-call(s32[6]{0:T(128)S(1)} %pad_add_fusion.place_ref, ...), custom_call_target="tpu_custom_call", output_to_operand_aliasing={{0}: (7, {}), {1}: (8, {}), {2}: (9, {}), {3}: (10, {}), {4... | custom-call | flops 230000000 | tf_op jit(solution)/shard_map/attention/pallas_call | solution.py:115
  31.8 2.4 %collective-permute-done.6.refs_0_ = bf16[512,512]{1,0:T(8,128)(2,1)} collective-permute-done((bf16[512,512]{1,0:T(8,128)(2,1)S(1)}, bf16[512,512]{1,0:T(8,128)(2,1)}, u32[]{:S(2)}, u32[]{:S(2)}) %collective-permute-start.6) | collective-permute-done | bytes 524320 | tf_op jit(solution)/shard_map/ppermute | solution.py:410
  34.2 1.3 %pick_other.4 = bf16[512,512]{1,0:T(8,128)(2,1)S(1)} custom-call(s32[6]{0:T(128)S(1)} %pad_add_fusion.place_ref, bf16[512,512]{1,0:T(8,128)(2,1)} %get-tuple-element.49.near_ref.refs_0_, bf16[512,512]{1,0:T(8,128)(2,1)} %gate.10.refs_0_.refs_2_), custom_call_target="tpu_custom_call" | custom-call | flops 115000 | tf_op jit(solution)/shard_map/pick_other/pallas_call | solution.py:200
  36.1 3.2 %collective-permute-start.12 = (bf16[512,512]{1,0:T(8,128)(2,1)}, bf16[512,512]{1,0:T(8,128)(2,1)S(1)}, u32[]{:S(2)}, u32[]{:S(2)}) collective-permute-start(bf16[512,512]{1,0:T(8,128)(2,1)} %gate.10.refs_0_.refs_2_), channel_id=1, source_target_pairs={{0,7},{1,0},{2,1},{3,2},{4,3},{5,4},{6,5},{7,6},{8,15},{9,8},{10,9... | collective-permute-start | bytes 1572872 | tf_op jit(solution)/shard_map/ppermute | solution.py:413
  39.4 3.4 %weight_block.3 = (bf16[16,32,512]{2,1,0:T(8,128)(2,1)S(1)}, f32[2,512]{1,0:T(2,128)S(1)}) custom-call(s32[6]{0:T(128)S(1)} %pad_add_fusion.place_ref, bf16[512,512]{1,0:T(8,128)(2,1)} %get-tuple-element.49.near_ref.refs_0_, bf16[512,512]{1,0:T(8,128)(2,1)S(1)} %collective-permute-done.9.refs_1_, bf16[512,512]{1,0:T(8,128)(2,1)} %gate.10.refs_0_.refs_2_, ...), custom_call_target="tpu_custom_call" | custom-call | flops 115000 | tf_op jit(solution)/shard_map/weight_block/pallas_call | solution.py:297
  42.8 0.8 copy-done.7
  43.6 7.5 %all-to-all-start = ((bf16[16,32,512]{2,1,0:T(8,128)(2,1)}), bf16[16,32,512]{2,1,0:T(8,128)(2,1)}, u32[]{:S(2)}, u32[]{:S(2)}) async-start(bf16[16,32,512]{2,1,0:T(8,128)(2,1)} %copy-done.7), calls=%async_computation | async-start | bytes 1048576 | tf_op jit(solution)/shard_map/all_to_all | solution.py:452
  51.6 1.4 %pick_other.6 = bf16[512,512]{1,0:T(8,128)(2,1)} custom-call(s32[6]{0:T(128)S(1)} %pad_add_fusion.place_ref, bf16[512,512]{1,0:T(8,128)(2,1)S(1)} %gate.11.whole_ref.near_ref.refs_1_, bf16[512,512]{1,0:T(8,128)(2,1)S(1)} %gate.8.refs_7_.refs_0_.refs_5_), custom_call_target="tpu_custom_call" | custom-call | flops 115000 | tf_op jit(solution)/shard_map/pick_other/pallas_call | solution.py:200
  53.0 1.4 %pick_other.5 = bf16[512,512]{1,0:T(8,128)(2,1)} custom-call(s32[6]{0:T(128)S(1)} %pad_add_fusion.place_ref, bf16[512,512]{1,0:T(8,128)(2,1)S(1)} %gate.7.refs_6_.near_ref.refs_0_, bf16[512,512]{1,0:T(8,128)(2,1)S(1)} %gate.12.whole_ref.refs_0_.refs_4_), custom_call_target="tpu_custom_call" | custom-call | flops 115000 | tf_op jit(solution)/shard_map/pick_other/pallas_call | solution.py:200
  56.9 2.7 %collective-permute-start.13 = (bf16[256,512]{1,0:T(8,128)(2,1)}, bf16[256,512]{1,0:T(8,128)(2,1)}, u32[]{:S(2)}, u32[]{:S(2)}) collective-permute-start(bf16[256,512]{1,0:T(8,128)(2,1)} %half_of.3), channel_id=1, source_target_pairs={{0,7},{1,0},{2,1},{3,2},{4,3},{5,4},{6,5},{7,6},{8,15},{9,8},{10,9... | collective-permute-start | bytes 786440 | tf_op jit(solution)/shard_map/ppermute | solution.py:413
  59.6 1.6 %all-to-all-done = bf16[16,32,512]{2,1,0:T(8,128)(2,1)} async-done(((bf16[16,32,512]{2,1,0:T(8,128)(2,1)}), bf16[16,32,512]{2,1,0:T(8,128)(2,1)}, u32[]{:S(2)}, u32[]{:S(2)}) %all-to-all-start) | async-done | bytes 524320 | tf_op jit(solution)/shard_map/all_to_all | solution.py:452
  61.2 1.1 %convert_reduce_fusion.1.refs_4_.middle_ref = f32[32,512]{1,0:T(8,128)S(1)} fusion(bf16[16,32,512]{2,1,0:T(8,128)(2,1)} %all-to-all-done), kind=kLoop, calls=%fused_computation.1 | loop fusion | flops 507904 | bytes 589824 | tf_op jit(solution)/shard_map/reduce_sum | solution.py:456
  62.4 5.2 %weight_block.4 = (bf16[16,64,512]{2,1,0:T(8,128)(2,1)S(1)}, f32[4,512]{1,0:T(4,128)S(1)}) custom-call(s32[6]{0:T(128)S(1)} %pad_add_fusion.place_ref, bf16[512,512]{1,0:T(8,128)(2,1)S(1)} %gate.7.refs_6_.near_ref.refs_0_, bf16[512,512]{1,0:T(8,128)(2,1)S(1)} %gate.11.whole_ref.near_ref.refs_1_, bf16[512,512]{1,0:T(8,128)(2,1)} %collective-permute-done.14.refs_2_, ...), custom_call_target="tpu_custom_call" | custom-call | flops 115000 | tf_op jit(solution)/shard_map/weight_block/pallas_call | solution.py:297
  67.6 0.9 copy-done
  68.6 5.9 %all-to-all-start.2 = ((bf16[16,64,512]{2,1,0:T(8,128)(2,1)}), bf16[16,64,512]{2,1,0:T(8,128)(2,1)}, u32[]{:S(2)}, u32[]{:S(2)}) async-start(bf16[16,64,512]{2,1,0:T(8,128)(2,1)} %copy-done), calls=%async_computation.2 | async-start | bytes 2097152 | tf_op jit(solution)/shard_map/all_to_all | solution.py:452
  74.5 1.0 copy-done.1
  75.5 1.0 pick_other.7
  76.6 1.9 %collective-permute-done.16.refs_1_ = bf16[512,512]{1,0:T(8,128)(2,1)S(1)} collective-permute-done((bf16[512,512]{1,0:T(8,128)(2,1)S(1)}, bf16[512,512]{1,0:T(8,128)(2,1)S(1)}, u32[]{:S(2)}, u32[]{:S(2)}) %collective-permute-start.16) | collective-permute-done | bytes 524320 | tf_op jit(solution)/shard_map/ppermute | solution.py:403
  78.5 4.0 %weight_block.5 = (bf16[16,48,512]{2,1,0:T(8,128)(2,1)S(1)}, f32[2,512]{1,0:T(2,128)}) custom-call(s32[6]{0:T(128)S(1)} %pad_add_fusion.place_ref, bf16[512,512]{1,0:T(8,128)(2,1)S(1)} %bitcast.15, bf16[512,512]{1,0:T(8,128)(2,1)S(1)} %collective-permute-done.16.refs_1_, bf16[256,512]{1,0:T(8,128)(2,1)S(1)} %get-tuple-element.55.refs_0_.refs_2_, ...), custom_call_target="tpu_custom_call" | custom-call | flops 115000 | tf_op jit(solution)/shard_map/weight_block/pallas_call | solution.py:297
  82.6 0.9 copy-done.6
  83.5 6.5 %all-to-all-done.2 = bf16[16,64,512]{2,1,0:T(8,128)(2,1)} async-done(((bf16[16,64,512]{2,1,0:T(8,128)(2,1)}), bf16[16,64,512]{2,1,0:T(8,128)(2,1)}, u32[]{:S(2)}, u32[]{:S(2)}) %all-to-all-start.2) | async-done | bytes 1048608 | tf_op jit(solution)/shard_map/all_to_all | solution.py:452
  90.0 5.3 %all-to-all-start.1 = ((bf16[16,48,512]{2,1,0:T(8,128)(2,1)}), bf16[16,48,512]{2,1,0:T(8,128)(2,1)S(1)}, u32[]{:S(2)}, u32[]{:S(2)}) async-start(bf16[16,48,512]{2,1,0:T(8,128)(2,1)} %copy-done.6), calls=%async_computation.1 | async-start | bytes 1572864 | tf_op jit(solution)/shard_map/all_to_all | solution.py:452
  95.8 1.6 %collective-permute-done.4.b_ref = bf16[512,512]{1,0:T(8,128)(2,1)S(1)} collective-permute-done((bf16[512,512]{1,0:T(8,128)(2,1)}, bf16[512,512]{1,0:T(8,128)(2,1)S(1)}, u32[]{:S(2)}, u32[]{:S(2)}) %collective-permute-start.4) | collective-permute-done | bytes 524320 | tf_op jit(solution)/shard_map/ppermute | solution.py:403
  98.1 1.6 %add_pairs.1 = (bf16[512,512]{1,0:T(8,128)(2,1)}, bf16[512,512]{1,0:T(8,128)(2,1)}) custom-call(bf16[512,512]{1,0:T(8,128)(2,1)S(1)} %copy-done.3, bf16[512,512]{1,0:T(8,128)(2,1)S(1)} %collective-permute-done.4.b_ref, bf16[512,512]{1,0:T(8,128)(2,1)S(1)} %copy-done.5, bf16[512,512]{1,0:T(8,128)(2,1)S(1)} %collective-permute-done.5.d_ref), custom_call_target="tpu_custom_call" | custom-call | flops 115000 | tf_op jit(solution)/shard_map/add_pairs/pallas_call | solution.py:343
  99.7 1.4 %convert_reduce_fusion.sides_ref = f32[64,512]{1,0:T(8,128)S(1)} fusion(bf16[16,64,512]{2,1,0:T(8,128)(2,1)} %all-to-all-done.2), kind=kLoop, calls=%fused_computation | loop fusion | flops 1015808 | bytes 1179648 | tf_op jit(solution)/shard_map/reduce_sum | solution.py:478
  101.1 6.1 %all-to-all-done.1.last_ref = bf16[16,48,512]{2,1,0:T(8,128)(2,1)S(1)} async-done(((bf16[16,48,512]{2,1,0:T(8,128)(2,1)}), bf16[16,48,512]{2,1,0:T(8,128)(2,1)S(1)}, u32[]{:S(2)}, u32[]{:S(2)}) %all-to-all-start.1) | async-done | bytes 786464 | tf_op jit(solution)/shard_map/all_to_all | solution.py:452
  107.2 1.4 %finish.1 = (f32[8,16,512]{2,1,0:T(8,128)}, f32[8,512]{1,0:T(8,128)}) custom-call(s32[6]{0:T(128)S(1)} %pad_add_fusion.place_ref, bf16[16,48,512]{2,1,0:T(8,128)(2,1)S(1)} %all-to-all-done.1.last_ref, f32[64,512]{1,0:T(8,128)S(1)} %convert_reduce_fusion.sides_ref, f32[32,512]{1,0:T(8,128)S(1)} %convert_reduce_fusion.1.refs_4_.middle_ref), custom_call_target="tpu_custom_call" | custom-call | flops 115000 | tf_op jit(solution)/shard_map/finish/pallas_call | solution.py:379
  (51 shorter events, 6.3 us)
Async XLA Ops:
  0.6 7.2 %collective-permute-start = (bf16[512,512]{1,0:T(8,128)(2,1)}, bf16[512,512]{1,0:T(8,128)(2,1)S(1)}, u32[]{:S(2)}, u32[]{:S(2)}) collective-permute-start(bf16[512,512]{1,0:T(8,128)(2,1)} %bitcast.19), channel_id=1, source_target_pairs={{0,8},{8,0},{1,9},{9,1},{2,10},{10,2},{3,11},{11,3},{4,12},{12,4},... | collective-permute-start | bytes 1572872 | tf_op jit(solution)/shard_map/ppermute | solution.py:403
  0.7 7.1 %collective-permute-start.1 = (bf16[512,512]{1,0:T(8,128)(2,1)}, bf16[512,512]{1,0:T(8,128)(2,1)S(1)}, u32[]{:S(2)}, u32[]{:S(2)}) collective-permute-start(bf16[512,512]{1,0:T(8,128)(2,1)} %bitcast.22), channel_id=1, source_target_pairs={{0,8},{8,0},{1,9},{9,1},{2,10},{10,2},{3,11},{11,3},{4,12},{12,4},... | collective-permute-start | bytes 1572872 | tf_op jit(solution)/shard_map/ppermute | solution.py:403
  1.2 18.3 %collective-permute-start.2 = (bf16[512,512]{1,0:T(8,128)(2,1)}, bf16[512,512]{1,0:T(8,128)(2,1)S(1)}, u32[]{:S(2)}, u32[]{:S(2)}) collective-permute-start(bf16[512,512]{1,0:T(8,128)(2,1)} %bitcast.12), channel_id=1, source_target_pairs={{0,1},{1,2},{2,3},{3,4},{4,5},{5,6},{6,7},{7,0},{8,9},{9,10},{10,1... | collective-permute-start | bytes 1572872 | tf_op jit(solution)/shard_map/ppermute | solution.py:410
  3.1 16.3 %collective-permute-start.3 = (bf16[512,512]{1,0:T(8,128)(2,1)}, bf16[512,512]{1,0:T(8,128)(2,1)S(1)}, u32[]{:S(2)}, u32[]{:S(2)}) collective-permute-start(bf16[512,512]{1,0:T(8,128)(2,1)} %bitcast.13), channel_id=1, source_target_pairs={{0,7},{1,0},{2,1},{3,2},{4,3},{5,4},{6,5},{7,6},{8,15},{9,8},{10,9... | collective-permute-start | bytes 1572872 | tf_op jit(solution)/shard_map/ppermute | solution.py:413
  19.5 14.7 %collective-permute-start.6 = (bf16[512,512]{1,0:T(8,128)(2,1)S(1)}, bf16[512,512]{1,0:T(8,128)(2,1)}, u32[]{:S(2)}, u32[]{:S(2)}) collective-permute-start(bf16[512,512]{1,0:T(8,128)(2,1)S(1)} %gate.7.refs_6_.near_ref.refs_0_), channel_id=1, source_target_pairs={{0,1},{1,2},{2,3},{3,4},{4,5},{5,6},{6,7},{7,0},{8,9},{9,10},{10,1... | collective-permute-start | bytes 1572872 | tf_op jit(solution)/shard_map/ppermute | solution.py:410
  19.5 14.7 %collective-permute-start.8 = (bf16[512,512]{1,0:T(8,128)(2,1)S(1)}, bf16[512,512]{1,0:T(8,128)(2,1)}, u32[]{:S(2)}, u32[]{:S(2)}) collective-permute-start(bf16[512,512]{1,0:T(8,128)(2,1)S(1)} %gate.8.refs_7_.refs_0_.refs_5_), channel_id=1, source_target_pairs={{0,7},{1,0},{2,1},{3,2},{4,3},{5,4},{6,5},{7,6},{8,15},{9,8},{10,9... | collective-permute-start | bytes 1572872 | tf_op jit(solution)/shard_map/ppermute | solution.py:413
  31.8 7.5 %copy-start.2 = (bf16[512,512]{1,0:T(8,128)(2,1)}, bf16[512,512]{1,0:T(8,128)(2,1)S(1)}, u32[]{:S(2)}) copy-start(bf16[512,512]{1,0:T(8,128)(2,1)S(1)} %get-tuple-element.41.a_ref) | copy-start | bytes 1572868
  31.8 7.5 %copy-start.4 = (bf16[512,512]{1,0:T(8,128)(2,1)}, bf16[512,512]{1,0:T(8,128)(2,1)S(1)}, u32[]{:S(2)}) copy-start(bf16[512,512]{1,0:T(8,128)(2,1)S(1)} %get-tuple-element.43.c_ref) | copy-start | bytes 1572868
  31.8 7.5 %copy-start.8 = (bf16[512,512]{1,0:T(8,128)(2,1)}, bf16[512,512]{1,0:T(8,128)(2,1)S(1)}, u32[]{:S(2)}) copy-start(bf16[512,512]{1,0:T(8,128)(2,1)S(1)} %get-tuple-element.42) | copy-start | bytes 1572868
  31.8 7.5 %copy-start.9 = (bf16[512,512]{1,0:T(8,128)(2,1)}, bf16[512,512]{1,0:T(8,128)(2,1)S(1)}, u32[]{:S(2)}) copy-start(bf16[512,512]{1,0:T(8,128)(2,1)S(1)} %get-tuple-element.44) | copy-start | bytes 1572868
  34.2 5.1 %collective-permute-start.10 = (bf16[512,512]{1,0:T(8,128)(2,1)S(1)}, bf16[512,512]{1,0:T(8,128)(2,1)S(1)}, u32[]{:S(2)}, u32[]{:S(2)}) collective-permute-start(bf16[512,512]{1,0:T(8,128)(2,1)S(1)} %get-tuple-element.50.refs_3_.refs_6_.refs_4_), channel_id=1, source_target_pairs={{0,8},{8,0},{1,9},{9,1},{2,10},{10,2},{3,11},{11,3},{4,12},{12,4},... | collective-permute-start | bytes 1572872 | tf_op jit(solution)/shard_map/ppermute | solution.py:403
  35.5 3.8 %collective-permute-start.9 = (bf16[512,512]{1,0:T(8,128)(2,1)S(1)}, bf16[512,512]{1,0:T(8,128)(2,1)S(1)}, u32[]{:S(2)}, u32[]{:S(2)}) collective-permute-start(bf16[512,512]{1,0:T(8,128)(2,1)S(1)} %pick_other.4), channel_id=1, source_target_pairs={{0,8},{8,0},{1,9},{9,1},{2,10},{10,2},{3,11},{11,3},{4,12},{12,4},... | collective-permute-start | bytes 1572872 | tf_op jit(solution)/shard_map/ppermute | solution.py:403
  36.1 15.5 %collective-permute-start.7 = (bf16[512,512]{1,0:T(8,128)(2,1)}, bf16[512,512]{1,0:T(8,128)(2,1)S(1)}, u32[]{:S(2)}, u32[]{:S(2)}) collective-permute-start(bf16[512,512]{1,0:T(8,128)(2,1)} %get-tuple-element.49.near_ref.refs_0_), channel_id=1, source_target_pairs={{0,1},{1,2},{2,3},{3,4},{4,5},{5,6},{6,7},{7,0},{8,9},{9,10},{10,1... | collective-permute-start | bytes 1572872 | tf_op jit(solution)/shard_map/ppermute | solution.py:410
  36.1 16.9 %collective-permute-start.12 = (bf16[512,512]{1,0:T(8,128)(2,1)}, bf16[512,512]{1,0:T(8,128)(2,1)S(1)}, u32[]{:S(2)}, u32[]{:S(2)}) collective-permute-start(bf16[512,512]{1,0:T(8,128)(2,1)} %gate.10.refs_0_.refs_2_), channel_id=1, source_target_pairs={{0,7},{1,0},{2,1},{3,2},{4,3},{5,4},{6,5},{7,6},{8,15},{9,8},{10,9... | collective-permute-start | bytes 1572872 | tf_op jit(solution)/shard_map/ppermute | solution.py:413
  42.8 0.8 copy-start.7
  43.6 17.6 %all-to-all-start = ((bf16[16,32,512]{2,1,0:T(8,128)(2,1)}), bf16[16,32,512]{2,1,0:T(8,128)(2,1)}, u32[]{:S(2)}, u32[]{:S(2)}) async-start(bf16[16,32,512]{2,1,0:T(8,128)(2,1)} %copy-done.7), calls=%async_computation | async-start | bytes 1048576 | tf_op jit(solution)/shard_map/all_to_all | solution.py:452
  53.0 9.4 %collective-permute-start.15 = (bf16[512,512]{1,0:T(8,128)(2,1)}, bf16[512,512]{1,0:T(8,128)(2,1)}, u32[]{:S(2)}, u32[]{:S(2)}) collective-permute-start(bf16[512,512]{1,0:T(8,128)(2,1)} %pick_other.6), channel_id=1, source_target_pairs={{0,8},{8,0},{1,9},{9,1},{2,10},{10,2},{3,11},{11,3},{4,12},{12,4},... | collective-permute-start | bytes 1572872 | tf_op jit(solution)/shard_map/ppermute | solution.py:403
  54.4 8.0 %collective-permute-start.14 = (bf16[512,512]{1,0:T(8,128)(2,1)}, bf16[512,512]{1,0:T(8,128)(2,1)}, u32[]{:S(2)}, u32[]{:S(2)}) collective-permute-start(bf16[512,512]{1,0:T(8,128)(2,1)} %pick_other.5), channel_id=1, source_target_pairs={{0,8},{8,0},{1,9},{9,1},{2,10},{10,2},{3,11},{11,3},{4,12},{12,4},... | collective-permute-start | bytes 1572872 | tf_op jit(solution)/shard_map/ppermute | solution.py:403
  55.6 12.0 %collective-permute-start.11 = (bf16[256,512]{1,0:T(8,128)(2,1)}, bf16[256,512]{1,0:T(8,128)(2,1)S(1)}, u32[]{:S(2)}, u32[]{:S(2)}) collective-permute-start(bf16[256,512]{1,0:T(8,128)(2,1)} %half_of.2), channel_id=1, source_target_pairs={{0,1},{1,2},{2,3},{3,4},{4,5},{5,6},{6,7},{7,0},{8,9},{9,10},{10,1... | collective-permute-start | bytes 786440 | tf_op jit(solution)/shard_map/ppermute | solution.py:410
  56.9 10.7 %collective-permute-start.13 = (bf16[256,512]{1,0:T(8,128)(2,1)}, bf16[256,512]{1,0:T(8,128)(2,1)}, u32[]{:S(2)}, u32[]{:S(2)}) collective-permute-start(bf16[256,512]{1,0:T(8,128)(2,1)} %half_of.3), channel_id=1, source_target_pairs={{0,7},{1,0},{2,1},{3,2},{4,3},{5,4},{6,5},{7,6},{8,15},{9,8},{10,9... | collective-permute-start | bytes 786440 | tf_op jit(solution)/shard_map/ppermute | solution.py:413
  67.6 1.0 copy-start
  68.6 21.4 %all-to-all-start.2 = ((bf16[16,64,512]{2,1,0:T(8,128)(2,1)}), bf16[16,64,512]{2,1,0:T(8,128)(2,1)}, u32[]{:S(2)}, u32[]{:S(2)}) async-start(bf16[16,64,512]{2,1,0:T(8,128)(2,1)} %copy-done), calls=%async_computation.2 | async-start | bytes 2097152 | tf_op jit(solution)/shard_map/all_to_all | solution.py:452
  74.4 1.0 copy-start.1
  76.5 21.6 %copy-start.3 = (bf16[512,512]{1,0:T(8,128)(2,1)S(1)}, bf16[512,512]{1,0:T(8,128)(2,1)}, u32[]{:S(2)}) copy-start(bf16[512,512]{1,0:T(8,128)(2,1)} %copy-done.2) | copy-start | bytes 1572868
  76.5 21.6 %copy-start.5 = (bf16[512,512]{1,0:T(8,128)(2,1)S(1)}, bf16[512,512]{1,0:T(8,128)(2,1)}, u32[]{:S(2)}) copy-start(bf16[512,512]{1,0:T(8,128)(2,1)} %copy-done.4) | copy-start | bytes 1572868
  76.5 2.0 %collective-permute-start.16 = (bf16[512,512]{1,0:T(8,128)(2,1)S(1)}, bf16[512,512]{1,0:T(8,128)(2,1)S(1)}, u32[]{:S(2)}, u32[]{:S(2)}) collective-permute-start(bf16[512,512]{1,0:T(8,128)(2,1)S(1)} %pick_other.7), channel_id=1, source_target_pairs={{0,8},{8,0},{1,9},{9,1},{2,10},{10,2},{3,11},{11,3},{4,12},{12,4},... | collective-permute-start | bytes 1572872 | tf_op jit(solution)/shard_map/ppermute | solution.py:403
  82.6 0.9 copy-start.6
  90.0 17.2 %all-to-all-start.1 = ((bf16[16,48,512]{2,1,0:T(8,128)(2,1)}), bf16[16,48,512]{2,1,0:T(8,128)(2,1)S(1)}, u32[]{:S(2)}, u32[]{:S(2)}) async-start(bf16[16,48,512]{2,1,0:T(8,128)(2,1)} %copy-done.6), calls=%async_computation.1 | async-start | bytes 1572864 | tf_op jit(solution)/shard_map/all_to_all | solution.py:452
  95.2 2.1 %collective-permute-start.4 = (bf16[512,512]{1,0:T(8,128)(2,1)}, bf16[512,512]{1,0:T(8,128)(2,1)S(1)}, u32[]{:S(2)}, u32[]{:S(2)}) collective-permute-start(bf16[512,512]{1,0:T(8,128)(2,1)} %copy-done.8), channel_id=1, source_target_pairs={{0,8},{8,0},{1,9},{9,1},{2,10},{10,2},{3,11},{11,3},{4,12},{12,4},... | collective-permute-start | bytes 1572872 | tf_op jit(solution)/shard_map/ppermute | solution.py:403
  95.3 2.9 %collective-permute-start.5 = (bf16[512,512]{1,0:T(8,128)(2,1)}, bf16[512,512]{1,0:T(8,128)(2,1)S(1)}, u32[]{:S(2)}, u32[]{:S(2)}) collective-permute-start(bf16[512,512]{1,0:T(8,128)(2,1)} %copy-done.9), channel_id=1, source_target_pairs={{0,8},{8,0},{1,9},{9,1},{2,10},{10,2},{3,11},{11,3},{4,12},{12,4},... | collective-permute-start | bytes 1572872 | tf_op jit(solution)/shard_map/ppermute | solution.py:403

commit v3 on v2

--- a/solution.py
+++ b/solution.py
@@ -13,6 +13,7 @@
 F32 = jnp.float32
 BF16 = jnp.bfloat16
 MIB = 2**20
+LANES = 128
 TOKEN = jax.ShapeDtypeStruct((8, 128), F32)
 TOKEN_SPEC = pl.BlockSpec((8, 128), lambda i, *_: (0, 0))
 
@@ -103,9 +104,10 @@
     dvp_ref[...] = dv_acc[rows:].astype(BF16)
 
 
-def cost(microseconds):
+def cost(microseconds, *arrays):
+    size = sum(array.size * array.dtype.itemsize for array in arrays)
     return pl.CostEstimate(
-        flops=int(microseconds * 1.15e9), bytes_accessed=0, transcendentals=0
+        flops=int(microseconds * 1.15e9), bytes_accessed=size, transcendentals=0
     )
 
 
@@ -129,9 +131,11 @@
                 pltpu.SemaphoreType.DMA((count, 4)),
             ],
         ),
-        out_shape=[jax.ShapeDtypeStruct((rows, width), BF16)] * 6 + [TOKEN],
+        out_shape=[pltpu.VMEM((rows, width), BF16)]
+        + [pltpu.HBM((rows, width), BF16)] * 5
+        + [TOKEN],
         input_output_aliases={7 + i: i for i in range(len(held))},
-        compiler_params=pltpu.CompilerParams(vmem_limit_bytes=24 * MIB),
+        compiler_params=pltpu.CompilerParams(vmem_limit_bytes=18 * MIB),
         cost_estimate=cost(0.2),
         name="attention",
     )(place, kp, vp, q, ko, vo, g, *held, *after)
@@ -141,36 +145,18 @@
     pass
 
 
-def gate(arrays, after):
+def gate(arrays, after, microseconds=0.01, space=jax.ShapeDtypeStruct):
     anywhere = pl.BlockSpec(memory_space=pl.ANY)
     return pl.pallas_call(
         gate_kernel,
         in_specs=[anywhere] * (len(arrays) + len(after)),
         out_specs=[anywhere] * len(arrays),
-        out_shape=[jax.ShapeDtypeStruct(a.shape, a.dtype) for a in arrays],
+        out_shape=[space(a.shape, a.dtype) for a in arrays],
         input_output_aliases={i: i for i in range(len(arrays))},
         compiler_params=pltpu.CompilerParams(vmem_limit_bytes=2 * MIB),
-        cost_estimate=cost(0.0001),
+        cost_estimate=cost(microseconds),
         name="gate",
     )(*arrays, *after)
-
-
-def half_kernel(whole_ref, half_ref, *, start):
-    half_ref[...] = whole_ref[pl.ds(start, half_ref.shape[0]), :]
-
-
-def half_of(array, second):
-    rows, width = array.shape
-    whole = pl.BlockSpec(memory_space=pltpu.VMEM)
-    return pl.pallas_call(
-        functools.partial(half_kernel, start=rows // 2 * second),
-        in_specs=[whole],
-        out_specs=whole,
-        out_shape=jax.ShapeDtypeStruct((rows // 2, width), array.dtype),
-        compiler_params=pltpu.CompilerParams(vmem_limit_bytes=4 * MIB),
-        cost_estimate=cost(0.0001),
-        name="half_of",
-    )(array)
 
 
 def origin(place_ref, pair, chips):
@@ -203,97 +189,156 @@
         + [whole] * (1 + len(far))
         + [pl.BlockSpec(memory_space=pl.ANY)] * len(after),
         out_specs=whole,
-        out_shape=jax.ShapeDtypeStruct((rows, width), near.dtype),
-        compiler_params=pltpu.CompilerParams(vmem_limit_bytes=8 * MIB),
-        cost_estimate=cost(0.0001),
+        out_shape=pltpu.VMEM((rows, width), near.dtype),
+        compiler_params=pltpu.CompilerParams(vmem_limit_bytes=4 * MIB),
+        cost_estimate=cost(0.01),
         name="pick_other",
     )(place, near, *far, *after)
 
 
-def weight_kernel(place_ref, *refs, pairs, pieces, chips, dp_count, after):
-    near, refs = refs[: len(pairs)], refs[len(pairs) :]
-    recv, refs = refs[: len(pairs)], refs[len(pairs) :]
-    far, refs = refs[: len(pairs) * pieces], refs[len(pairs) * pieces :]
-    atts, carried_hbm = refs[:2], refs[2]
-    *known_refs, out_ref, peak_ref, carried_ref, sems = refs[3 + after :]
-    step = pl.program_id(0)
-
-    def fetch(index):
-        block = 2 * spot(place_ref, pairs[index // 2], chips) + index % 2
-        return pltpu.make_async_copy(carried_hbm.at[block], carried_ref.at[index], sems.at[index])
-
-    @pl.when(step == 0)
-    def _():
-        for index in range(2 * len(pairs)):
-            fetch(index).start()
-
-    rows = near[0].shape[0]
-
-    def chunk(side, part, piece):
-        found = None
-        for index, pair in enumerate(pairs):
-            if side:
-                value = recv[index][part, :]
+def fork_kernel(place_ref, down_ref, up_ref, old_down_ref, old_up_ref, *out_refs, chips):
+    top_ref, bottom_ref, first_ref, third_ref = out_refs
+    half = top_ref.shape[0]
+    top_ref[...] = down_ref[:half, :]
+    bottom_ref[...] = up_ref[half:, :]
+    first_ref[...] = jnp.where(
+        owns(place_ref, 1, chips) == 1, up_ref[...], old_down_ref[...]
+    )
+    third_ref[...] = jnp.where(
+        owns(place_ref, 3, chips) == 1, old_up_ref[...], down_ref[...]
+    )
+
+
+def fork(place, down, up, old_down, old_up, chips):
+    rows, width = down.shape
+    vmem = pl.BlockSpec(memory_space=pltpu.VMEM)
+    return pl.pallas_call(
+        functools.partial(fork_kernel, chips=chips),
+        in_specs=[pl.BlockSpec(memory_space=pltpu.SMEM)] + [vmem] * 4,
+        out_specs=[vmem] * 4,
+        out_shape=[jax.ShapeDtypeStruct((rows // 2, width), down.dtype)] * 2
+        + [jax.ShapeDtypeStruct((rows, width), down.dtype)] * 2,
+        compiler_params=pltpu.CompilerParams(vmem_limit_bytes=6 * MIB),
+        cost_estimate=cost(0.01),
+        name="fork",
+    )(place, down, up, old_down, old_up)
+
+
+def weight_kernel(place_ref, *refs, pairs, pieces, chips, dp_count, known, keep_att):
+    count = len(pairs)
+    near, refs = refs[:count], refs[count:]
+    recv, refs = refs[:count], refs[count:]
+    far, refs = refs[: count * pieces], refs[count * pieces :]
+    att_refs, carried_ref, refs = refs[:2], refs[2], refs[3:]
+    known_refs, refs = refs[:known], refs[known:]
+    out_ref, peak_ref, *kept_refs, atts, mine, other, carried, terms, sems, out_sems = refs
+    rows, width = att_refs[0].shape
+    block = carried.shape[1]
+    share = block // dp_count
+    part_rows = rows // pieces
+    groups = width // LANES
+    peak_rows = 8 * groups
+
+    def part(piece):
+        return slice(piece * part_rows, (piece + 1) * part_rows)
+
+    def fetch_mine(index, piece, from_near):
+        source = near[index].at[part(piece)] if from_near else far[index * pieces + piece]
+        return pltpu.make_async_copy(source, mine.at[index, part(piece)], sems.at[1 + piece, index])
+
+    def fetch_other(index):
+        return pltpu.make_async_copy(recv[index], other.at[index], sems.at[0, index])
+
+    def fetch_att(side):
+        return pltpu.make_async_copy(att_refs[side], atts.at[side], sems.at[3, side])
+
+    def fetch_carried(index):
+        place = 2 * spot(place_ref, pairs[index // 2], chips) + index % 2
+        return pltpu.make_async_copy(carried_ref.at[place], carried.at[index], sems.at[4, index])
+
+    def send(index):
+        if known:
+            place = pl.ds(index * groups * share, groups * share if index < 2 * count else peak_rows)
+            return pltpu.make_async_copy(
+                terms.at[:, place], out_ref.at[:, place], out_sems.at[index]
+            )
+        place = pl.ds(index * share, share)
+        return pltpu.make_async_copy(terms.at[index], out_ref.at[:, place], out_sems.at[index])
+
+    def keep_copy():
+        return pltpu.make_async_copy(atts.at[1], kept_refs[0], out_sems.at[2 * count])
+
+    fetch_att(0).start()
+    for index, pair in enumerate(pairs):
+        keep = owns(place_ref, pair, chips) == 1
+        for piece in range(pieces):
+            pl.when(keep)(fetch_mine(index, piece, True).start)
+            pl.when(jnp.logical_not(keep))(fetch_mine(index, piece, False).start)
+        fetch_other(index).start()
+        if index == 0:
+            fetch_att(1).start()
+        fetch_carried(2 * index).start()
+        fetch_carried(2 * index + 1).start()
+    fetch_att(0).wait()
+    for index in range(count):
+        for piece in range(pieces):
+            fetch_mine(index, piece, True).wait()
+        for half in range(2):
+            columns = slice(half * block, (half + 1) * block)
+            corrected = dot_on(mine[index, :, columns], atts[0], 0, 0)
+            if half == 0:
+                fetch_other(index).wait()
+                if index == 0:
+                    fetch_att(1).wait()
+                    if keep_att:
+                        keep_copy().start()
+            corrected = corrected + dot_on(other[index, :, columns], atts[1], 0, 0)
+            slot = 2 * index + half
+            fetch_carried(slot).wait()
+            corrected = corrected + carried[slot]
+            peak_ref[slot : slot + 1, :] = jnp.max(jnp.abs(corrected), axis=0, keepdims=True)
+            rounded = corrected.astype(BF16).reshape(dp_count, share, width)
+            if known:
+                for group in range(groups):
+                    row = (slot * groups + group) * share
+                    lanes = slice(group * LANES, (group + 1) * LANES)
+                    terms[:, row : row + share, :] = rounded[:, :, lanes]
             else:
-                keep = owns(place_ref, pair, chips) == 1
-                value = jnp.where(keep, near[index][part, :], far[index * pieces + piece][...])
-            found = value if index == 0 else jnp.where(step < 2 * index, found, value)
-        return found
-
-    corrected = None
-    for side in range(2):
-        for piece in range(pieces):
-            part = slice(piece * rows // pieces, (piece + 1) * rows // pieces)
-            product = dot_on(chunk(side, part, piece), atts[side][part, :], 0, 0)
-            corrected = product if corrected is None else corrected + product
-    for index in range(2 * len(pairs)):
-
-        @pl.when(step == index)
-        def _():
-            fetch(index).wait()
-
-    corrected = corrected + carried_ref[step]
-    share = corrected.shape[0] // dp_count
-    peak_ref[pl.ds(step, 1), :] = jnp.max(jnp.abs(corrected), axis=0, keepdims=True)
-    rounded = corrected.astype(BF16)
-    place = pl.ds(pl.multiple_of(step * share, share), share)
-    for dest in range(dp_count):
-        out_ref[dest, place, :] = rounded[dest * share : (dest + 1) * share]
-    if known_refs:
-
-        @pl.when(step == 2 * len(pairs) - 1)
-        def _():
-            peaks = jnp.concatenate([peak_ref[...]] + [ref[...] for ref in known_refs], 0)
-            high = peaks.astype(BF16).astype(F32)
-            both = jnp.concatenate([high, peaks - high], 0).astype(BF16)
-            for dest in range(dp_count):
-                out_ref[dest, 2 * len(pairs) * share :, :] = both
-
-
-def weight_block(
-    place, near, far, recv, att, carried, known, pairs, chips, dp_count, after
-):
+                terms[slot] = rounded
+            send(slot).start()
+    slots = 2 * count
+    if known:
+        peaks = jnp.concatenate([peak_ref[...]] + [ref[...] for ref in known_refs], 0)
+        peaks = jnp.concatenate(
+            [peaks[:, group * LANES : (group + 1) * LANES] for group in range(groups)], 0
+        ).astype(BF16)
+        for dest in range(dp_count):
+            terms[dest, slots * groups * share :, :] = peaks
+        send(slots).start()
+        slots += 1
+    for slot in range(slots):
+        send(slot).wait()
+    if keep_att:
+        keep_copy().wait()
+
+
+def weight_block(place, near, far, recv, att, carried, known, pairs, chips, dp_count, keep_att):
     rows, width = att[0].shape
     block = carried.shape[1]
     share = block // dp_count
     count = len(pairs)
     pieces = len(far[0])
-    out_rows = 2 * count * share + (16 if known else 0)
-    whole = lambda i, *_: (0, 0)
-
-    def column(index, wanted):
-        def find(i, ref):
-            return 0, jnp.clip(i - 2 * index, 0, 1) * wanted(owns(ref, pairs[index], chips))
-
-        return find
-
-    near_specs = [pl.BlockSpec((rows, block), column(n, lambda own: own)) for n in range(count)]
-    recv_specs = [pl.BlockSpec((rows, block), column(n, lambda own: 1)) for n in range(count)]
-    far_specs = [
-        pl.BlockSpec((rows // pieces, block), column(n, lambda own: 1 - own))
-        for n in range(count)
-        for _ in range(pieces)
-    ]
+    if known:
+        groups = width // LANES
+        out_rows = 2 * count * groups * share + 8 * groups
+        out_shape = pltpu.HBM((dp_count, out_rows, LANES), BF16)
+        terms = pltpu.VMEM((dp_count, out_rows, LANES), BF16)
+    else:
+        out_shape = pltpu.HBM((dp_count, 2 * count * share, width), BF16)
+        terms = pltpu.VMEM((2 * count, dp_count, share, width), BF16)
+    vmem = pl.BlockSpec(memory_space=pltpu.VMEM)
+    anywhere = pl.BlockSpec(memory_space=pl.ANY)
+    hbm = pl.BlockSpec(memory_space=pltpu.HBM)
     return pl.pallas_call(
         functools.partial(
             weight_kernel,
@@ -301,35 +346,29 @@
             pieces=pieces,
             chips=chips,
             dp_count=dp_count,
-            after=len(after),
+            known=len(known),
+            keep_att=keep_att,
         ),
-        grid_spec=pltpu.PrefetchScalarGridSpec(
-            num_scalar_prefetch=1,
-            grid=(2 * count,),
-            in_specs=near_specs
-            + recv_specs
-            + far_specs
-            + [pl.BlockSpec((rows, width), whole)] * 2
-            + [pl.BlockSpec(memory_space=pltpu.HBM)]
-            + [pl.BlockSpec(memory_space=pl.ANY)] * len(after)
-            + [pl.BlockSpec(array.shape, whole) for array in known],
-            out_specs=[
-                pl.BlockSpec((dp_count, out_rows, width), lambda i, *_: (0, 0, 0)),
-                pl.BlockSpec((2 * count, width), whole),
-            ],
-            scratch_shapes=[
-                pltpu.VMEM((2 * count, block, width), F32),
-                pltpu.SemaphoreType.DMA((2 * count,)),
-            ],
-        ),
-        out_shape=[
-            jax.ShapeDtypeStruct((dp_count, out_rows, width), BF16),
-            jax.ShapeDtypeStruct((2 * count, width), F32),
+        in_specs=[pl.BlockSpec(memory_space=pltpu.SMEM)]
+        + [anywhere] * (count * (2 + pieces) + 2)
+        + [hbm]
+        + [vmem] * len(known),
+        out_specs=[hbm, vmem] + [hbm] * keep_att,
+        out_shape=[out_shape, jax.ShapeDtypeStruct((2 * count, width), F32)]
+        + [pltpu.HBM((rows, width), BF16)] * keep_att,
+        scratch_shapes=[
+            pltpu.VMEM((2, rows, width), BF16),
+            pltpu.VMEM((count, rows, 2 * block), BF16),
+            pltpu.VMEM((count, rows, 2 * block), BF16),
+            pltpu.VMEM((2 * count, block, width), F32),
+            terms,
+            pltpu.SemaphoreType.DMA((5, 2 * max(count, 1))),
+            pltpu.SemaphoreType.DMA((2 * count + 1,)),
         ],
-        compiler_params=pltpu.CompilerParams(vmem_limit_bytes=28 * MIB),
-        cost_estimate=cost(0.0001),
+        compiler_params=pltpu.CompilerParams(vmem_limit_bytes=20 * MIB),
+        cost_estimate=cost(0.1),
         name="weight_block",
-    )(place, *near, *recv, *[p for f in far for p in f], *att, carried, *after, *known)
+    )(place, *near, *recv, *[p for f in far for p in f], *att, carried, *known)
 
 
 def add_kernel(a_ref, b_ref, c_ref, d_ref, first_ref, second_ref):
@@ -347,34 +386,39 @@
         out_specs=[spec] * 2,
         out_shape=[jax.ShapeDtypeStruct((rows, width), BF16)] * 2,
         compiler_params=pltpu.CompilerParams(vmem_limit_bytes=8 * MIB),
-        cost_estimate=cost(0.0001),
+        cost_estimate=cost(0.1),
         name="add_pairs",
     )(a, b, c, d)
 
 
 def finish_kernel(place_ref, last_ref, sides_ref, middle_ref, levels_ref, scale_ref, *, chips):
-    share = levels_ref.shape[1]
-    head = 2 * share
-    peaks = jnp.max(
-        last_ref[:, head : head + 8, :].astype(F32) + last_ref[:, head + 8 : head + 16, :].astype(F32),
-        axis=0,
-    )
-    scale = (peaks + 1e-6) / 7.0
+    share, width = levels_ref.shape[1:]
+    groups = width // LANES
+    rows = 2 * groups * share
+    total = jnp.sum(last_ref[:, :rows, :].astype(F32), axis=0)
+    peaks = jnp.max(last_ref[:, rows:, :].astype(F32), axis=0)
+    scale = jnp.concatenate([peaks[group * 8 : group * 8 + 8] for group in range(groups)], 1)
+    scale = (scale + 1e-6) / 7.0
     for index, pair in enumerate((0, 1, 3, 2)):
         for half in range(2):
             block = 2 * spot(place_ref, pair, chips) + half
             row = scale[2 * index + half : 2 * index + half + 1]
             scale_ref[pl.ds(block, 1), :] = row
-            terms_ref = (last_ref, sides_ref, sides_ref, middle_ref)[index]
-            start = ((pair == 3) * 2 + half) * share
-            terms = terms_ref[pl.ds(start, share), :] if index else jnp.sum(
-                terms_ref[:, start : start + share, :].astype(F32), axis=0
-            )
+            if pair == 0:
+                pieces = [
+                    total[(half * groups + group) * share : (half * groups + group + 1) * share]
+                    for group in range(groups)
+                ]
+                terms = jnp.concatenate(pieces, 1)
+            else:
+                terms_ref = middle_ref if pair == 2 else sides_ref
+                start = ((pair == 3) * 2 + half) * share
+                terms = terms_ref[pl.ds(start, share), :]
             levels_ref[block] = terms / row
 
 
 def finish(place, last, sides, middle, share, chips):
-    width = last.shape[2]
+    width = middle.shape[1]
     vmem = pl.BlockSpec(memory_space=pltpu.VMEM)
     return pl.pallas_call(
         functools.partial(finish_kernel, chips=chips),
@@ -385,7 +429,7 @@
             jax.ShapeDtypeStruct((8, width), F32),
         ],
         compiler_params=pltpu.CompilerParams(vmem_limit_bytes=12 * MIB),
-        cost_estimate=cost(0.0001),
+        cost_estimate=cost(0.1),
         name="finish",
     )(place, last, sides, middle)
 
@@ -437,46 +481,49 @@
     from_down[3] = send_up(from_down[2])
     (from_up[2],) = gate([from_up[2]], [token])
     from_up[3] = send_down(from_up[2])
-    atts = (att, peer(att))
     share = carried.shape[1] // dp_count
 
     def swapped(pair, near, far, after=()):
         return peer(pick_other(place, near, far, pair, z_count, after))
 
-    def weigh(pairs, near, far, recv, known=(), after=()):
+    def weigh(pairs, near, far, recv, atts, known=(), keep_att=False):
         return weight_block(
-            place, near, far, recv, atts, carried, known, pairs, z_count, dp_count, after
+            place, near, far, recv, atts, carried, known, pairs, z_count, dp_count, keep_att
         )
 
     def exchange(array):
         return lax.all_to_all(array, "dp", 0, 0, tiled=True)
 
     recv2 = swapped(2, from_down[2], [from_up[2]])
-    terms, peaks2 = weigh((2,), [from_down[2]], [[from_up[2]]], [recv2])
-    middle = jnp.sum(exchange(terms).astype(F32), axis=0)
-    (from_down[3],) = gate([from_down[3]], [peaks2])
-    farthest = [send_up(half_of(from_down[3], 0))]
-    (from_up[3],) = gate([from_up[3]], [peaks2])
-    farthest.append(send_down(half_of(from_up[3], 1)))
-    recv1 = swapped(1, from_down[1], [from_up[3]])
-    recv3 = swapped(3, from_down[3], [from_up[1]])
+    terms, peaks2, att_peer = weigh(
+        (2,), [from_down[2]], [[from_up[2]]], [recv2], (att, peer(att)), keep_att=True
+    )
+    atts = (att, stay(att_peer))
+    (middle,) = gate([exchange(terms)], [], 6.0)
+    from_down[3], from_up[3] = gate([from_down[3], from_up[3]], [peaks2])
+    top, bottom, send1, send3 = fork(
+        place, from_down[3], from_up[3], from_down[1], from_up[1], z_count
+    )
+    farthest = [send_up(top), send_down(bottom)]
     terms, peaks13 = weigh(
         (1, 3),
         [from_down[1], from_down[3]],
         [[from_up[3]], [from_up[1]]],
-        [recv1, recv3],
-    )
-    *farthest, terms = gate([*farthest, terms], [peaks13, middle])
-    sides = exchange(terms)
+        [peer(send1), peer(send3)],
+        atts,
+    )
+    farthest = gate(farthest, [peaks13, middle])
+    (terms,) = gate([terms], farthest, space=pltpu.HBM)
+    (sides,) = gate([exchange(terms)], [])
     recv0 = swapped(0, own, farthest)
-    terms, _ = weigh((0,), [own], [farthest], [recv0], (peaks13, peaks2))
+    terms, _ = weigh((0,), [own], [farthest], [recv0], atts, (peaks13, peaks2))
     last = exchange(terms)
     d_keys, d_values = add_pairs(dk_own, peer(dk_peer), dv_own, peer(dv_peer))
     level_sums, block_scale = finish(
         place,
         last,
         jnp.sum(sides.astype(F32), axis=0),
-        middle,
+        jnp.sum(middle.astype(F32), axis=0),
         share,
         z_count,
     )

time: 109 us -> 107 us (0.982)
  other arithmetic: 3.23 us -> 0.95 us
  local copies, waits for them, and re-layouts: 3.7 us -> 2.08 us
  starting transfers between devices: 36.5 us -> 37.6 us
    all_to_all x3, waiting for transfers between devices: 14.2 us -> 17.7 us  [exchange(): return lax.all_to_all(array, 'dp', 0, 0, tiled=True)]
    ppermute x9, waiting for transfers between devices: 4.27 us -> 1.32 us  [peer(): return lax.ppermute(array, 'seq', swap)]
    pallas_call x4 -> x2, Pallas kernels: 5.07 us -> 2.31 us  [pick_other(): pl.pallas_call(functools.partial(pick_kernel, pair=pair, chips=chips, cou...]
    pallas_call x1, Pallas kernels: 1.57 us -> 3.45 us  [add_pairs(): pl.pallas_call(add_kernel, grid=(4,), in_specs=[spec] * 4, out_specs=[spe...]
    unnamed x20 -> x6, local copies, waits for them, and re-layouts: 3.7 us -> 2.08 us
    ppermute x4, starting transfers between devices: 2.41 us -> 3.8 us  [send_up(): return lax.ppermute(array, 'tensor', up)]
    ppermute x4, starting transfers between devices: 13.2 us -> 11.8 us  [send_down(): return lax.ppermute(array, 'tensor', down)]
    reduce_sum x1, other arithmetic: 1.38 us -> 0.15 us  [body(): jnp.sum(sides.astype(F32), axis=0)]
  transfers between devices with their start and end apart: 20 -> 20, of which waited for: 9 -> 7; matrix products, arithmetic and copies ran while one was open for 3% -> 1% of each run, Pallas kernels for 36% -> 36%
where the time goes in v3:
time: 107 us; the launch traced here: 106 us
  Pallas kernels  39.8 us (37%)
  starting transfers between devices  37.6 us (35%)
  waiting for transfers between devices  25 us (23%)
  local copies, waits for them, and re-layouts  2.08 us (2%)
    all_to_all x3, starting transfers between devices, exchange(): return lax.all_to_all(array, 'dp', 0, 0, tiled=True)  19.6 us
    pallas_call x2, Pallas kernels, attention(): pl.pallas_call(functools.partial(attention_kernel, tile=256, first=first,...  18.4 us
    all_to_all x3, waiting for transfers between devices, exchange(): return lax.all_to_all(array, 'dp', 0, 0, tiled=True)  17.7 us
    pallas_call x3, Pallas kernels, weight_block(): pl.pallas_call(functools.partial(weight_kernel, pairs=pairs, pieces=piece...  12.5 us
    ppermute x4, starting transfers between devices, send_down(): return lax.ppermute(array, 'tensor', down)  11.8 us
    ppermute x4, waiting for transfers between devices, send_up(): return lax.ppermute(array, 'tensor', up)  6.04 us
    ppermute x4, starting transfers between devices, send_up(): return lax.ppermute(array, 'tensor', up)  3.8 us
    pallas_call x1, Pallas kernels, add_pairs(): pl.pallas_call(add_kernel, grid=(4,), in_specs=[spec] * 4, out_specs=[spe...  3.45 us
  transfers between devices with their start and end apart: 20, of which 7 were waited for; matrix products, arithmetic and copies ran while one was open for 1% of the time, Pallas kernels for 36%

profile of v3, /device:TPU:2, one launch (start us, length us, event | category | flops | bytes accessed | tf_op | source)
XLA Modules:
  0.0 106.3 jit_solution(7965975568672452570)
XLA Ops:
  1.2 1.9 %collective-permute-start.2 = (bf16[512,512]{1,0:T(8,128)(2,1)}, bf16[512,512]{1,0:T(8,128)(2,1)S(1)}, u32[]{:S(2)}, u32[]{:S(2)}) collective-permute-start(bf16[512,512]{1,0:T(8,128)(2,1)} %bitcast.12), channel_id=1, source_target_pairs={{0,1},{1,2},{2,3},{3,4},{4,5},{5,6},{6,7},{7,0},{8,9},{9,10},{10,1... | collective-permute-start | bytes 1572872 | tf_op jit(solution)/shard_map/ppermute | solution.py:454
  3.1 3.9 %collective-permute-start.3 = (bf16[512,512]{1,0:T(8,128)(2,1)}, bf16[512,512]{1,0:T(8,128)(2,1)S(1)}, u32[]{:S(2)}, u32[]{:S(2)}) collective-permute-start(bf16[512,512]{1,0:T(8,128)(2,1)} %bitcast.13), channel_id=1, source_target_pairs={{0,7},{1,0},{2,1},{3,2},{4,3},{5,4},{6,5},{7,6},{8,15},{9,8},{10,9... | collective-permute-start | bytes 1572872 | tf_op jit(solution)/shard_map/ppermute | solution.py:457
  7.1 0.7 pad_add_fusion.place_ref
  7.8 9.2 %attention.2 = (bf16[512,512]{1,0:T(8,128)(2,1)S(1)}, bf16[512,512]{1,0:T(8,128)(2,1)}, bf16[512,512]{1,0:T(8,128)(2,1)}, bf16[512,512]{1,0:T(8,128)(2,1)}, bf16...) custom-call(s32[6]{0:T(128)S(1)} %pad_add_fusion.place_ref, ...), custom_call_target="tpu_custom_call" | custom-call | flops 230000000 | tf_op jit(solution)/shard_map/attention/pallas_call | solution.py:117
  17.0 2.5 %collective-permute-done.2.refs_0_ = bf16[512,512]{1,0:T(8,128)(2,1)S(1)} collective-permute-done((bf16[512,512]{1,0:T(8,128)(2,1)}, bf16[512,512]{1,0:T(8,128)(2,1)S(1)}, u32[]{:S(2)}, u32[]{:S(2)}) %collective-permute-start.2) | collective-permute-done | bytes 524320 | tf_op jit(solution)/shard_map/ppermute | solution.py:454
  19.5 3.2 %collective-permute-start.8 = (bf16[512,512]{1,0:T(8,128)(2,1)S(1)}, bf16[512,512]{1,0:T(8,128)(2,1)}, u32[]{:S(2)}, u32[]{:S(2)}) collective-permute-start(bf16[512,512]{1,0:T(8,128)(2,1)S(1)} %gate.10.refs_7_.old_up_ref.refs_5_), channel_id=1, source_target_pairs={{0,7},{1,0},{2,1},{3,2},{4,3},{5,4},{6,5},{7,6},{8,15},{9,8},{10,9... | collective-permute-start | bytes 1572872 | tf_op jit(solution)/shard_map/ppermute | solution.py:457
  22.7 9.2 %attention.3 = (bf16[512,512]{1,0:T(8,128)(2,1)S(1)}, bf16[512,512]{1,0:T(8,128)(2,1)}, bf16[512,512]{1,0:T(8,128)(2,1)}, bf16[512,512]{1,0:T(8,128)(2,1)}, bf16...) custom-call(s32[6]{0:T(128)S(1)} %pad_add_fusion.place_ref, ...), custom_call_target="tpu_custom_call", output_to_operand_aliasing={{0}: (7, {}), {1}: (8, {}), {2}: (9, {}), {3}: (10, {}), {4... | custom-call | flops 230000000 | tf_op jit(solution)/shard_map/attention/pallas_call | solution.py:117
  31.9 2.3 %collective-permute-done.6.refs_0_ = bf16[512,512]{1,0:T(8,128)(2,1)} collective-permute-done((bf16[512,512]{1,0:T(8,128)(2,1)S(1)}, bf16[512,512]{1,0:T(8,128)(2,1)}, u32[]{:S(2)}, u32[]{:S(2)}) %collective-permute-start.6) | collective-permute-done | bytes 524320 | tf_op jit(solution)/shard_map/ppermute | solution.py:454
  34.2 1.3 %pick_other.2 = bf16[512,512]{1,0:T(8,128)(2,1)S(1)} custom-call(s32[6]{0:T(128)S(1)} %pad_add_fusion.place_ref, bf16[512,512]{1,0:T(8,128)(2,1)} %get-tuple-element.55.near_ref.refs_0_, bf16[512,512]{1,0:T(8,128)(2,1)} %gate.12.refs_0_.refs_2_), custom_call_target="tpu_custom_call" | custom-call | flops 11500000 | tf_op jit(solution)/shard_map/pick_other/pallas_call | solution.py:186
  35.5 0.6 collective-permute-start.10
  36.1 3.2 %collective-permute-start.9 = (bf16[512,512]{1,0:T(8,128)(2,1)}, bf16[512,512]{1,0:T(8,128)(2,1)S(1)}, u32[]{:S(2)}, u32[]{:S(2)}) collective-permute-start(bf16[512,512]{1,0:T(8,128)(2,1)} %gate.12.refs_0_.refs_2_), channel_id=1, source_target_pairs={{0,7},{1,0},{2,1},{3,2},{4,3},{5,4},{6,5},{7,6},{8,15},{9,8},{10,9... | collective-permute-start | bytes 1572872 | tf_op jit(solution)/shard_map/ppermute | solution.py:457
  39.3 3.5 %weight_block.3 = (bf16[16,32,512]{2,1,0:T(8,128)(2,1)}, f32[2,512]{1,0:T(2,128)S(1)}, bf16[512,512]{1,0:T(8,128)(2,1)}) custom-call(s32[6]{0:T(128)S(1)} %pad_add_fusion.place_ref, bf16[512,512]{1,0:T(8,128)(2,1)} %get-tuple-element.55.near_ref.refs_0_, bf16[512,512]{1,0:T(8,128)(2,1)S(1)} %collective-permute-done.10.refs_1_, ...), custom_call_target="tpu_custom_call" | custom-call | flops 115000000 | tf_op jit(solution)/shard_map/weight_block/pallas_call | solution.py:342
  42.8 7.5 %all-to-all-start = ((bf16[16,32,512]{2,1,0:T(8,128)(2,1)}), bf16[16,32,512]{2,1,0:T(8,128)(2,1)S(1)}, u32[]{:S(2)}, u32[]{:S(2)}) async-start(bf16[16,32,512]{2,1,0:T(8,128)(2,1)} %get-tuple-element.66), calls=%async_computation | async-start | bytes 1048576 | tf_op jit(solution)/shard_map/all_to_all | solution.py:495
  50.3 1.3 %collective-permute-done.7.refs_0_ = bf16[512,512]{1,0:T(8,128)(2,1)S(1)} collective-permute-done((bf16[512,512]{1,0:T(8,128)(2,1)}, bf16[512,512]{1,0:T(8,128)(2,1)S(1)}, u32[]{:S(2)}, u32[]{:S(2)}) %collective-permute-start.7) | collective-permute-done | bytes 524320 | tf_op jit(solution)/shard_map/ppermute | solution.py:454
  51.6 1.9 %fork.1 = (bf16[256,512]{1,0:T(8,128)(2,1)}, bf16[256,512]{1,0:T(8,128)(2,1)}, bf16[512,512]{1,0:T(8,128)(2,1)}, bf16[512,512]{1,0:T(8,128)(2,1)}) custom-call(s32[6]{0:T(128)S(1)} %pad_add_fusion.place_ref, bf16[512,512]{1,0:T(8,128)(2,1)S(1)} %get-tuple-element.58.down_ref.refs_1_, bf16[512,512]{1,0:T(8,128)(2,1)S(1)} %get-tuple-element.59.up_ref.refs_4_, ...), custom_call_target="tpu_custom_call" | custom-call | flops 11500000 | tf_op jit(solution)/shard_map/fork/pallas_call | solution.py:215
  53.5 1.9 %collective-permute-start.12 = (bf16[256,512]{1,0:T(8,128)(2,1)}, bf16[256,512]{1,0:T(8,128)(2,1)S(1)}, u32[]{:S(2)}, u32[]{:S(2)}) collective-permute-start(bf16[256,512]{1,0:T(8,128)(2,1)} %get-tuple-element.60), channel_id=1, source_target_pairs={{0,1},{1,2},{2,3},{3,4},{4,5},{5,6},{6,7},{7,0},{8,9},{9,10},{10,1... | collective-permute-start | bytes 786440 | tf_op jit(solution)/shard_map/ppermute | solution.py:454
  55.3 1.4 %collective-permute-start.13 = (bf16[256,512]{1,0:T(8,128)(2,1)}, bf16[256,512]{1,0:T(8,128)(2,1)}, u32[]{:S(2)}, u32[]{:S(2)}) collective-permute-start(bf16[256,512]{1,0:T(8,128)(2,1)} %get-tuple-element.61), channel_id=1, source_target_pairs={{0,7},{1,0},{2,1},{3,2},{4,3},{5,4},{6,5},{7,6},{8,15},{9,8},{10,9... | collective-permute-start | bytes 786440 | tf_op jit(solution)/shard_map/ppermute | solution.py:457
  56.7 0.5 collective-permute-start.15
  57.2 3.2 %all-to-all-done.refs_0_ = bf16[16,32,512]{2,1,0:T(8,128)(2,1)S(1)} async-done(((bf16[16,32,512]{2,1,0:T(8,128)(2,1)}), bf16[16,32,512]{2,1,0:T(8,128)(2,1)S(1)}, u32[]{:S(2)}, u32[]{:S(2)}) %all-to-all-start) | async-done | bytes 524320 | tf_op jit(solution)/shard_map/all_to_all | solution.py:495
  60.4 4.8 %weight_block.4 = (bf16[16,64,512]{2,1,0:T(8,128)(2,1)}, f32[4,512]{1,0:T(4,128)S(1)}) custom-call(s32[6]{0:T(128)S(1)} %pad_add_fusion.place_ref, bf16[512,512]{1,0:T(8,128)(2,1)S(1)} %gate.9.refs_6_.old_down_ref.refs_0_, bf16[512,512]{1,0:T(8,128)(2,1)S(1)} %get-tuple-element.58.down_ref.refs_1_, bf16[512,512]{1,0:T(8,128)(2,1)} %collective-permute-done.14.refs_2_, ...), custom_call_target="tpu_custom_call" | custom-call | flops 115000000 | tf_op jit(solution)/shard_map/weight_block/pallas_call | solution.py:342
  65.3 6.9 %all-to-all-start.2 = ((bf16[16,64,512]{2,1,0:T(8,128)(2,1)}), bf16[16,64,512]{2,1,0:T(8,128)(2,1)S(1)}, u32[]{:S(2)}, u32[]{:S(2)}) async-start(bf16[16,64,512]{2,1,0:T(8,128)(2,1)} %gate.16), calls=%async_computation.2 | async-start | bytes 2097152 | tf_op jit(solution)/shard_map/all_to_all | solution.py:495
  72.2 1.0 pick_other.3
  73.4 0.5 collective-permute-start.4
  74.0 1.3 %collective-permute-done.16.refs_1_ = bf16[512,512]{1,0:T(8,128)(2,1)S(1)} collective-permute-done((bf16[512,512]{1,0:T(8,128)(2,1)S(1)}, bf16[512,512]{1,0:T(8,128)(2,1)S(1)}, u32[]{:S(2)}, u32[]{:S(2)}) %collective-permute-start.16) | collective-permute-done | bytes 524320 | tf_op jit(solution)/shard_map/ppermute | solution.py:447
  75.3 4.1 %weight_block.5 = (bf16[16,160,128]{2,1,0:T(8,128)(2,1)}, f32[2,512]{1,0:T(2,128)}) custom-call(s32[6]{0:T(128)S(1)} %pad_add_fusion.place_ref, bf16[512,512]{1,0:T(8,128)(2,1)S(1)} %bitcast.15, bf16[512,512]{1,0:T(8,128)(2,1)S(1)} %collective-permute-done.16.refs_1_, bf16[256,512]{1,0:T(8,128)(2,1)S(1)} %get-tuple-element.67.refs_0_.refs_2_.refs_1_, ...), custom_call_target="tpu_custom_call" | custom-call | flops 115000000 | tf_op jit(solution)/shard_map/weight_block/pallas_call | solution.py:342
  79.4 8.9 %all-to-all-done.2.refs_0_ = bf16[16,64,512]{2,1,0:T(8,128)(2,1)S(1)} async-done(((bf16[16,64,512]{2,1,0:T(8,128)(2,1)}), bf16[16,64,512]{2,1,0:T(8,128)(2,1)S(1)}, u32[]{:S(2)}, u32[]{:S(2)}) %all-to-all-start.2) | async-done | bytes 1048608 | tf_op jit(solution)/shard_map/all_to_all | solution.py:495
  88.3 5.2 %all-to-all-start.1 = ((bf16[16,160,128]{2,1,0:T(8,128)(2,1)}), bf16[16,160,128]{2,1,0:T(8,128)(2,1)S(1)}, u32[]{:S(2)}, u32[]{:S(2)}) async-start(bf16[16,160,128]{2,1,0:T(8,128)(2,1)} %get-tuple-element.69), calls=%async_computation.1 | async-start | bytes 1310720 | tf_op jit(solution)/shard_map/all_to_all | solution.py:495
  93.5 1.0 copy-done.1
  94.6 1.0 copy-done.2
  95.6 3.5 %add_pairs.1 = (bf16[512,512]{1,0:T(8,128)(2,1)}, bf16[512,512]{1,0:T(8,128)(2,1)}) custom-call(bf16[512,512]{1,0:T(8,128)(2,1)S(1)} %copy-done.1, bf16[512,512]{1,0:T(8,128)(2,1)} %collective-permute-done.4.b_ref, bf16[512,512]{1,0:T(8,128)(2,1)S(1)} %copy-done.2, bf16[512,512]{1,0:T(8,128)(2,1)} %collective-permute-done.5.d_ref), custom_call_target="tpu_custom_call" | custom-call | flops 115000000 | tf_op jit(solution)/shard_map/add_pairs/pallas_call | solution.py:382
  99.3 5.6 %all-to-all-done.1.last_ref = bf16[16,160,128]{2,1,0:T(8,128)(2,1)S(1)} async-done(((bf16[16,160,128]{2,1,0:T(8,128)(2,1)}), bf16[16,160,128]{2,1,0:T(8,128)(2,1)S(1)}, u32[]{:S(2)}, u32[]{:S(2)}) %all-to-all-start.1) | async-done | bytes 655392 | tf_op jit(solution)/shard_map/all_to_all | solution.py:495
  104.9 1.4 %finish.1 = (f32[8,16,512]{2,1,0:T(8,128)}, f32[8,512]{1,0:T(8,128)}) custom-call(s32[6]{0:T(128)S(1)} %pad_add_fusion.place_ref, bf16[16,160,128]{2,1,0:T(8,128)(2,1)S(1)} %all-to-all-done.1.last_ref, f32[64,512]{1,0:T(8,128)S(1)} %convert_reduce_fusion.sides_ref, f32[32,512]{1,0:T(8,128)S(1)} %convert_reduce_fusion.1.middle_ref), custom_call_target="tpu_custom_call" | custom-call | flops 115000000 | tf_op jit(solution)/shard_map/finish/pallas_call | solution.py:423
  (36 shorter events, 1.1 us)
Async XLA Ops:
  0.6 7.2 %collective-permute-start = (bf16[512,512]{1,0:T(8,128)(2,1)}, bf16[512,512]{1,0:T(8,128)(2,1)S(1)}, u32[]{:S(2)}, u32[]{:S(2)}) collective-permute-start(bf16[512,512]{1,0:T(8,128)(2,1)} %bitcast.19), channel_id=1, source_target_pairs={{0,8},{8,0},{1,9},{9,1},{2,10},{10,2},{3,11},{11,3},{4,12},{12,4},... | collective-permute-start | bytes 1572872 | tf_op jit(solution)/shard_map/ppermute | solution.py:447
  0.7 7.1 %collective-permute-start.1 = (bf16[512,512]{1,0:T(8,128)(2,1)}, bf16[512,512]{1,0:T(8,128)(2,1)S(1)}, u32[]{:S(2)}, u32[]{:S(2)}) collective-permute-start(bf16[512,512]{1,0:T(8,128)(2,1)} %bitcast.22), channel_id=1, source_target_pairs={{0,8},{8,0},{1,9},{9,1},{2,10},{10,2},{3,11},{11,3},{4,12},{12,4},... | collective-permute-start | bytes 1572872 | tf_op jit(solution)/shard_map/ppermute | solution.py:447
  1.2 18.3 %collective-permute-start.2 = (bf16[512,512]{1,0:T(8,128)(2,1)}, bf16[512,512]{1,0:T(8,128)(2,1)S(1)}, u32[]{:S(2)}, u32[]{:S(2)}) collective-permute-start(bf16[512,512]{1,0:T(8,128)(2,1)} %bitcast.12), channel_id=1, source_target_pairs={{0,1},{1,2},{2,3},{3,4},{4,5},{5,6},{6,7},{7,0},{8,9},{9,10},{10,1... | collective-permute-start | bytes 1572872 | tf_op jit(solution)/shard_map/ppermute | solution.py:454
  3.1 16.3 %collective-permute-start.3 = (bf16[512,512]{1,0:T(8,128)(2,1)}, bf16[512,512]{1,0:T(8,128)(2,1)S(1)}, u32[]{:S(2)}, u32[]{:S(2)}) collective-permute-start(bf16[512,512]{1,0:T(8,128)(2,1)} %bitcast.13), channel_id=1, source_target_pairs={{0,7},{1,0},{2,1},{3,2},{4,3},{5,4},{6,5},{7,6},{8,15},{9,8},{10,9... | collective-permute-start | bytes 1572872 | tf_op jit(solution)/shard_map/ppermute | solution.py:457
  19.5 14.7 %collective-permute-start.6 = (bf16[512,512]{1,0:T(8,128)(2,1)S(1)}, bf16[512,512]{1,0:T(8,128)(2,1)}, u32[]{:S(2)}, u32[]{:S(2)}) collective-permute-start(bf16[512,512]{1,0:T(8,128)(2,1)S(1)} %gate.9.refs_6_.old_down_ref.refs_0_), channel_id=1, source_target_pairs={{0,1},{1,2},{2,3},{3,4},{4,5},{5,6},{6,7},{7,0},{8,9},{9,10},{10,1... | collective-permute-start | bytes 1572872 | tf_op jit(solution)/shard_map/ppermute | solution.py:454
  19.5 14.7 %collective-permute-start.8 = (bf16[512,512]{1,0:T(8,128)(2,1)S(1)}, bf16[512,512]{1,0:T(8,128)(2,1)}, u32[]{:S(2)}, u32[]{:S(2)}) collective-permute-start(bf16[512,512]{1,0:T(8,128)(2,1)S(1)} %gate.10.refs_7_.old_up_ref.refs_5_), channel_id=1, source_target_pairs={{0,7},{1,0},{2,1},{3,2},{4,3},{5,4},{6,5},{7,6},{8,15},{9,8},{10,9... | collective-permute-start | bytes 1572872 | tf_op jit(solution)/shard_map/ppermute | solution.py:457
  34.2 5.1 %collective-permute-start.11 = (bf16[512,512]{1,0:T(8,128)(2,1)S(1)}, bf16[512,512]{1,0:T(8,128)(2,1)S(1)}, u32[]{:S(2)}, u32[]{:S(2)}) collective-permute-start(bf16[512,512]{1,0:T(8,128)(2,1)S(1)} %get-tuple-element.56.refs_3_.refs_6_.refs_4_), channel_id=1, source_target_pairs={{0,8},{8,0},{1,9},{9,1},{2,10},{10,2},{3,11},{11,3},{4,12},{12,4},... | collective-permute-start | bytes 1572872 | tf_op jit(solution)/shard_map/ppermute | solution.py:447
  35.5 3.8 %collective-permute-start.10 = (bf16[512,512]{1,0:T(8,128)(2,1)S(1)}, bf16[512,512]{1,0:T(8,128)(2,1)S(1)}, u32[]{:S(2)}, u32[]{:S(2)}) collective-permute-start(bf16[512,512]{1,0:T(8,128)(2,1)S(1)} %pick_other.2), channel_id=1, source_target_pairs={{0,8},{8,0},{1,9},{9,1},{2,10},{10,2},{3,11},{11,3},{4,12},{12,4},... | collective-permute-start | bytes 1572872 | tf_op jit(solution)/shard_map/ppermute | solution.py:447
  36.1 15.5 %collective-permute-start.7 = (bf16[512,512]{1,0:T(8,128)(2,1)}, bf16[512,512]{1,0:T(8,128)(2,1)S(1)}, u32[]{:S(2)}, u32[]{:S(2)}) collective-permute-start(bf16[512,512]{1,0:T(8,128)(2,1)} %get-tuple-element.55.near_ref.refs_0_), channel_id=1, source_target_pairs={{0,1},{1,2},{2,3},{3,4},{4,5},{5,6},{6,7},{7,0},{8,9},{9,10},{10,1... | collective-permute-start | bytes 1572872 | tf_op jit(solution)/shard_map/ppermute | solution.py:454
  36.1 15.5 %collective-permute-start.9 = (bf16[512,512]{1,0:T(8,128)(2,1)}, bf16[512,512]{1,0:T(8,128)(2,1)S(1)}, u32[]{:S(2)}, u32[]{:S(2)}) collective-permute-start(bf16[512,512]{1,0:T(8,128)(2,1)} %gate.12.refs_0_.refs_2_), channel_id=1, source_target_pairs={{0,7},{1,0},{2,1},{3,2},{4,3},{5,4},{6,5},{7,6},{8,15},{9,8},{10,9... | collective-permute-start | bytes 1572872 | tf_op jit(solution)/shard_map/ppermute | solution.py:457
  42.8 17.5 %all-to-all-start = ((bf16[16,32,512]{2,1,0:T(8,128)(2,1)}), bf16[16,32,512]{2,1,0:T(8,128)(2,1)S(1)}, u32[]{:S(2)}, u32[]{:S(2)}) async-start(bf16[16,32,512]{2,1,0:T(8,128)(2,1)} %get-tuple-element.66), calls=%async_computation | async-start | bytes 1048576 | tf_op jit(solution)/shard_map/all_to_all | solution.py:495
  53.5 11.8 %collective-permute-start.12 = (bf16[256,512]{1,0:T(8,128)(2,1)}, bf16[256,512]{1,0:T(8,128)(2,1)S(1)}, u32[]{:S(2)}, u32[]{:S(2)}) collective-permute-start(bf16[256,512]{1,0:T(8,128)(2,1)} %get-tuple-element.60), channel_id=1, source_target_pairs={{0,1},{1,2},{2,3},{3,4},{4,5},{5,6},{6,7},{7,0},{8,9},{9,10},{10,1... | collective-permute-start | bytes 786440 | tf_op jit(solution)/shard_map/ppermute | solution.py:454
  55.3 9.9 %collective-permute-start.13 = (bf16[256,512]{1,0:T(8,128)(2,1)}, bf16[256,512]{1,0:T(8,128)(2,1)}, u32[]{:S(2)}, u32[]{:S(2)}) collective-permute-start(bf16[256,512]{1,0:T(8,128)(2,1)} %get-tuple-element.61), channel_id=1, source_target_pairs={{0,7},{1,0},{2,1},{3,2},{4,3},{5,4},{6,5},{7,6},{8,15},{9,8},{10,9... | collective-permute-start | bytes 786440 | tf_op jit(solution)/shard_map/ppermute | solution.py:457
  56.7 3.7 %collective-permute-start.14 = (bf16[512,512]{1,0:T(8,128)(2,1)}, bf16[512,512]{1,0:T(8,128)(2,1)}, u32[]{:S(2)}, u32[]{:S(2)}) collective-permute-start(bf16[512,512]{1,0:T(8,128)(2,1)} %get-tuple-element.62), channel_id=1, source_target_pairs={{0,8},{8,0},{1,9},{9,1},{2,10},{10,2},{3,11},{11,3},{4,12},{12,4},... | collective-permute-start | bytes 1572872 | tf_op jit(solution)/shard_map/ppermute | solution.py:447
  56.7 3.7 %collective-permute-start.15 = (bf16[512,512]{1,0:T(8,128)(2,1)}, bf16[512,512]{1,0:T(8,128)(2,1)}, u32[]{:S(2)}, u32[]{:S(2)}) collective-permute-start(bf16[512,512]{1,0:T(8,128)(2,1)} %get-tuple-element.63), channel_id=1, source_target_pairs={{0,8},{8,0},{1,9},{9,1},{2,10},{10,2},{3,11},{11,3},{4,12},{12,4},... | collective-permute-start | bytes 1572872 | tf_op jit(solution)/shard_map/ppermute | solution.py:447
  65.2 7.0 %copy-start = (bf16[1,512,512]{2,1,0:T(8,128)(2,1)S(1)}, bf16[1,512,512]{2,1,0:T(8,128)(2,1)}, u32[]{:S(2)}) copy-start(bf16[1,512,512]{2,1,0:T(8,128)(2,1)} %param.11) | copy-start | bytes 1572868
  65.3 23.0 %all-to-all-start.2 = ((bf16[16,64,512]{2,1,0:T(8,128)(2,1)}), bf16[16,64,512]{2,1,0:T(8,128)(2,1)S(1)}, u32[]{:S(2)}, u32[]{:S(2)}) async-start(bf16[16,64,512]{2,1,0:T(8,128)(2,1)} %gate.16), calls=%async_computation.2 | async-start | bytes 2097152 | tf_op jit(solution)/shard_map/all_to_all | solution.py:495
  73.3 2.0 %collective-permute-start.16 = (bf16[512,512]{1,0:T(8,128)(2,1)S(1)}, bf16[512,512]{1,0:T(8,128)(2,1)S(1)}, u32[]{:S(2)}, u32[]{:S(2)}) collective-permute-start(bf16[512,512]{1,0:T(8,128)(2,1)S(1)} %pick_other.3), channel_id=1, source_target_pairs={{0,8},{8,0},{1,9},{9,1},{2,10},{10,2},{3,11},{11,3},{4,12},{12,4},... | collective-permute-start | bytes 1572872 | tf_op jit(solution)/shard_map/ppermute | solution.py:447
  73.4 20.1 %collective-permute-start.4 = (bf16[512,512]{1,0:T(8,128)(2,1)}, bf16[512,512]{1,0:T(8,128)(2,1)}, u32[]{:S(2)}, u32[]{:S(2)}) collective-permute-start(bf16[512,512]{1,0:T(8,128)(2,1)} %get-tuple-element.48), channel_id=1, source_target_pairs={{0,8},{8,0},{1,9},{9,1},{2,10},{10,2},{3,11},{11,3},{4,12},{12,4},... | collective-permute-start | bytes 1572872 | tf_op jit(solution)/shard_map/ppermute | solution.py:447
  73.9 19.6 %collective-permute-start.5 = (bf16[512,512]{1,0:T(8,128)(2,1)}, bf16[512,512]{1,0:T(8,128)(2,1)}, u32[]{:S(2)}, u32[]{:S(2)}) collective-permute-start(bf16[512,512]{1,0:T(8,128)(2,1)} %get-tuple-element.50), channel_id=1, source_target_pairs={{0,8},{8,0},{1,9},{9,1},{2,10},{10,2},{3,11},{11,3},{4,12},{12,4},... | collective-permute-start | bytes 1572872 | tf_op jit(solution)/shard_map/ppermute | solution.py:447
  88.3 16.6 %all-to-all-start.1 = ((bf16[16,160,128]{2,1,0:T(8,128)(2,1)}), bf16[16,160,128]{2,1,0:T(8,128)(2,1)S(1)}, u32[]{:S(2)}, u32[]{:S(2)}) async-start(bf16[16,160,128]{2,1,0:T(8,128)(2,1)} %get-tuple-element.69), calls=%async_computation.1 | async-start | bytes 1310720 | tf_op jit(solution)/shard_map/all_to_all | solution.py:495
  93.5 1.0 copy-start.1
  94.6 1.0 copy-start.2

commit v4 on v3

--- a/solution.py
+++ b/solution.py
@@ -197,7 +197,7 @@
 
 
 def fork_kernel(place_ref, down_ref, up_ref, old_down_ref, old_up_ref, *out_refs, chips):
-    top_ref, bottom_ref, first_ref, third_ref = out_refs
+    first_ref, third_ref, top_ref, bottom_ref = out_refs
     half = top_ref.shape[0]
     top_ref[...] = down_ref[:half, :]
     bottom_ref[...] = up_ref[half:, :]
@@ -216,8 +216,8 @@
         functools.partial(fork_kernel, chips=chips),
         in_specs=[pl.BlockSpec(memory_space=pltpu.SMEM)] + [vmem] * 4,
         out_specs=[vmem] * 4,
-        out_shape=[jax.ShapeDtypeStruct((rows // 2, width), down.dtype)] * 2
-        + [jax.ShapeDtypeStruct((rows, width), down.dtype)] * 2,
+        out_shape=[jax.ShapeDtypeStruct((rows, width), down.dtype)] * 2
+        + [jax.ShapeDtypeStruct((rows // 2, width), down.dtype)] * 2,
         compiler_params=pltpu.CompilerParams(vmem_limit_bytes=6 * MIB),
         cost_estimate=cost(0.01),
         name="fork",
@@ -499,17 +499,18 @@
         (2,), [from_down[2]], [[from_up[2]]], [recv2], (att, peer(att)), keep_att=True
     )
     atts = (att, stay(att_peer))
-    (middle,) = gate([exchange(terms)], [], 6.0)
+    (middle,) = gate([exchange(terms)], [], 1.0)
     from_down[3], from_up[3] = gate([from_down[3], from_up[3]], [peaks2])
-    top, bottom, send1, send3 = fork(
+    send1, send3, top, bottom = fork(
         place, from_down[3], from_up[3], from_down[1], from_up[1], z_count
     )
+    recv13 = [peer(send1), peer(send3)]
     farthest = [send_up(top), send_down(bottom)]
     terms, peaks13 = weigh(
         (1, 3),
         [from_down[1], from_down[3]],
         [[from_up[3]], [from_up[1]]],
-        [peer(send1), peer(send3)],
+        recv13,
         atts,
     )
     farthest = gate(farthest, [peaks13, middle])

time: 107 us -> 105 us (0.981)
  waiting for transfers between devices: 25 us -> 23.5 us
  starting transfers between devices: 37.6 us -> 36.5 us
    all_to_all x3, waiting for transfers between devices: 17.7 us -> 16.1 us  [exchange(): return lax.all_to_all(array, 'dp', 0, 0, tiled=True)]
  transfers between devices with their start and end apart: 20 -> 20, of which waited for: 7 -> 7; matrix products, arithmetic and copies ran while one was open for 1% -> 1% of each run, Pallas kernels for 36% -> 37%
where the time goes in v4:
time: 105 us; the launch traced here: 104 us
  Pallas kernels  39.8 us (38%)
  starting transfers between devices  36.5 us (35%)
  waiting for transfers between devices  23.5 us (22%)
  local copies, waits for them, and re-layouts  2.08 us (2%)
    all_to_all x3, starting transfers between devices, exchange(): return lax.all_to_all(array, 'dp', 0, 0, tiled=True)  18.6 us
    pallas_call x2, Pallas kernels, attention(): pl.pallas_call(functools.partial(attention_kernel, tile=256, first=first,...  18.4 us
    all_to_all x3, waiting for transfers between devices, exchange(): return lax.all_to_all(array, 'dp', 0, 0, tiled=True)  16.1 us
    pallas_call x3, Pallas kernels, weight_block(): pl.pallas_call(functools.partial(weight_kernel, pairs=pairs, pieces=piece...  12.5 us
    ppermute x4, starting transfers between devices, send_down(): return lax.ppermute(array, 'tensor', down)  11.8 us
    ppermute x4, waiting for transfers between devices, send_up(): return lax.ppermute(array, 'tensor', up)  6.04 us
    ppermute x4, starting transfers between devices, send_up(): return lax.ppermute(array, 'tensor', up)  3.8 us
    pallas_call x1, Pallas kernels, add_pairs(): pl.pallas_call(add_kernel, grid=(4,), in_specs=[spec] * 4, out_specs=[spe...  3.45 us
  transfers between devices with their start and end apart: 20, of which 7 were waited for; matrix products, arithmetic and copies ran while one was open for 1% of the time, Pallas kernels for 37%

profile of v4, /device:TPU:2, one launch (start us, length us, event | category | flops | bytes accessed | tf_op | source)
XLA Modules:
  0.0 103.7 jit_solution(2370292795177672701)
XLA Ops:
  1.2 1.9 %collective-permute-start.2 = (bf16[512,512]{1,0:T(8,128)(2,1)}, bf16[512,512]{1,0:T(8,128)(2,1)S(1)}, u32[]{:S(2)}, u32[]{:S(2)}) collective-permute-start(bf16[512,512]{1,0:T(8,128)(2,1)} %bitcast.12), channel_id=1, source_target_pairs={{0,1},{1,2},{2,3},{3,4},{4,5},{5,6},{6,7},{7,0},{8,9},{9,10},{10,1... | collective-permute-start | bytes 1572872 | tf_op jit(solution)/shard_map/ppermute | solution.py:454
  3.1 3.9 %collective-permute-start.3 = (bf16[512,512]{1,0:T(8,128)(2,1)}, bf16[512,512]{1,0:T(8,128)(2,1)S(1)}, u32[]{:S(2)}, u32[]{:S(2)}) collective-permute-start(bf16[512,512]{1,0:T(8,128)(2,1)} %bitcast.13), channel_id=1, source_target_pairs={{0,7},{1,0},{2,1},{3,2},{4,3},{5,4},{6,5},{7,6},{8,15},{9,8},{10,9... | collective-permute-start | bytes 1572872 | tf_op jit(solution)/shard_map/ppermute | solution.py:457
  7.1 0.7 pad_add_fusion.place_ref
  7.8 9.2 %attention.2 = (bf16[512,512]{1,0:T(8,128)(2,1)S(1)}, bf16[512,512]{1,0:T(8,128)(2,1)}, bf16[512,512]{1,0:T(8,128)(2,1)}, bf16[512,512]{1,0:T(8,128)(2,1)}, bf16...) custom-call(s32[6]{0:T(128)S(1)} %pad_add_fusion.place_ref, ...), custom_call_target="tpu_custom_call" | custom-call | flops 230000000 | tf_op jit(solution)/shard_map/attention/pallas_call | solution.py:117
  17.0 2.5 %collective-permute-done.2.refs_0_ = bf16[512,512]{1,0:T(8,128)(2,1)S(1)} collective-permute-done((bf16[512,512]{1,0:T(8,128)(2,1)}, bf16[512,512]{1,0:T(8,128)(2,1)S(1)}, u32[]{:S(2)}, u32[]{:S(2)}) %collective-permute-start.2) | collective-permute-done | bytes 524320 | tf_op jit(solution)/shard_map/ppermute | solution.py:454
  19.5 3.2 %collective-permute-start.8 = (bf16[512,512]{1,0:T(8,128)(2,1)S(1)}, bf16[512,512]{1,0:T(8,128)(2,1)}, u32[]{:S(2)}, u32[]{:S(2)}) collective-permute-start(bf16[512,512]{1,0:T(8,128)(2,1)S(1)} %gate.10.refs_7_.old_up_ref.refs_5_), channel_id=1, source_target_pairs={{0,7},{1,0},{2,1},{3,2},{4,3},{5,4},{6,5},{7,6},{8,15},{9,8},{10,9... | collective-permute-start | bytes 1572872 | tf_op jit(solution)/shard_map/ppermute | solution.py:457
  22.7 9.2 %attention.3 = (bf16[512,512]{1,0:T(8,128)(2,1)S(1)}, bf16[512,512]{1,0:T(8,128)(2,1)}, bf16[512,512]{1,0:T(8,128)(2,1)}, bf16[512,512]{1,0:T(8,128)(2,1)}, bf16...) custom-call(s32[6]{0:T(128)S(1)} %pad_add_fusion.place_ref, ...), custom_call_target="tpu_custom_call", output_to_operand_aliasing={{0}: (7, {}), {1}: (8, {}), {2}: (9, {}), {3}: (10, {}), {4... | custom-call | flops 230000000 | tf_op jit(solution)/shard_map/attention/pallas_call | solution.py:117
  31.9 2.3 %collective-permute-done.6.refs_0_ = bf16[512,512]{1,0:T(8,128)(2,1)} collective-permute-done((bf16[512,512]{1,0:T(8,128)(2,1)S(1)}, bf16[512,512]{1,0:T(8,128)(2,1)}, u32[]{:S(2)}, u32[]{:S(2)}) %collective-permute-start.6) | collective-permute-done | bytes 524320 | tf_op jit(solution)/shard_map/ppermute | solution.py:454
  34.2 1.3 %pick_other.2 = bf16[512,512]{1,0:T(8,128)(2,1)S(1)} custom-call(s32[6]{0:T(128)S(1)} %pad_add_fusion.place_ref, bf16[512,512]{1,0:T(8,128)(2,1)} %get-tuple-element.55.near_ref.refs_0_, bf16[512,512]{1,0:T(8,128)(2,1)} %gate.12.refs_0_.refs_2_), custom_call_target="tpu_custom_call" | custom-call | flops 11500000 | tf_op jit(solution)/shard_map/pick_other/pallas_call | solution.py:186
  35.5 0.6 collective-permute-start.10
  36.1 3.2 %collective-permute-start.9 = (bf16[512,512]{1,0:T(8,128)(2,1)}, bf16[512,512]{1,0:T(8,128)(2,1)S(1)}, u32[]{:S(2)}, u32[]{:S(2)}) collective-permute-start(bf16[512,512]{1,0:T(8,128)(2,1)} %gate.12.refs_0_.refs_2_), channel_id=1, source_target_pairs={{0,7},{1,0},{2,1},{3,2},{4,3},{5,4},{6,5},{7,6},{8,15},{9,8},{10,9... | collective-permute-start | bytes 1572872 | tf_op jit(solution)/shard_map/ppermute | solution.py:457
  39.3 3.5 %weight_block.3 = (bf16[16,32,512]{2,1,0:T(8,128)(2,1)}, f32[2,512]{1,0:T(2,128)S(1)}, bf16[512,512]{1,0:T(8,128)(2,1)}) custom-call(s32[6]{0:T(128)S(1)} %pad_add_fusion.place_ref, bf16[512,512]{1,0:T(8,128)(2,1)} %get-tuple-element.55.near_ref.refs_0_, bf16[512,512]{1,0:T(8,128)(2,1)S(1)} %collective-permute-done.10.refs_1_, ...), custom_call_target="tpu_custom_call" | custom-call | flops 115000000 | tf_op jit(solution)/shard_map/weight_block/pallas_call | solution.py:342
  42.8 7.5 %all-to-all-start = ((bf16[16,32,512]{2,1,0:T(8,128)(2,1)}), bf16[16,32,512]{2,1,0:T(8,128)(2,1)S(1)}, u32[]{:S(2)}, u32[]{:S(2)}) async-start(bf16[16,32,512]{2,1,0:T(8,128)(2,1)} %get-tuple-element.66), calls=%async_computation | async-start | bytes 1048576 | tf_op jit(solution)/shard_map/all_to_all | solution.py:495
  50.3 1.3 %collective-permute-done.7.refs_0_ = bf16[512,512]{1,0:T(8,128)(2,1)S(1)} collective-permute-done((bf16[512,512]{1,0:T(8,128)(2,1)}, bf16[512,512]{1,0:T(8,128)(2,1)S(1)}, u32[]{:S(2)}, u32[]{:S(2)}) %collective-permute-start.7) | collective-permute-done | bytes 524320 | tf_op jit(solution)/shard_map/ppermute | solution.py:454
  51.6 1.9 %fork.1 = (bf16[512,512]{1,0:T(8,128)(2,1)}, bf16[512,512]{1,0:T(8,128)(2,1)}, bf16[256,512]{1,0:T(8,128)(2,1)}, bf16[256,512]{1,0:T(8,128)(2,1)}) custom-call(s32[6]{0:T(128)S(1)} %pad_add_fusion.place_ref, bf16[512,512]{1,0:T(8,128)(2,1)S(1)} %get-tuple-element.58.down_ref.refs_1_, bf16[512,512]{1,0:T(8,128)(2,1)S(1)} %get-tuple-element.59.up_ref.refs_4_, ...), custom_call_target="tpu_custom_call" | custom-call | flops 11500000 | tf_op jit(solution)/shard_map/fork/pallas_call | solution.py:215
  53.5 0.5 collective-permute-start.15
  54.0 1.9 %collective-permute-start.12 = (bf16[256,512]{1,0:T(8,128)(2,1)}, bf16[256,512]{1,0:T(8,128)(2,1)S(1)}, u32[]{:S(2)}, u32[]{:S(2)}) collective-permute-start(bf16[256,512]{1,0:T(8,128)(2,1)} %get-tuple-element.60), channel_id=1, source_target_pairs={{0,1},{1,2},{2,3},{3,4},{4,5},{5,6},{6,7},{7,0},{8,9},{9,10},{10,1... | collective-permute-start | bytes 786440 | tf_op jit(solution)/shard_map/ppermute | solution.py:454
  55.9 1.4 %collective-permute-start.13 = (bf16[256,512]{1,0:T(8,128)(2,1)}, bf16[256,512]{1,0:T(8,128)(2,1)}, u32[]{:S(2)}, u32[]{:S(2)}) collective-permute-start(bf16[256,512]{1,0:T(8,128)(2,1)} %get-tuple-element.61), channel_id=1, source_target_pairs={{0,7},{1,0},{2,1},{3,2},{4,3},{5,4},{6,5},{7,6},{8,15},{9,8},{10,9... | collective-permute-start | bytes 786440 | tf_op jit(solution)/shard_map/ppermute | solution.py:457
  57.2 3.2 %all-to-all-done.refs_0_ = bf16[16,32,512]{2,1,0:T(8,128)(2,1)S(1)} async-done(((bf16[16,32,512]{2,1,0:T(8,128)(2,1)}), bf16[16,32,512]{2,1,0:T(8,128)(2,1)S(1)}, u32[]{:S(2)}, u32[]{:S(2)}) %all-to-all-start) | async-done | bytes 524320 | tf_op jit(solution)/shard_map/all_to_all | solution.py:495
  60.4 4.8 %weight_block.4 = (bf16[16,64,512]{2,1,0:T(8,128)(2,1)}, f32[4,512]{1,0:T(4,128)S(1)}) custom-call(s32[6]{0:T(128)S(1)} %pad_add_fusion.place_ref, bf16[512,512]{1,0:T(8,128)(2,1)S(1)} %gate.9.refs_6_.old_down_ref.refs_0_, bf16[512,512]{1,0:T(8,128)(2,1)S(1)} %get-tuple-element.58.down_ref.refs_1_, bf16[512,512]{1,0:T(8,128)(2,1)} %collective-permute-done.14.refs_2_, ...), custom_call_target="tpu_custom_call" | custom-call | flops 115000000 | tf_op jit(solution)/shard_map/weight_block/pallas_call | solution.py:342
  65.3 6.3 %all-to-all-start.2 = ((bf16[16,64,512]{2,1,0:T(8,128)(2,1)}), bf16[16,64,512]{2,1,0:T(8,128)(2,1)S(1)}, u32[]{:S(2)}, u32[]{:S(2)}) async-start(bf16[16,64,512]{2,1,0:T(8,128)(2,1)} %gate.16), calls=%async_computation.2 | async-start | bytes 2097152 | tf_op jit(solution)/shard_map/all_to_all | solution.py:495
  71.6 1.0 %pick_other.3 = bf16[512,512]{1,0:T(8,128)(2,1)S(1)} custom-call(s32[6]{0:T(128)S(1)} %pad_add_fusion.place_ref, bf16[512,512]{1,0:T(8,128)(2,1)S(1)} %bitcast.14, bf16[256,512]{1,0:T(8,128)(2,1)S(1)} %get-tuple-element.67.refs_0_.refs_2_.refs_1_, bf16[256,512]{1,0:T(8,128)(2,1)} %get-tuple-element.68.refs_1_.refs_3_.refs_2_), custom_call_target="tpu_custom_call" | custom-call | flops 11500000 | tf_op jit(solution)/shard_map/pick_other/pallas_call | solution.py:186
  72.7 0.5 collective-permute-start.4
  73.3 1.3 %collective-permute-done.16.refs_1_ = bf16[512,512]{1,0:T(8,128)(2,1)S(1)} collective-permute-done((bf16[512,512]{1,0:T(8,128)(2,1)S(1)}, bf16[512,512]{1,0:T(8,128)(2,1)S(1)}, u32[]{:S(2)}, u32[]{:S(2)}) %collective-permute-start.16) | collective-permute-done | bytes 524320 | tf_op jit(solution)/shard_map/ppermute | solution.py:447
  74.6 4.1 %weight_block.5 = (bf16[16,160,128]{2,1,0:T(8,128)(2,1)}, f32[2,512]{1,0:T(2,128)}) custom-call(s32[6]{0:T(128)S(1)} %pad_add_fusion.place_ref, bf16[512,512]{1,0:T(8,128)(2,1)S(1)} %bitcast.15, bf16[512,512]{1,0:T(8,128)(2,1)S(1)} %collective-permute-done.16.refs_1_, bf16[256,512]{1,0:T(8,128)(2,1)S(1)} %get-tuple-element.67.refs_0_.refs_2_.refs_1_, ...), custom_call_target="tpu_custom_call" | custom-call | flops 115000000 | tf_op jit(solution)/shard_map/weight_block/pallas_call | solution.py:342
  78.8 7.9 %all-to-all-done.2.refs_0_ = bf16[16,64,512]{2,1,0:T(8,128)(2,1)S(1)} async-done(((bf16[16,64,512]{2,1,0:T(8,128)(2,1)}), bf16[16,64,512]{2,1,0:T(8,128)(2,1)S(1)}, u32[]{:S(2)}, u32[]{:S(2)}) %all-to-all-start.2) | async-done | bytes 1048608 | tf_op jit(solution)/shard_map/all_to_all | solution.py:495
  86.7 4.8 %all-to-all-start.1 = ((bf16[16,160,128]{2,1,0:T(8,128)(2,1)}), bf16[16,160,128]{2,1,0:T(8,128)(2,1)S(1)}, u32[]{:S(2)}, u32[]{:S(2)}) async-start(bf16[16,160,128]{2,1,0:T(8,128)(2,1)} %get-tuple-element.69), calls=%async_computation.1 | async-start | bytes 1310720 | tf_op jit(solution)/shard_map/all_to_all | solution.py:495
  91.5 1.0 copy-done.1
  92.5 1.0 %copy-done.2 = bf16[512,512]{1,0:T(8,128)(2,1)S(1)} copy-done((bf16[512,512]{1,0:T(8,128)(2,1)S(1)}, bf16[512,512]{1,0:T(8,128)(2,1)}, u32[]{:S(2)}) %copy-start.2) | copy-done | bytes 524312
  93.6 3.5 %add_pairs.1 = (bf16[512,512]{1,0:T(8,128)(2,1)}, bf16[512,512]{1,0:T(8,128)(2,1)}) custom-call(bf16[512,512]{1,0:T(8,128)(2,1)S(1)} %copy-done.1, bf16[512,512]{1,0:T(8,128)(2,1)} %collective-permute-done.4.b_ref, bf16[512,512]{1,0:T(8,128)(2,1)S(1)} %copy-done.2, bf16[512,512]{1,0:T(8,128)(2,1)} %collective-permute-done.5.d_ref), custom_call_target="tpu_custom_call" | custom-call | flops 115000000 | tf_op jit(solution)/shard_map/add_pairs/pallas_call | solution.py:382
  97.3 5.0 %all-to-all-done.1.last_ref = bf16[16,160,128]{2,1,0:T(8,128)(2,1)S(1)} async-done(((bf16[16,160,128]{2,1,0:T(8,128)(2,1)}), bf16[16,160,128]{2,1,0:T(8,128)(2,1)S(1)}, u32[]{:S(2)}, u32[]{:S(2)}) %all-to-all-start.1) | async-done | bytes 655392 | tf_op jit(solution)/shard_map/all_to_all | solution.py:495
  102.3 1.4 %finish.1 = (f32[8,16,512]{2,1,0:T(8,128)}, f32[8,512]{1,0:T(8,128)}) custom-call(s32[6]{0:T(128)S(1)} %pad_add_fusion.place_ref, bf16[16,160,128]{2,1,0:T(8,128)(2,1)S(1)} %all-to-all-done.1.last_ref, f32[64,512]{1,0:T(8,128)S(1)} %convert_reduce_fusion.sides_ref, f32[32,512]{1,0:T(8,128)S(1)} %convert_reduce_fusion.1.middle_ref), custom_call_target="tpu_custom_call" | custom-call | flops 115000000 | tf_op jit(solution)/shard_map/finish/pallas_call | solution.py:423
  (36 shorter events, 1.1 us)
Async XLA Ops:
  0.6 7.2 %collective-permute-start = (bf16[512,512]{1,0:T(8,128)(2,1)}, bf16[512,512]{1,0:T(8,128)(2,1)S(1)}, u32[]{:S(2)}, u32[]{:S(2)}) collective-permute-start(bf16[512,512]{1,0:T(8,128)(2,1)} %bitcast.19), channel_id=1, source_target_pairs={{0,8},{8,0},{1,9},{9,1},{2,10},{10,2},{3,11},{11,3},{4,12},{12,4},... | collective-permute-start | bytes 1572872 | tf_op jit(solution)/shard_map/ppermute | solution.py:447
  0.7 7.1 %collective-permute-start.1 = (bf16[512,512]{1,0:T(8,128)(2,1)}, bf16[512,512]{1,0:T(8,128)(2,1)S(1)}, u32[]{:S(2)}, u32[]{:S(2)}) collective-permute-start(bf16[512,512]{1,0:T(8,128)(2,1)} %bitcast.22), channel_id=1, source_target_pairs={{0,8},{8,0},{1,9},{9,1},{2,10},{10,2},{3,11},{11,3},{4,12},{12,4},... | collective-permute-start | bytes 1572872 | tf_op jit(solution)/shard_map/ppermute | solution.py:447
  1.2 18.3 %collective-permute-start.2 = (bf16[512,512]{1,0:T(8,128)(2,1)}, bf16[512,512]{1,0:T(8,128)(2,1)S(1)}, u32[]{:S(2)}, u32[]{:S(2)}) collective-permute-start(bf16[512,512]{1,0:T(8,128)(2,1)} %bitcast.12), channel_id=1, source_target_pairs={{0,1},{1,2},{2,3},{3,4},{4,5},{5,6},{6,7},{7,0},{8,9},{9,10},{10,1... | collective-permute-start | bytes 1572872 | tf_op jit(solution)/shard_map/ppermute | solution.py:454
  3.1 16.3 %collective-permute-start.3 = (bf16[512,512]{1,0:T(8,128)(2,1)}, bf16[512,512]{1,0:T(8,128)(2,1)S(1)}, u32[]{:S(2)}, u32[]{:S(2)}) collective-permute-start(bf16[512,512]{1,0:T(8,128)(2,1)} %bitcast.13), channel_id=1, source_target_pairs={{0,7},{1,0},{2,1},{3,2},{4,3},{5,4},{6,5},{7,6},{8,15},{9,8},{10,9... | collective-permute-start | bytes 1572872 | tf_op jit(solution)/shard_map/ppermute | solution.py:457
  19.5 14.7 %collective-permute-start.6 = (bf16[512,512]{1,0:T(8,128)(2,1)S(1)}, bf16[512,512]{1,0:T(8,128)(2,1)}, u32[]{:S(2)}, u32[]{:S(2)}) collective-permute-start(bf16[512,512]{1,0:T(8,128)(2,1)S(1)} %gate.9.refs_6_.old_down_ref.refs_0_), channel_id=1, source_target_pairs={{0,1},{1,2},{2,3},{3,4},{4,5},{5,6},{6,7},{7,0},{8,9},{9,10},{10,1... | collective-permute-start | bytes 1572872 | tf_op jit(solution)/shard_map/ppermute | solution.py:454
  19.5 14.7 %collective-permute-start.8 = (bf16[512,512]{1,0:T(8,128)(2,1)S(1)}, bf16[512,512]{1,0:T(8,128)(2,1)}, u32[]{:S(2)}, u32[]{:S(2)}) collective-permute-start(bf16[512,512]{1,0:T(8,128)(2,1)S(1)} %gate.10.refs_7_.old_up_ref.refs_5_), channel_id=1, source_target_pairs={{0,7},{1,0},{2,1},{3,2},{4,3},{5,4},{6,5},{7,6},{8,15},{9,8},{10,9... | collective-permute-start | bytes 1572872 | tf_op jit(solution)/shard_map/ppermute | solution.py:457
  34.2 5.1 %collective-permute-start.11 = (bf16[512,512]{1,0:T(8,128)(2,1)S(1)}, bf16[512,512]{1,0:T(8,128)(2,1)S(1)}, u32[]{:S(2)}, u32[]{:S(2)}) collective-permute-start(bf16[512,512]{1,0:T(8,128)(2,1)S(1)} %get-tuple-element.56.refs_3_.refs_6_.refs_4_), channel_id=1, source_target_pairs={{0,8},{8,0},{1,9},{9,1},{2,10},{10,2},{3,11},{11,3},{4,12},{12,4},... | collective-permute-start | bytes 1572872 | tf_op jit(solution)/shard_map/ppermute | solution.py:447
  35.5 3.8 %collective-permute-start.10 = (bf16[512,512]{1,0:T(8,128)(2,1)S(1)}, bf16[512,512]{1,0:T(8,128)(2,1)S(1)}, u32[]{:S(2)}, u32[]{:S(2)}) collective-permute-start(bf16[512,512]{1,0:T(8,128)(2,1)S(1)} %pick_other.2), channel_id=1, source_target_pairs={{0,8},{8,0},{1,9},{9,1},{2,10},{10,2},{3,11},{11,3},{4,12},{12,4},... | collective-permute-start | bytes 1572872 | tf_op jit(solution)/shard_map/ppermute | solution.py:447
  36.1 15.5 %collective-permute-start.7 = (bf16[512,512]{1,0:T(8,128)(2,1)}, bf16[512,512]{1,0:T(8,128)(2,1)S(1)}, u32[]{:S(2)}, u32[]{:S(2)}) collective-permute-start(bf16[512,512]{1,0:T(8,128)(2,1)} %get-tuple-element.55.near_ref.refs_0_), channel_id=1, source_target_pairs={{0,1},{1,2},{2,3},{3,4},{4,5},{5,6},{6,7},{7,0},{8,9},{9,10},{10,1... | collective-permute-start | bytes 1572872 | tf_op jit(solution)/shard_map/ppermute | solution.py:454
  36.1 15.5 %collective-permute-start.9 = (bf16[512,512]{1,0:T(8,128)(2,1)}, bf16[512,512]{1,0:T(8,128)(2,1)S(1)}, u32[]{:S(2)}, u32[]{:S(2)}) collective-permute-start(bf16[512,512]{1,0:T(8,128)(2,1)} %gate.12.refs_0_.refs_2_), channel_id=1, source_target_pairs={{0,7},{1,0},{2,1},{3,2},{4,3},{5,4},{6,5},{7,6},{8,15},{9,8},{10,9... | collective-permute-start | bytes 1572872 | tf_op jit(solution)/shard_map/ppermute | solution.py:457
  42.8 17.5 %all-to-all-start = ((bf16[16,32,512]{2,1,0:T(8,128)(2,1)}), bf16[16,32,512]{2,1,0:T(8,128)(2,1)S(1)}, u32[]{:S(2)}, u32[]{:S(2)}) async-start(bf16[16,32,512]{2,1,0:T(8,128)(2,1)} %get-tuple-element.66), calls=%async_computation | async-start | bytes 1048576 | tf_op jit(solution)/shard_map/all_to_all | solution.py:495
  53.5 6.9 %collective-permute-start.14 = (bf16[512,512]{1,0:T(8,128)(2,1)}, bf16[512,512]{1,0:T(8,128)(2,1)}, u32[]{:S(2)}, u32[]{:S(2)}) collective-permute-start(bf16[512,512]{1,0:T(8,128)(2,1)} %get-tuple-element.62), channel_id=1, source_target_pairs={{0,8},{8,0},{1,9},{9,1},{2,10},{10,2},{3,11},{11,3},{4,12},{12,4},... | collective-permute-start | bytes 1572872 | tf_op jit(solution)/shard_map/ppermute | solution.py:447
  53.5 6.9 %collective-permute-start.15 = (bf16[512,512]{1,0:T(8,128)(2,1)}, bf16[512,512]{1,0:T(8,128)(2,1)}, u32[]{:S(2)}, u32[]{:S(2)}) collective-permute-start(bf16[512,512]{1,0:T(8,128)(2,1)} %get-tuple-element.63), channel_id=1, source_target_pairs={{0,8},{8,0},{1,9},{9,1},{2,10},{10,2},{3,11},{11,3},{4,12},{12,4},... | collective-permute-start | bytes 1572872 | tf_op jit(solution)/shard_map/ppermute | solution.py:447
  54.0 11.3 %collective-permute-start.12 = (bf16[256,512]{1,0:T(8,128)(2,1)}, bf16[256,512]{1,0:T(8,128)(2,1)S(1)}, u32[]{:S(2)}, u32[]{:S(2)}) collective-permute-start(bf16[256,512]{1,0:T(8,128)(2,1)} %get-tuple-element.60), channel_id=1, source_target_pairs={{0,1},{1,2},{2,3},{3,4},{4,5},{5,6},{6,7},{7,0},{8,9},{9,10},{10,1... | collective-permute-start | bytes 786440 | tf_op jit(solution)/shard_map/ppermute | solution.py:454
  55.9 9.4 %collective-permute-start.13 = (bf16[256,512]{1,0:T(8,128)(2,1)}, bf16[256,512]{1,0:T(8,128)(2,1)}, u32[]{:S(2)}, u32[]{:S(2)}) collective-permute-start(bf16[256,512]{1,0:T(8,128)(2,1)} %get-tuple-element.61), channel_id=1, source_target_pairs={{0,7},{1,0},{2,1},{3,2},{4,3},{5,4},{6,5},{7,6},{8,15},{9,8},{10,9... | collective-permute-start | bytes 786440 | tf_op jit(solution)/shard_map/ppermute | solution.py:457
  65.2 6.4 %copy-start = (bf16[1,512,512]{2,1,0:T(8,128)(2,1)S(1)}, bf16[1,512,512]{2,1,0:T(8,128)(2,1)}, u32[]{:S(2)}) copy-start(bf16[1,512,512]{2,1,0:T(8,128)(2,1)} %param.11) | copy-start | bytes 1572868
  65.3 21.4 %all-to-all-start.2 = ((bf16[16,64,512]{2,1,0:T(8,128)(2,1)}), bf16[16,64,512]{2,1,0:T(8,128)(2,1)S(1)}, u32[]{:S(2)}, u32[]{:S(2)}) async-start(bf16[16,64,512]{2,1,0:T(8,128)(2,1)} %gate.16), calls=%async_computation.2 | async-start | bytes 2097152 | tf_op jit(solution)/shard_map/all_to_all | solution.py:495
  72.6 2.0 %collective-permute-start.16 = (bf16[512,512]{1,0:T(8,128)(2,1)S(1)}, bf16[512,512]{1,0:T(8,128)(2,1)S(1)}, u32[]{:S(2)}, u32[]{:S(2)}) collective-permute-start(bf16[512,512]{1,0:T(8,128)(2,1)S(1)} %pick_other.3), channel_id=1, source_target_pairs={{0,8},{8,0},{1,9},{9,1},{2,10},{10,2},{3,11},{11,3},{4,12},{12,4},... | collective-permute-start | bytes 1572872 | tf_op jit(solution)/shard_map/ppermute | solution.py:447
  72.7 18.7 %collective-permute-start.4 = (bf16[512,512]{1,0:T(8,128)(2,1)}, bf16[512,512]{1,0:T(8,128)(2,1)}, u32[]{:S(2)}, u32[]{:S(2)}) collective-permute-start(bf16[512,512]{1,0:T(8,128)(2,1)} %get-tuple-element.48), channel_id=1, source_target_pairs={{0,8},{8,0},{1,9},{9,1},{2,10},{10,2},{3,11},{11,3},{4,12},{12,4},... | collective-permute-start | bytes 1572872 | tf_op jit(solution)/shard_map/ppermute | solution.py:447
  73.2 18.3 %collective-permute-start.5 = (bf16[512,512]{1,0:T(8,128)(2,1)}, bf16[512,512]{1,0:T(8,128)(2,1)}, u32[]{:S(2)}, u32[]{:S(2)}) collective-permute-start(bf16[512,512]{1,0:T(8,128)(2,1)} %get-tuple-element.50), channel_id=1, source_target_pairs={{0,8},{8,0},{1,9},{9,1},{2,10},{10,2},{3,11},{11,3},{4,12},{12,4},... | collective-permute-start | bytes 1572872 | tf_op jit(solution)/shard_map/ppermute | solution.py:447
  86.7 15.6 %all-to-all-start.1 = ((bf16[16,160,128]{2,1,0:T(8,128)(2,1)}), bf16[16,160,128]{2,1,0:T(8,128)(2,1)S(1)}, u32[]{:S(2)}, u32[]{:S(2)}) async-start(bf16[16,160,128]{2,1,0:T(8,128)(2,1)} %get-tuple-element.69), calls=%async_computation.1 | async-start | bytes 1310720 | tf_op jit(solution)/shard_map/all_to_all | solution.py:495
  91.5 1.0 %copy-start.1 = (bf16[512,512]{1,0:T(8,128)(2,1)S(1)}, bf16[512,512]{1,0:T(8,128)(2,1)}, u32[]{:S(2)}) copy-start(bf16[512,512]{1,0:T(8,128)(2,1)} %get-tuple-element.47.a_ref) | copy-start | bytes 1572868
  92.5 1.0 %copy-start.2 = (bf16[512,512]{1,0:T(8,128)(2,1)S(1)}, bf16[512,512]{1,0:T(8,128)(2,1)}, u32[]{:S(2)}) copy-start(bf16[512,512]{1,0:T(8,128)(2,1)} %get-tuple-element.49.c_ref) | copy-start | bytes 1572868

commit v5 on v4

--- a/solution.py
+++ b/solution.py
@@ -224,10 +224,12 @@
     )(place, down, up, old_down, old_up)
 
 
-def weight_kernel(place_ref, *refs, pairs, pieces, chips, dp_count, known, keep_att):
+def weight_kernel(
+    place_ref, *refs, pairs, pieces, choices, chips, dp_count, known, keep_att
+):
     count = len(pairs)
     near, refs = refs[:count], refs[count:]
-    recv, refs = refs[:count], refs[count:]
+    recv, refs = refs[: count * choices], refs[count * choices :]
     far, refs = refs[: count * pieces], refs[count * pieces :]
     att_refs, carried_ref, refs = refs[:2], refs[2], refs[3:]
     known_refs, refs = refs[:known], refs[known:]
@@ -246,8 +248,10 @@
         source = near[index].at[part(piece)] if from_near else far[index * pieces + piece]
         return pltpu.make_async_copy(source, mine.at[index, part(piece)], sems.at[1 + piece, index])
 
-    def fetch_other(index):
-        return pltpu.make_async_copy(recv[index], other.at[index], sems.at[0, index])
+    def fetch_other(index, choice=0):
+        return pltpu.make_async_copy(
+            recv[index * choices + choice], other.at[index], sems.at[0, index]
+        )
 
     def fetch_att(side):
         return pltpu.make_async_copy(att_refs[side], atts.at[side], sems.at[3, side])
@@ -274,7 +278,11 @@
         for piece in range(pieces):
             pl.when(keep)(fetch_mine(index, piece, True).start)
             pl.when(jnp.logical_not(keep))(fetch_mine(index, piece, False).start)
-        fetch_other(index).start()
+        if choices == 1:
+            fetch_other(index).start()
+        else:
+            pl.when(keep)(fetch_other(index, 0).start)
+            pl.when(jnp.logical_not(keep))(fetch_other(index, 1).start)
         if index == 0:
             fetch_att(1).start()
         fetch_carried(2 * index).start()
@@ -344,13 +352,14 @@
             weight_kernel,
             pairs=pairs,
             pieces=pieces,
+            choices=len(recv) // count,
             chips=chips,
             dp_count=dp_count,
             known=len(known),
             keep_att=keep_att,
         ),
         in_specs=[pl.BlockSpec(memory_space=pltpu.SMEM)]
-        + [anywhere] * (count * (2 + pieces) + 2)
+        + [anywhere] * (count * (1 + pieces) + len(recv) + 2)
         + [hbm]
         + [vmem] * len(known),
         out_specs=[hbm, vmem] + [hbm] * keep_att,
@@ -494,9 +503,9 @@
     def exchange(array):
         return lax.all_to_all(array, "dp", 0, 0, tiled=True)
 
-    recv2 = swapped(2, from_down[2], [from_up[2]])
+    recv2 = [peer(from_down[2]), peer(from_up[2])]
     terms, peaks2, att_peer = weigh(
-        (2,), [from_down[2]], [[from_up[2]]], [recv2], (att, peer(att)), keep_att=True
+        (2,), [from_down[2]], [[from_up[2]]], recv2, (att, peer(att)), keep_att=True
     )
     atts = (att, stay(att_peer))
     (middle,) = gate([exchange(terms)], [], 1.0)

time: 105 us -> 104 us (level)
  Pallas kernels: 39.8 us -> 38.5 us
    pallas_call x2 -> x1, Pallas kernels: 2.31 us -> 1.04 us  [pick_other(): pl.pallas_call(functools.partial(pick_kernel, pair=pair, chips=chips, cou...]
    ppermute x9 -> x10, starting transfers between devices: 2.38 us -> 2.3 us  [peer(): return lax.ppermute(array, 'seq', swap)]
  transfers between devices with their start and end apart: 20 -> 21, of which waited for: 7 -> 7; matrix products, arithmetic and copies ran while one was open for 1% -> 1% of each run, Pallas kernels for 37% -> 36%
where the time goes in v5:
time: 104 us; the launch traced here: 102 us
  Pallas kernels  38.5 us (37%)
  starting transfers between devices  36.3 us (35%)
  waiting for transfers between devices  23.7 us (23%)
  local copies, waits for them, and re-layouts  2.08 us (2%)
    pallas_call x2, Pallas kernels, attention(): pl.pallas_call(functools.partial(attention_kernel, tile=256, first=first,...  18.4 us
    all_to_all x3, starting transfers between devices, exchange(): return lax.all_to_all(array, 'dp', 0, 0, tiled=True)  18.4 us
    all_to_all x3, waiting for transfers between devices, exchange(): return lax.all_to_all(array, 'dp', 0, 0, tiled=True)  16.2 us
    pallas_call x3, Pallas kernels, weight_block(): pl.pallas_call(functools.partial(weight_kernel, pairs=pairs, pieces=piece...  12.5 us
    ppermute x4, starting transfers between devices, send_down(): return lax.ppermute(array, 'tensor', down)  12 us
    ppermute x4, waiting for transfers between devices, send_up(): return lax.ppermute(array, 'tensor', up)  6.22 us
    ppermute x4, starting transfers between devices, send_up(): return lax.ppermute(array, 'tensor', up)  3.63 us
    pallas_call x1, Pallas kernels, add_pairs(): pl.pallas_call(add_kernel, grid=(4,), in_specs=[spec] * 4, out_specs=[spe...  3.45 us
  transfers between devices with their start and end apart: 21, of which 7 were waited for; matrix products, arithmetic and copies ran while one was open for 1% of the time, Pallas kernels for 36%

profile of v5, /device:TPU:2, one launch (start us, length us, event | category | flops | bytes accessed | tf_op | source)
XLA Modules:
  0.0 102.4 jit_solution(10328560952333059750)
XLA Ops:
  0.7 0.5 collective-permute-start.1
  1.2 1.9 %collective-permute-start.2 = (bf16[512,512]{1,0:T(8,128)(2,1)}, bf16[512,512]{1,0:T(8,128)(2,1)S(1)}, u32[]{:S(2)}, u32[]{:S(2)}) collective-permute-start(bf16[512,512]{1,0:T(8,128)(2,1)} %bitcast.12), channel_id=1, source_target_pairs={{0,1},{1,2},{2,3},{3,4},{4,5},{5,6},{6,7},{7,0},{8,9},{9,10},{10,1... | collective-permute-start | bytes 1572872 | tf_op jit(solution)/shard_map/ppermute | solution.py:463
  3.1 3.9 %collective-permute-start.3 = (bf16[512,512]{1,0:T(8,128)(2,1)}, bf16[512,512]{1,0:T(8,128)(2,1)S(1)}, u32[]{:S(2)}, u32[]{:S(2)}) collective-permute-start(bf16[512,512]{1,0:T(8,128)(2,1)} %bitcast.13), channel_id=1, source_target_pairs={{0,7},{1,0},{2,1},{3,2},{4,3},{5,4},{6,5},{7,6},{8,15},{9,8},{10,9... | collective-permute-start | bytes 1572872 | tf_op jit(solution)/shard_map/ppermute | solution.py:466
  7.1 0.7 pad_add_fusion.place_ref
  7.8 9.2 %attention.2 = (bf16[512,512]{1,0:T(8,128)(2,1)S(1)}, bf16[512,512]{1,0:T(8,128)(2,1)}, bf16[512,512]{1,0:T(8,128)(2,1)}, bf16[512,512]{1,0:T(8,128)(2,1)}, bf16...) custom-call(s32[6]{0:T(128)S(1)} %pad_add_fusion.place_ref, ...), custom_call_target="tpu_custom_call" | custom-call | flops 230000000 | tf_op jit(solution)/shard_map/attention/pallas_call | solution.py:117
  17.0 2.5 %collective-permute-done.2.refs_0_ = bf16[512,512]{1,0:T(8,128)(2,1)S(1)} collective-permute-done((bf16[512,512]{1,0:T(8,128)(2,1)}, bf16[512,512]{1,0:T(8,128)(2,1)S(1)}, u32[]{:S(2)}, u32[]{:S(2)}) %collective-permute-start.2) | collective-permute-done | bytes 524320 | tf_op jit(solution)/shard_map/ppermute | solution.py:463
  19.5 3.2 %collective-permute-start.8 = (bf16[512,512]{1,0:T(8,128)(2,1)S(1)}, bf16[512,512]{1,0:T(8,128)(2,1)}, u32[]{:S(2)}, u32[]{:S(2)}) collective-permute-start(bf16[512,512]{1,0:T(8,128)(2,1)S(1)} %gate.10.refs_7_.old_up_ref.refs_5_), channel_id=1, source_target_pairs={{0,7},{1,0},{2,1},{3,2},{4,3},{5,4},{6,5},{7,6},{8,15},{9,8},{10,9... | collective-permute-start | bytes 1572872 | tf_op jit(solution)/shard_map/ppermute | solution.py:466
  22.7 9.2 %attention.3 = (bf16[512,512]{1,0:T(8,128)(2,1)S(1)}, bf16[512,512]{1,0:T(8,128)(2,1)}, bf16[512,512]{1,0:T(8,128)(2,1)}, bf16[512,512]{1,0:T(8,128)(2,1)}, bf16...) custom-call(s32[6]{0:T(128)S(1)} %pad_add_fusion.place_ref, ...), custom_call_target="tpu_custom_call", output_to_operand_aliasing={{0}: (7, {}), {1}: (8, {}), {2}: (9, {}), {3}: (10, {}), {4... | custom-call | flops 230000000 | tf_op jit(solution)/shard_map/attention/pallas_call | solution.py:117
  31.9 2.3 %collective-permute-done.6.refs_0_ = bf16[512,512]{1,0:T(8,128)(2,1)} collective-permute-done((bf16[512,512]{1,0:T(8,128)(2,1)S(1)}, bf16[512,512]{1,0:T(8,128)(2,1)}, u32[]{:S(2)}, u32[]{:S(2)}) %collective-permute-start.6) | collective-permute-done | bytes 524320 | tf_op jit(solution)/shard_map/ppermute | solution.py:463
  34.2 0.5 collective-permute-start.12
  34.8 3.2 %collective-permute-start.9 = (bf16[512,512]{1,0:T(8,128)(2,1)}, bf16[512,512]{1,0:T(8,128)(2,1)S(1)}, u32[]{:S(2)}, u32[]{:S(2)}) collective-permute-start(bf16[512,512]{1,0:T(8,128)(2,1)} %gate.12.refs_3_), channel_id=1, source_target_pairs={{0,7},{1,0},{2,1},{3,2},{4,3},{5,4},{6,5},{7,6},{8,15},{9,8},{10,9... | collective-permute-start | bytes 1572872 | tf_op jit(solution)/shard_map/ppermute | solution.py:466
  38.1 3.5 %weight_block.3 = (bf16[16,32,512]{2,1,0:T(8,128)(2,1)}, f32[2,512]{1,0:T(2,128)S(1)}, bf16[512,512]{1,0:T(8,128)(2,1)}) custom-call(s32[6]{0:T(128)S(1)} %pad_add_fusion.place_ref, bf16[512,512]{1,0:T(8,128)(2,1)} %get-tuple-element.55.refs_0_, bf16[512,512]{1,0:T(8,128)(2,1)S(1)} %collective-permute-done.10.refs_1_, ...), custom_call_target="tpu_custom_call" | custom-call | flops 115000000 | tf_op jit(solution)/shard_map/weight_block/pallas_call | solution.py:350
  41.5 7.5 %all-to-all-start = ((bf16[16,32,512]{2,1,0:T(8,128)(2,1)}), bf16[16,32,512]{2,1,0:T(8,128)(2,1)S(1)}, u32[]{:S(2)}, u32[]{:S(2)}) async-start(bf16[16,32,512]{2,1,0:T(8,128)(2,1)} %get-tuple-element.66), calls=%async_computation | async-start | bytes 1048576 | tf_op jit(solution)/shard_map/all_to_all | solution.py:504
  49.0 1.5 %collective-permute-done.7.refs_0_ = bf16[512,512]{1,0:T(8,128)(2,1)S(1)} collective-permute-done((bf16[512,512]{1,0:T(8,128)(2,1)}, bf16[512,512]{1,0:T(8,128)(2,1)S(1)}, u32[]{:S(2)}, u32[]{:S(2)}) %collective-permute-start.7) | collective-permute-done | bytes 524320 | tf_op jit(solution)/shard_map/ppermute | solution.py:463
  50.5 1.9 %fork.1 = (bf16[512,512]{1,0:T(8,128)(2,1)}, bf16[512,512]{1,0:T(8,128)(2,1)}, bf16[256,512]{1,0:T(8,128)(2,1)}, bf16[256,512]{1,0:T(8,128)(2,1)}) custom-call(s32[6]{0:T(128)S(1)} %pad_add_fusion.place_ref, bf16[512,512]{1,0:T(8,128)(2,1)S(1)} %get-tuple-element.58.down_ref.refs_1_, bf16[512,512]{1,0:T(8,128)(2,1)S(1)} %get-tuple-element.59.up_ref.refs_4_, ...), custom_call_target="tpu_custom_call" | custom-call | flops 11500000 | tf_op jit(solution)/shard_map/fork/pallas_call | solution.py:215
  52.3 0.5 collective-permute-start.16
  52.9 1.6 %collective-permute-start.13 = (bf16[256,512]{1,0:T(8,128)(2,1)}, bf16[256,512]{1,0:T(8,128)(2,1)S(1)}, u32[]{:S(2)}, u32[]{:S(2)}) collective-permute-start(bf16[256,512]{1,0:T(8,128)(2,1)} %get-tuple-element.60), channel_id=1, source_target_pairs={{0,1},{1,2},{2,3},{3,4},{4,5},{5,6},{6,7},{7,0},{8,9},{9,10},{10,1... | collective-permute-start | bytes 786440 | tf_op jit(solution)/shard_map/ppermute | solution.py:463
  54.5 1.6 %collective-permute-start.14 = (bf16[256,512]{1,0:T(8,128)(2,1)}, bf16[256,512]{1,0:T(8,128)(2,1)}, u32[]{:S(2)}, u32[]{:S(2)}) collective-permute-start(bf16[256,512]{1,0:T(8,128)(2,1)} %get-tuple-element.61), channel_id=1, source_target_pairs={{0,7},{1,0},{2,1},{3,2},{4,3},{5,4},{6,5},{7,6},{8,15},{9,8},{10,9... | collective-permute-start | bytes 786440 | tf_op jit(solution)/shard_map/ppermute | solution.py:466
  56.1 3.2 %all-to-all-done.refs_0_ = bf16[16,32,512]{2,1,0:T(8,128)(2,1)S(1)} async-done(((bf16[16,32,512]{2,1,0:T(8,128)(2,1)}), bf16[16,32,512]{2,1,0:T(8,128)(2,1)S(1)}, u32[]{:S(2)}, u32[]{:S(2)}) %all-to-all-start) | async-done | bytes 524320 | tf_op jit(solution)/shard_map/all_to_all | solution.py:504
  59.3 4.8 %weight_block.4 = (bf16[16,64,512]{2,1,0:T(8,128)(2,1)}, f32[4,512]{1,0:T(4,128)S(1)}) custom-call(s32[6]{0:T(128)S(1)} %pad_add_fusion.place_ref, bf16[512,512]{1,0:T(8,128)(2,1)S(1)} %gate.9.refs_6_.old_down_ref.refs_0_, bf16[512,512]{1,0:T(8,128)(2,1)S(1)} %get-tuple-element.58.down_ref.refs_1_, bf16[512,512]{1,0:T(8,128)(2,1)} %collective-permute-done.15.refs_2_, ...), custom_call_target="tpu_custom_call" | custom-call | flops 115000000 | tf_op jit(solution)/shard_map/weight_block/pallas_call | solution.py:350
  64.2 6.1 %all-to-all-start.2 = ((bf16[16,64,512]{2,1,0:T(8,128)(2,1)}), bf16[16,64,512]{2,1,0:T(8,128)(2,1)S(1)}, u32[]{:S(2)}, u32[]{:S(2)}) async-start(bf16[16,64,512]{2,1,0:T(8,128)(2,1)} %gate.16), calls=%async_computation.2 | async-start | bytes 2097152 | tf_op jit(solution)/shard_map/all_to_all | solution.py:504
  70.2 1.0 %pick_other.1 = bf16[512,512]{1,0:T(8,128)(2,1)S(1)} custom-call(s32[6]{0:T(128)S(1)} %pad_add_fusion.place_ref, bf16[512,512]{1,0:T(8,128)(2,1)S(1)} %bitcast.14, bf16[256,512]{1,0:T(8,128)(2,1)S(1)} %get-tuple-element.67.refs_0_.refs_2_.refs_1_, bf16[256,512]{1,0:T(8,128)(2,1)} %get-tuple-element.68.refs_1_.refs_3_.refs_2_), custom_call_target="tpu_custom_call" | custom-call | flops 11500000 | tf_op jit(solution)/shard_map/pick_other/pallas_call | solution.py:186
  71.4 0.5 collective-permute-start.4
  72.0 1.3 %collective-permute-done.17.refs_1_ = bf16[512,512]{1,0:T(8,128)(2,1)S(1)} collective-permute-done((bf16[512,512]{1,0:T(8,128)(2,1)S(1)}, bf16[512,512]{1,0:T(8,128)(2,1)S(1)}, u32[]{:S(2)}, u32[]{:S(2)}) %collective-permute-start.17) | collective-permute-done | bytes 524320 | tf_op jit(solution)/shard_map/ppermute | solution.py:456
  73.3 4.2 %weight_block.5 = (bf16[16,160,128]{2,1,0:T(8,128)(2,1)}, f32[2,512]{1,0:T(2,128)}) custom-call(s32[6]{0:T(128)S(1)} %pad_add_fusion.place_ref, bf16[512,512]{1,0:T(8,128)(2,1)S(1)} %bitcast.15, bf16[512,512]{1,0:T(8,128)(2,1)S(1)} %collective-permute-done.17.refs_1_, bf16[256,512]{1,0:T(8,128)(2,1)S(1)} %get-tuple-element.67.refs_0_.refs_2_.refs_1_, ...), custom_call_target="tpu_custom_call" | custom-call | flops 115000000 | tf_op jit(solution)/shard_map/weight_block/pallas_call | solution.py:350
  77.4 7.9 %all-to-all-done.2.refs_0_ = bf16[16,64,512]{2,1,0:T(8,128)(2,1)S(1)} async-done(((bf16[16,64,512]{2,1,0:T(8,128)(2,1)}), bf16[16,64,512]{2,1,0:T(8,128)(2,1)S(1)}, u32[]{:S(2)}, u32[]{:S(2)}) %all-to-all-start.2) | async-done | bytes 1048608 | tf_op jit(solution)/shard_map/all_to_all | solution.py:504
  85.3 4.8 %all-to-all-start.1 = ((bf16[16,160,128]{2,1,0:T(8,128)(2,1)}), bf16[16,160,128]{2,1,0:T(8,128)(2,1)S(1)}, u32[]{:S(2)}, u32[]{:S(2)}) async-start(bf16[16,160,128]{2,1,0:T(8,128)(2,1)} %get-tuple-element.69), calls=%async_computation.1 | async-start | bytes 1310720 | tf_op jit(solution)/shard_map/all_to_all | solution.py:504
  90.2 1.0 %copy-done.1 = bf16[512,512]{1,0:T(8,128)(2,1)S(1)} copy-done((bf16[512,512]{1,0:T(8,128)(2,1)S(1)}, bf16[512,512]{1,0:T(8,128)(2,1)}, u32[]{:S(2)}) %copy-start.1) | copy-done | bytes 524312
  91.2 1.0 %copy-done.2 = bf16[512,512]{1,0:T(8,128)(2,1)S(1)} copy-done((bf16[512,512]{1,0:T(8,128)(2,1)S(1)}, bf16[512,512]{1,0:T(8,128)(2,1)}, u32[]{:S(2)}) %copy-start.2) | copy-done | bytes 524312
  92.2 3.5 %add_pairs.1 = (bf16[512,512]{1,0:T(8,128)(2,1)}, bf16[512,512]{1,0:T(8,128)(2,1)}) custom-call(bf16[512,512]{1,0:T(8,128)(2,1)S(1)} %copy-done.1, bf16[512,512]{1,0:T(8,128)(2,1)} %collective-permute-done.4.b_ref, bf16[512,512]{1,0:T(8,128)(2,1)S(1)} %copy-done.2, bf16[512,512]{1,0:T(8,128)(2,1)} %collective-permute-done.5.d_ref), custom_call_target="tpu_custom_call" | custom-call | flops 115000000 | tf_op jit(solution)/shard_map/add_pairs/pallas_call | solution.py:391
  95.9 5.1 %all-to-all-done.1.last_ref = bf16[16,160,128]{2,1,0:T(8,128)(2,1)S(1)} async-done(((bf16[16,160,128]{2,1,0:T(8,128)(2,1)}), bf16[16,160,128]{2,1,0:T(8,128)(2,1)S(1)}, u32[]{:S(2)}, u32[]{:S(2)}) %all-to-all-start.1) | async-done | bytes 655392 | tf_op jit(solution)/shard_map/all_to_all | solution.py:504
  101.0 1.4 %finish.1 = (f32[8,16,512]{2,1,0:T(8,128)}, f32[8,512]{1,0:T(8,128)}) custom-call(s32[6]{0:T(128)S(1)} %pad_add_fusion.place_ref, bf16[16,160,128]{2,1,0:T(8,128)(2,1)S(1)} %all-to-all-done.1.last_ref, f32[64,512]{1,0:T(8,128)S(1)} %convert_reduce_fusion.sides_ref, f32[32,512]{1,0:T(8,128)S(1)} %convert_reduce_fusion.1.middle_ref), custom_call_target="tpu_custom_call" | custom-call | flops 115000000 | tf_op jit(solution)/shard_map/finish/pallas_call | solution.py:432
  (37 shorter events, 0.7 us)
Async XLA Ops:
  0.6 7.2 %collective-permute-start = (bf16[512,512]{1,0:T(8,128)(2,1)}, bf16[512,512]{1,0:T(8,128)(2,1)S(1)}, u32[]{:S(2)}, u32[]{:S(2)}) collective-permute-start(bf16[512,512]{1,0:T(8,128)(2,1)} %bitcast.19), channel_id=1, source_target_pairs={{0,8},{8,0},{1,9},{9,1},{2,10},{10,2},{3,11},{11,3},{4,12},{12,4},... | collective-permute-start | bytes 1572872 | tf_op jit(solution)/shard_map/ppermute | solution.py:456
  0.7 7.1 %collective-permute-start.1 = (bf16[512,512]{1,0:T(8,128)(2,1)}, bf16[512,512]{1,0:T(8,128)(2,1)S(1)}, u32[]{:S(2)}, u32[]{:S(2)}) collective-permute-start(bf16[512,512]{1,0:T(8,128)(2,1)} %bitcast.22), channel_id=1, source_target_pairs={{0,8},{8,0},{1,9},{9,1},{2,10},{10,2},{3,11},{11,3},{4,12},{12,4},... | collective-permute-start | bytes 1572872 | tf_op jit(solution)/shard_map/ppermute | solution.py:456
  1.2 18.3 %collective-permute-start.2 = (bf16[512,512]{1,0:T(8,128)(2,1)}, bf16[512,512]{1,0:T(8,128)(2,1)S(1)}, u32[]{:S(2)}, u32[]{:S(2)}) collective-permute-start(bf16[512,512]{1,0:T(8,128)(2,1)} %bitcast.12), channel_id=1, source_target_pairs={{0,1},{1,2},{2,3},{3,4},{4,5},{5,6},{6,7},{7,0},{8,9},{9,10},{10,1... | collective-permute-start | bytes 1572872 | tf_op jit(solution)/shard_map/ppermute | solution.py:463
  3.1 16.3 %collective-permute-start.3 = (bf16[512,512]{1,0:T(8,128)(2,1)}, bf16[512,512]{1,0:T(8,128)(2,1)S(1)}, u32[]{:S(2)}, u32[]{:S(2)}) collective-permute-start(bf16[512,512]{1,0:T(8,128)(2,1)} %bitcast.13), channel_id=1, source_target_pairs={{0,7},{1,0},{2,1},{3,2},{4,3},{5,4},{6,5},{7,6},{8,15},{9,8},{10,9... | collective-permute-start | bytes 1572872 | tf_op jit(solution)/shard_map/ppermute | solution.py:466
  19.5 14.7 %collective-permute-start.6 = (bf16[512,512]{1,0:T(8,128)(2,1)S(1)}, bf16[512,512]{1,0:T(8,128)(2,1)}, u32[]{:S(2)}, u32[]{:S(2)}) collective-permute-start(bf16[512,512]{1,0:T(8,128)(2,1)S(1)} %gate.9.refs_6_.old_down_ref.refs_0_), channel_id=1, source_target_pairs={{0,1},{1,2},{2,3},{3,4},{4,5},{5,6},{6,7},{7,0},{8,9},{9,10},{10,1... | collective-permute-start | bytes 1572872 | tf_op jit(solution)/shard_map/ppermute | solution.py:463
  19.5 15.2 %collective-permute-start.8 = (bf16[512,512]{1,0:T(8,128)(2,1)S(1)}, bf16[512,512]{1,0:T(8,128)(2,1)}, u32[]{:S(2)}, u32[]{:S(2)}) collective-permute-start(bf16[512,512]{1,0:T(8,128)(2,1)S(1)} %gate.10.refs_7_.old_up_ref.refs_5_), channel_id=1, source_target_pairs={{0,7},{1,0},{2,1},{3,2},{4,3},{5,4},{6,5},{7,6},{8,15},{9,8},{10,9... | collective-permute-start | bytes 1572872 | tf_op jit(solution)/shard_map/ppermute | solution.py:466
  34.2 3.8 %collective-permute-start.10 = (bf16[512,512]{1,0:T(8,128)(2,1)}, bf16[512,512]{1,0:T(8,128)(2,1)S(1)}, u32[]{:S(2)}, u32[]{:S(2)}) collective-permute-start(bf16[512,512]{1,0:T(8,128)(2,1)} %get-tuple-element.55.refs_0_), channel_id=1, source_target_pairs={{0,8},{8,0},{1,9},{9,1},{2,10},{10,2},{3,11},{11,3},{4,12},{12,4},... | collective-permute-start | bytes 1572872 | tf_op jit(solution)/shard_map/ppermute | solution.py:456
  34.2 3.8 %collective-permute-start.12 = (bf16[512,512]{1,0:T(8,128)(2,1)S(1)}, bf16[512,512]{1,0:T(8,128)(2,1)S(1)}, u32[]{:S(2)}, u32[]{:S(2)}) collective-permute-start(bf16[512,512]{1,0:T(8,128)(2,1)S(1)} %get-tuple-element.56.refs_4_.refs_6_), channel_id=1, source_target_pairs={{0,8},{8,0},{1,9},{9,1},{2,10},{10,2},{3,11},{11,3},{4,12},{12,4},... | collective-permute-start | bytes 1572872 | tf_op jit(solution)/shard_map/ppermute | solution.py:456
  34.7 3.3 %collective-permute-start.11 = (bf16[512,512]{1,0:T(8,128)(2,1)}, bf16[512,512]{1,0:T(8,128)(2,1)S(1)}, u32[]{:S(2)}, u32[]{:S(2)}) collective-permute-start(bf16[512,512]{1,0:T(8,128)(2,1)} %gate.12.refs_3_), channel_id=1, source_target_pairs={{0,8},{8,0},{1,9},{9,1},{2,10},{10,2},{3,11},{11,3},{4,12},{12,4},... | collective-permute-start | bytes 1572872 | tf_op jit(solution)/shard_map/ppermute | solution.py:456
  34.7 15.8 %collective-permute-start.7 = (bf16[512,512]{1,0:T(8,128)(2,1)}, bf16[512,512]{1,0:T(8,128)(2,1)S(1)}, u32[]{:S(2)}, u32[]{:S(2)}) collective-permute-start(bf16[512,512]{1,0:T(8,128)(2,1)} %get-tuple-element.55.refs_0_), channel_id=1, source_target_pairs={{0,1},{1,2},{2,3},{3,4},{4,5},{5,6},{6,7},{7,0},{8,9},{9,10},{10,1... | collective-permute-start | bytes 1572872 | tf_op jit(solution)/shard_map/ppermute | solution.py:463
  34.8 15.7 %collective-permute-start.9 = (bf16[512,512]{1,0:T(8,128)(2,1)}, bf16[512,512]{1,0:T(8,128)(2,1)S(1)}, u32[]{:S(2)}, u32[]{:S(2)}) collective-permute-start(bf16[512,512]{1,0:T(8,128)(2,1)} %gate.12.refs_3_), channel_id=1, source_target_pairs={{0,7},{1,0},{2,1},{3,2},{4,3},{5,4},{6,5},{7,6},{8,15},{9,8},{10,9... | collective-permute-start | bytes 1572872 | tf_op jit(solution)/shard_map/ppermute | solution.py:466
  41.5 17.7 %all-to-all-start = ((bf16[16,32,512]{2,1,0:T(8,128)(2,1)}), bf16[16,32,512]{2,1,0:T(8,128)(2,1)S(1)}, u32[]{:S(2)}, u32[]{:S(2)}) async-start(bf16[16,32,512]{2,1,0:T(8,128)(2,1)} %get-tuple-element.66), calls=%async_computation | async-start | bytes 1048576 | tf_op jit(solution)/shard_map/all_to_all | solution.py:504
  52.3 6.9 %collective-permute-start.15 = (bf16[512,512]{1,0:T(8,128)(2,1)}, bf16[512,512]{1,0:T(8,128)(2,1)}, u32[]{:S(2)}, u32[]{:S(2)}) collective-permute-start(bf16[512,512]{1,0:T(8,128)(2,1)} %get-tuple-element.62), channel_id=1, source_target_pairs={{0,8},{8,0},{1,9},{9,1},{2,10},{10,2},{3,11},{11,3},{4,12},{12,4},... | collective-permute-start | bytes 1572872 | tf_op jit(solution)/shard_map/ppermute | solution.py:456
  52.3 6.9 %collective-permute-start.16 = (bf16[512,512]{1,0:T(8,128)(2,1)}, bf16[512,512]{1,0:T(8,128)(2,1)}, u32[]{:S(2)}, u32[]{:S(2)}) collective-permute-start(bf16[512,512]{1,0:T(8,128)(2,1)} %get-tuple-element.63), channel_id=1, source_target_pairs={{0,8},{8,0},{1,9},{9,1},{2,10},{10,2},{3,11},{11,3},{4,12},{12,4},... | collective-permute-start | bytes 1572872 | tf_op jit(solution)/shard_map/ppermute | solution.py:456
  52.9 11.3 %collective-permute-start.13 = (bf16[256,512]{1,0:T(8,128)(2,1)}, bf16[256,512]{1,0:T(8,128)(2,1)S(1)}, u32[]{:S(2)}, u32[]{:S(2)}) collective-permute-start(bf16[256,512]{1,0:T(8,128)(2,1)} %get-tuple-element.60), channel_id=1, source_target_pairs={{0,1},{1,2},{2,3},{3,4},{4,5},{5,6},{6,7},{7,0},{8,9},{9,10},{10,1... | collective-permute-start | bytes 786440 | tf_op jit(solution)/shard_map/ppermute | solution.py:463
  54.5 9.6 %collective-permute-start.14 = (bf16[256,512]{1,0:T(8,128)(2,1)}, bf16[256,512]{1,0:T(8,128)(2,1)}, u32[]{:S(2)}, u32[]{:S(2)}) collective-permute-start(bf16[256,512]{1,0:T(8,128)(2,1)} %get-tuple-element.61), channel_id=1, source_target_pairs={{0,7},{1,0},{2,1},{3,2},{4,3},{5,4},{6,5},{7,6},{8,15},{9,8},{10,9... | collective-permute-start | bytes 786440 | tf_op jit(solution)/shard_map/ppermute | solution.py:466
  64.1 6.1 %copy-start = (bf16[1,512,512]{2,1,0:T(8,128)(2,1)S(1)}, bf16[1,512,512]{2,1,0:T(8,128)(2,1)}, u32[]{:S(2)}) copy-start(bf16[1,512,512]{2,1,0:T(8,128)(2,1)} %param.11) | copy-start | bytes 1572868
  64.2 21.2 %all-to-all-start.2 = ((bf16[16,64,512]{2,1,0:T(8,128)(2,1)}), bf16[16,64,512]{2,1,0:T(8,128)(2,1)S(1)}, u32[]{:S(2)}, u32[]{:S(2)}) async-start(bf16[16,64,512]{2,1,0:T(8,128)(2,1)} %gate.16), calls=%async_computation.2 | async-start | bytes 2097152 | tf_op jit(solution)/shard_map/all_to_all | solution.py:504
  71.3 2.0 %collective-permute-start.17 = (bf16[512,512]{1,0:T(8,128)(2,1)S(1)}, bf16[512,512]{1,0:T(8,128)(2,1)S(1)}, u32[]{:S(2)}, u32[]{:S(2)}) collective-permute-start(bf16[512,512]{1,0:T(8,128)(2,1)S(1)} %pick_other.1), channel_id=1, source_target_pairs={{0,8},{8,0},{1,9},{9,1},{2,10},{10,2},{3,11},{11,3},{4,12},{12,4},... | collective-permute-start | bytes 1572872 | tf_op jit(solution)/shard_map/ppermute | solution.py:456
  71.4 18.8 %collective-permute-start.4 = (bf16[512,512]{1,0:T(8,128)(2,1)}, bf16[512,512]{1,0:T(8,128)(2,1)}, u32[]{:S(2)}, u32[]{:S(2)}) collective-permute-start(bf16[512,512]{1,0:T(8,128)(2,1)} %get-tuple-element.48), channel_id=1, source_target_pairs={{0,8},{8,0},{1,9},{9,1},{2,10},{10,2},{3,11},{11,3},{4,12},{12,4},... | collective-permute-start | bytes 1572872 | tf_op jit(solution)/shard_map/ppermute | solution.py:456
  71.9 18.3 %collective-permute-start.5 = (bf16[512,512]{1,0:T(8,128)(2,1)}, bf16[512,512]{1,0:T(8,128)(2,1)}, u32[]{:S(2)}, u32[]{:S(2)}) collective-permute-start(bf16[512,512]{1,0:T(8,128)(2,1)} %get-tuple-element.50), channel_id=1, source_target_pairs={{0,8},{8,0},{1,9},{9,1},{2,10},{10,2},{3,11},{11,3},{4,12},{12,4},... | collective-permute-start | bytes 1572872 | tf_op jit(solution)/shard_map/ppermute | solution.py:456
  85.3 15.7 %all-to-all-start.1 = ((bf16[16,160,128]{2,1,0:T(8,128)(2,1)}), bf16[16,160,128]{2,1,0:T(8,128)(2,1)S(1)}, u32[]{:S(2)}, u32[]{:S(2)}) async-start(bf16[16,160,128]{2,1,0:T(8,128)(2,1)} %get-tuple-element.69), calls=%async_computation.1 | async-start | bytes 1310720 | tf_op jit(solution)/shard_map/all_to_all | solution.py:504
  90.2 1.0 %copy-start.1 = (bf16[512,512]{1,0:T(8,128)(2,1)S(1)}, bf16[512,512]{1,0:T(8,128)(2,1)}, u32[]{:S(2)}) copy-start(bf16[512,512]{1,0:T(8,128)(2,1)} %get-tuple-element.47.a_ref) | copy-start | bytes 1572868
  91.2 1.0 %copy-start.2 = (bf16[512,512]{1,0:T(8,128)(2,1)S(1)}, bf16[512,512]{1,0:T(8,128)(2,1)}, u32[]{:S(2)}) copy-start(bf16[512,512]{1,0:T(8,128)(2,1)} %get-tuple-element.49.c_ref) | copy-start | bytes 1572868

commit v6 on v5

--- a/solution.py
+++ b/solution.py
@@ -272,9 +272,10 @@
     def keep_copy():
         return pltpu.make_async_copy(atts.at[1], kept_refs[0], out_sems.at[2 * count])
 
-    fetch_att(0).start()
+    fetch_att(1).start()
     for index, pair in enumerate(pairs):
         keep = owns(place_ref, pair, chips) == 1
+        fetch_carried(2 * index).start()
         for piece in range(pieces):
             pl.when(keep)(fetch_mine(index, piece, True).start)
             pl.when(jnp.logical_not(keep))(fetch_mine(index, piece, False).start)
@@ -284,8 +285,7 @@
             pl.when(keep)(fetch_other(index, 0).start)
             pl.when(jnp.logical_not(keep))(fetch_other(index, 1).start)
         if index == 0:
-            fetch_att(1).start()
-        fetch_carried(2 * index).start()
+            fetch_att(0).start()
         fetch_carried(2 * index + 1).start()
     fetch_att(0).wait()
     for index in range(count):

time: 104 us -> 104 us (level)
  no operation moved by 1% of the time
where the time goes in v6:
time: 104 us; the launch traced here: 102 us
  Pallas kernels  38.6 us (37%)
  starting transfers between devices  36 us (35%)
  waiting for transfers between devices  23.9 us (23%)
  local copies, waits for them, and re-layouts  2.08 us (2%)
    pallas_call x2, Pallas kernels, attention(): pl.pallas_call(functools.partial(attention_kernel, tile=256, first=first,...  18.4 us
    all_to_all x3, starting transfers between devices, exchange(): return lax.all_to_all(array, 'dp', 0, 0, tiled=True)  18.1 us
    all_to_all x3, waiting for transfers between devices, exchange(): return lax.all_to_all(array, 'dp', 0, 0, tiled=True)  16.5 us
    pallas_call x3, Pallas kernels, weight_block(): pl.pallas_call(functools.partial(weight_kernel, pairs=pairs, pieces=piece...  12.6 us
    ppermute x4, starting transfers between devices, send_down(): return lax.ppermute(array, 'tensor', down)  12 us
    ppermute x4, waiting for transfers between devices, send_up(): return lax.ppermute(array, 'tensor', up)  6.07 us
    ppermute x4, starting transfers between devices, send_up(): return lax.ppermute(array, 'tensor', up)  3.63 us
    pallas_call x1, Pallas kernels, add_pairs(): pl.pallas_call(add_kernel, grid=(4,), in_specs=[spec] * 4, out_specs=[spe...  3.45 us
  transfers between devices with their start and end apart: 21, of which 7 were waited for; matrix products, arithmetic and copies ran while one was open for 1% of the time, Pallas kernels for 36%

profile of v6, /device:TPU:2, one launch (start us, length us, event | category | flops | bytes accessed | tf_op | source)
XLA Modules:
  0.0 102.4 jit_solution(6630537148798126817)
XLA Ops:
  0.7 0.5 collective-permute-start.1
  1.2 1.9 %collective-permute-start.2 = (bf16[512,512]{1,0:T(8,128)(2,1)}, bf16[512,512]{1,0:T(8,128)(2,1)S(1)}, u32[]{:S(2)}, u32[]{:S(2)}) collective-permute-start(bf16[512,512]{1,0:T(8,128)(2,1)} %bitcast.12), channel_id=1, source_target_pairs={{0,1},{1,2},{2,3},{3,4},{4,5},{5,6},{6,7},{7,0},{8,9},{9,10},{10,1... | collective-permute-start | bytes 1572872 | tf_op jit(solution)/shard_map/ppermute | solution.py:463
  3.1 3.9 %collective-permute-start.3 = (bf16[512,512]{1,0:T(8,128)(2,1)}, bf16[512,512]{1,0:T(8,128)(2,1)S(1)}, u32[]{:S(2)}, u32[]{:S(2)}) collective-permute-start(bf16[512,512]{1,0:T(8,128)(2,1)} %bitcast.13), channel_id=1, source_target_pairs={{0,7},{1,0},{2,1},{3,2},{4,3},{5,4},{6,5},{7,6},{8,15},{9,8},{10,9... | collective-permute-start | bytes 1572872 | tf_op jit(solution)/shard_map/ppermute | solution.py:466
  7.1 0.7 pad_add_fusion.place_ref
  7.8 9.2 %attention.2 = (bf16[512,512]{1,0:T(8,128)(2,1)S(1)}, bf16[512,512]{1,0:T(8,128)(2,1)}, bf16[512,512]{1,0:T(8,128)(2,1)}, bf16[512,512]{1,0:T(8,128)(2,1)}, bf16...) custom-call(s32[6]{0:T(128)S(1)} %pad_add_fusion.place_ref, ...), custom_call_target="tpu_custom_call" | custom-call | flops 230000000 | tf_op jit(solution)/shard_map/attention/pallas_call | solution.py:117
  17.0 2.5 %collective-permute-done.2.refs_0_ = bf16[512,512]{1,0:T(8,128)(2,1)S(1)} collective-permute-done((bf16[512,512]{1,0:T(8,128)(2,1)}, bf16[512,512]{1,0:T(8,128)(2,1)S(1)}, u32[]{:S(2)}, u32[]{:S(2)}) %collective-permute-start.2) | collective-permute-done | bytes 524320 | tf_op jit(solution)/shard_map/ppermute | solution.py:463
  19.5 3.2 %collective-permute-start.8 = (bf16[512,512]{1,0:T(8,128)(2,1)S(1)}, bf16[512,512]{1,0:T(8,128)(2,1)}, u32[]{:S(2)}, u32[]{:S(2)}) collective-permute-start(bf16[512,512]{1,0:T(8,128)(2,1)S(1)} %gate.10.refs_7_.old_up_ref.refs_5_), channel_id=1, source_target_pairs={{0,7},{1,0},{2,1},{3,2},{4,3},{5,4},{6,5},{7,6},{8,15},{9,8},{10,9... | collective-permute-start | bytes 1572872 | tf_op jit(solution)/shard_map/ppermute | solution.py:466
  22.7 9.2 %attention.3 = (bf16[512,512]{1,0:T(8,128)(2,1)S(1)}, bf16[512,512]{1,0:T(8,128)(2,1)}, bf16[512,512]{1,0:T(8,128)(2,1)}, bf16[512,512]{1,0:T(8,128)(2,1)}, bf16...) custom-call(s32[6]{0:T(128)S(1)} %pad_add_fusion.place_ref, ...), custom_call_target="tpu_custom_call", output_to_operand_aliasing={{0}: (7, {}), {1}: (8, {}), {2}: (9, {}), {3}: (10, {}), {4... | custom-call | flops 230000000 | tf_op jit(solution)/shard_map/attention/pallas_call | solution.py:117
  31.9 2.3 %collective-permute-done.6.refs_0_ = bf16[512,512]{1,0:T(8,128)(2,1)} collective-permute-done((bf16[512,512]{1,0:T(8,128)(2,1)S(1)}, bf16[512,512]{1,0:T(8,128)(2,1)}, u32[]{:S(2)}, u32[]{:S(2)}) %collective-permute-start.6) | collective-permute-done | bytes 524320 | tf_op jit(solution)/shard_map/ppermute | solution.py:463
  34.2 0.5 collective-permute-start.12
  34.8 3.2 %collective-permute-start.9 = (bf16[512,512]{1,0:T(8,128)(2,1)}, bf16[512,512]{1,0:T(8,128)(2,1)S(1)}, u32[]{:S(2)}, u32[]{:S(2)}) collective-permute-start(bf16[512,512]{1,0:T(8,128)(2,1)} %gate.12.refs_3_), channel_id=1, source_target_pairs={{0,7},{1,0},{2,1},{3,2},{4,3},{5,4},{6,5},{7,6},{8,15},{9,8},{10,9... | collective-permute-start | bytes 1572872 | tf_op jit(solution)/shard_map/ppermute | solution.py:466
  38.1 3.6 %weight_block.3 = (bf16[16,32,512]{2,1,0:T(8,128)(2,1)}, f32[2,512]{1,0:T(2,128)S(1)}, bf16[512,512]{1,0:T(8,128)(2,1)}) custom-call(s32[6]{0:T(128)S(1)} %pad_add_fusion.place_ref, bf16[512,512]{1,0:T(8,128)(2,1)} %get-tuple-element.55.refs_0_, bf16[512,512]{1,0:T(8,128)(2,1)S(1)} %collective-permute-done.10.refs_1_, ...), custom_call_target="tpu_custom_call" | custom-call | flops 115000000 | tf_op jit(solution)/shard_map/weight_block/pallas_call | solution.py:350
  41.7 7.5 %all-to-all-start = ((bf16[16,32,512]{2,1,0:T(8,128)(2,1)}), bf16[16,32,512]{2,1,0:T(8,128)(2,1)S(1)}, u32[]{:S(2)}, u32[]{:S(2)}) async-start(bf16[16,32,512]{2,1,0:T(8,128)(2,1)} %get-tuple-element.66), calls=%async_computation | async-start | bytes 1048576 | tf_op jit(solution)/shard_map/all_to_all | solution.py:504
  49.2 1.3 %collective-permute-done.7.refs_0_ = bf16[512,512]{1,0:T(8,128)(2,1)S(1)} collective-permute-done((bf16[512,512]{1,0:T(8,128)(2,1)}, bf16[512,512]{1,0:T(8,128)(2,1)S(1)}, u32[]{:S(2)}, u32[]{:S(2)}) %collective-permute-start.7) | collective-permute-done | bytes 524320 | tf_op jit(solution)/shard_map/ppermute | solution.py:463
  50.5 1.9 %fork.1 = (bf16[512,512]{1,0:T(8,128)(2,1)}, bf16[512,512]{1,0:T(8,128)(2,1)}, bf16[256,512]{1,0:T(8,128)(2,1)}, bf16[256,512]{1,0:T(8,128)(2,1)}) custom-call(s32[6]{0:T(128)S(1)} %pad_add_fusion.place_ref, bf16[512,512]{1,0:T(8,128)(2,1)S(1)} %get-tuple-element.58.down_ref.refs_1_, bf16[512,512]{1,0:T(8,128)(2,1)S(1)} %get-tuple-element.59.up_ref.refs_4_, ...), custom_call_target="tpu_custom_call" | custom-call | flops 11500000 | tf_op jit(solution)/shard_map/fork/pallas_call | solution.py:215
  52.3 0.5 collective-permute-start.16
  52.9 1.6 %collective-permute-start.13 = (bf16[256,512]{1,0:T(8,128)(2,1)}, bf16[256,512]{1,0:T(8,128)(2,1)S(1)}, u32[]{:S(2)}, u32[]{:S(2)}) collective-permute-start(bf16[256,512]{1,0:T(8,128)(2,1)} %get-tuple-element.60), channel_id=1, source_target_pairs={{0,1},{1,2},{2,3},{3,4},{4,5},{5,6},{6,7},{7,0},{8,9},{9,10},{10,1... | collective-permute-start | bytes 786440 | tf_op jit(solution)/shard_map/ppermute | solution.py:463
  54.5 1.6 %collective-permute-start.14 = (bf16[256,512]{1,0:T(8,128)(2,1)}, bf16[256,512]{1,0:T(8,128)(2,1)}, u32[]{:S(2)}, u32[]{:S(2)}) collective-permute-start(bf16[256,512]{1,0:T(8,128)(2,1)} %get-tuple-element.61), channel_id=1, source_target_pairs={{0,7},{1,0},{2,1},{3,2},{4,3},{5,4},{6,5},{7,6},{8,15},{9,8},{10,9... | collective-permute-start | bytes 786440 | tf_op jit(solution)/shard_map/ppermute | solution.py:466
  56.1 3.3 %all-to-all-done.refs_0_ = bf16[16,32,512]{2,1,0:T(8,128)(2,1)S(1)} async-done(((bf16[16,32,512]{2,1,0:T(8,128)(2,1)}), bf16[16,32,512]{2,1,0:T(8,128)(2,1)S(1)}, u32[]{:S(2)}, u32[]{:S(2)}) %all-to-all-start) | async-done | bytes 524320 | tf_op jit(solution)/shard_map/all_to_all | solution.py:504
  59.4 4.9 %weight_block.4 = (bf16[16,64,512]{2,1,0:T(8,128)(2,1)}, f32[4,512]{1,0:T(4,128)S(1)}) custom-call(s32[6]{0:T(128)S(1)} %pad_add_fusion.place_ref, bf16[512,512]{1,0:T(8,128)(2,1)S(1)} %gate.9.refs_6_.old_down_ref.refs_0_, bf16[512,512]{1,0:T(8,128)(2,1)S(1)} %get-tuple-element.58.down_ref.refs_1_, bf16[512,512]{1,0:T(8,128)(2,1)} %collective-permute-done.15.refs_2_, ...), custom_call_target="tpu_custom_call" | custom-call | flops 115000000 | tf_op jit(solution)/shard_map/weight_block/pallas_call | solution.py:350
  64.4 5.8 %all-to-all-start.2 = ((bf16[16,64,512]{2,1,0:T(8,128)(2,1)}), bf16[16,64,512]{2,1,0:T(8,128)(2,1)S(1)}, u32[]{:S(2)}, u32[]{:S(2)}) async-start(bf16[16,64,512]{2,1,0:T(8,128)(2,1)} %gate.16), calls=%async_computation.2 | async-start | bytes 2097152 | tf_op jit(solution)/shard_map/all_to_all | solution.py:504
  70.2 1.0 %pick_other.1 = bf16[512,512]{1,0:T(8,128)(2,1)S(1)} custom-call(s32[6]{0:T(128)S(1)} %pad_add_fusion.place_ref, bf16[512,512]{1,0:T(8,128)(2,1)S(1)} %bitcast.14, bf16[256,512]{1,0:T(8,128)(2,1)S(1)} %get-tuple-element.67.refs_0_.refs_2_.refs_1_, bf16[256,512]{1,0:T(8,128)(2,1)} %get-tuple-element.68.refs_1_.refs_3_.refs_2_), custom_call_target="tpu_custom_call" | custom-call | flops 11500000 | tf_op jit(solution)/shard_map/pick_other/pallas_call | solution.py:186
  71.4 0.5 collective-permute-start.4
  72.0 1.3 %collective-permute-done.17.refs_1_ = bf16[512,512]{1,0:T(8,128)(2,1)S(1)} collective-permute-done((bf16[512,512]{1,0:T(8,128)(2,1)S(1)}, bf16[512,512]{1,0:T(8,128)(2,1)S(1)}, u32[]{:S(2)}, u32[]{:S(2)}) %collective-permute-start.17) | collective-permute-done | bytes 524320 | tf_op jit(solution)/shard_map/ppermute | solution.py:456
  73.3 4.0 %weight_block.5 = (bf16[16,160,128]{2,1,0:T(8,128)(2,1)}, f32[2,512]{1,0:T(2,128)}) custom-call(s32[6]{0:T(128)S(1)} %pad_add_fusion.place_ref, bf16[512,512]{1,0:T(8,128)(2,1)S(1)} %bitcast.15, bf16[512,512]{1,0:T(8,128)(2,1)S(1)} %collective-permute-done.17.refs_1_, bf16[256,512]{1,0:T(8,128)(2,1)S(1)} %get-tuple-element.67.refs_0_.refs_2_.refs_1_, ...), custom_call_target="tpu_custom_call" | custom-call | flops 115000000 | tf_op jit(solution)/shard_map/weight_block/pallas_call | solution.py:350
  77.3 8.0 %all-to-all-done.2.refs_0_ = bf16[16,64,512]{2,1,0:T(8,128)(2,1)S(1)} async-done(((bf16[16,64,512]{2,1,0:T(8,128)(2,1)}), bf16[16,64,512]{2,1,0:T(8,128)(2,1)S(1)}, u32[]{:S(2)}, u32[]{:S(2)}) %all-to-all-start.2) | async-done | bytes 1048608 | tf_op jit(solution)/shard_map/all_to_all | solution.py:504
  85.3 4.8 %all-to-all-start.1 = ((bf16[16,160,128]{2,1,0:T(8,128)(2,1)}), bf16[16,160,128]{2,1,0:T(8,128)(2,1)S(1)}, u32[]{:S(2)}, u32[]{:S(2)}) async-start(bf16[16,160,128]{2,1,0:T(8,128)(2,1)} %get-tuple-element.69), calls=%async_computation.1 | async-start | bytes 1310720 | tf_op jit(solution)/shard_map/all_to_all | solution.py:504
  90.2 1.0 %copy-done.1 = bf16[512,512]{1,0:T(8,128)(2,1)S(1)} copy-done((bf16[512,512]{1,0:T(8,128)(2,1)S(1)}, bf16[512,512]{1,0:T(8,128)(2,1)}, u32[]{:S(2)}) %copy-start.1) | copy-done | bytes 524312
  91.2 1.0 %copy-done.2 = bf16[512,512]{1,0:T(8,128)(2,1)S(1)} copy-done((bf16[512,512]{1,0:T(8,128)(2,1)S(1)}, bf16[512,512]{1,0:T(8,128)(2,1)}, u32[]{:S(2)}) %copy-start.2) | copy-done | bytes 524312
  92.2 3.5 %add_pairs.1 = (bf16[512,512]{1,0:T(8,128)(2,1)}, bf16[512,512]{1,0:T(8,128)(2,1)}) custom-call(bf16[512,512]{1,0:T(8,128)(2,1)S(1)} %copy-done.1, bf16[512,512]{1,0:T(8,128)(2,1)} %collective-permute-done.4.b_ref, bf16[512,512]{1,0:T(8,128)(2,1)S(1)} %copy-done.2, bf16[512,512]{1,0:T(8,128)(2,1)} %collective-permute-done.5.d_ref), custom_call_target="tpu_custom_call" | custom-call | flops 115000000 | tf_op jit(solution)/shard_map/add_pairs/pallas_call | solution.py:391
  95.9 5.1 %all-to-all-done.1.last_ref = bf16[16,160,128]{2,1,0:T(8,128)(2,1)S(1)} async-done(((bf16[16,160,128]{2,1,0:T(8,128)(2,1)}), bf16[16,160,128]{2,1,0:T(8,128)(2,1)S(1)}, u32[]{:S(2)}, u32[]{:S(2)}) %all-to-all-start.1) | async-done | bytes 655392 | tf_op jit(solution)/shard_map/all_to_all | solution.py:504
  101.0 1.4 %finish.1 = (f32[8,16,512]{2,1,0:T(8,128)}, f32[8,512]{1,0:T(8,128)}) custom-call(s32[6]{0:T(128)S(1)} %pad_add_fusion.place_ref, bf16[16,160,128]{2,1,0:T(8,128)(2,1)S(1)} %all-to-all-done.1.last_ref, f32[64,512]{1,0:T(8,128)S(1)} %convert_reduce_fusion.sides_ref, f32[32,512]{1,0:T(8,128)S(1)} %convert_reduce_fusion.1.middle_ref), custom_call_target="tpu_custom_call" | custom-call | flops 115000000 | tf_op jit(solution)/shard_map/finish/pallas_call | solution.py:432
  (37 shorter events, 0.7 us)
Async XLA Ops:
  0.6 7.2 %collective-permute-start = (bf16[512,512]{1,0:T(8,128)(2,1)}, bf16[512,512]{1,0:T(8,128)(2,1)S(1)}, u32[]{:S(2)}, u32[]{:S(2)}) collective-permute-start(bf16[512,512]{1,0:T(8,128)(2,1)} %bitcast.19), channel_id=1, source_target_pairs={{0,8},{8,0},{1,9},{9,1},{2,10},{10,2},{3,11},{11,3},{4,12},{12,4},... | collective-permute-start | bytes 1572872 | tf_op jit(solution)/shard_map/ppermute | solution.py:456
  0.7 7.1 %collective-permute-start.1 = (bf16[512,512]{1,0:T(8,128)(2,1)}, bf16[512,512]{1,0:T(8,128)(2,1)S(1)}, u32[]{:S(2)}, u32[]{:S(2)}) collective-permute-start(bf16[512,512]{1,0:T(8,128)(2,1)} %bitcast.22), channel_id=1, source_target_pairs={{0,8},{8,0},{1,9},{9,1},{2,10},{10,2},{3,11},{11,3},{4,12},{12,4},... | collective-permute-start | bytes 1572872 | tf_op jit(solution)/shard_map/ppermute | solution.py:456
  1.2 18.3 %collective-permute-start.2 = (bf16[512,512]{1,0:T(8,128)(2,1)}, bf16[512,512]{1,0:T(8,128)(2,1)S(1)}, u32[]{:S(2)}, u32[]{:S(2)}) collective-permute-start(bf16[512,512]{1,0:T(8,128)(2,1)} %bitcast.12), channel_id=1, source_target_pairs={{0,1},{1,2},{2,3},{3,4},{4,5},{5,6},{6,7},{7,0},{8,9},{9,10},{10,1... | collective-permute-start | bytes 1572872 | tf_op jit(solution)/shard_map/ppermute | solution.py:463
  3.1 16.3 %collective-permute-start.3 = (bf16[512,512]{1,0:T(8,128)(2,1)}, bf16[512,512]{1,0:T(8,128)(2,1)S(1)}, u32[]{:S(2)}, u32[]{:S(2)}) collective-permute-start(bf16[512,512]{1,0:T(8,128)(2,1)} %bitcast.13), channel_id=1, source_target_pairs={{0,7},{1,0},{2,1},{3,2},{4,3},{5,4},{6,5},{7,6},{8,15},{9,8},{10,9... | collective-permute-start | bytes 1572872 | tf_op jit(solution)/shard_map/ppermute | solution.py:466
  19.5 14.7 %collective-permute-start.6 = (bf16[512,512]{1,0:T(8,128)(2,1)S(1)}, bf16[512,512]{1,0:T(8,128)(2,1)}, u32[]{:S(2)}, u32[]{:S(2)}) collective-permute-start(bf16[512,512]{1,0:T(8,128)(2,1)S(1)} %gate.9.refs_6_.old_down_ref.refs_0_), channel_id=1, source_target_pairs={{0,1},{1,2},{2,3},{3,4},{4,5},{5,6},{6,7},{7,0},{8,9},{9,10},{10,1... | collective-permute-start | bytes 1572872 | tf_op jit(solution)/shard_map/ppermute | solution.py:463
  19.5 15.2 %collective-permute-start.8 = (bf16[512,512]{1,0:T(8,128)(2,1)S(1)}, bf16[512,512]{1,0:T(8,128)(2,1)}, u32[]{:S(2)}, u32[]{:S(2)}) collective-permute-start(bf16[512,512]{1,0:T(8,128)(2,1)S(1)} %gate.10.refs_7_.old_up_ref.refs_5_), channel_id=1, source_target_pairs={{0,7},{1,0},{2,1},{3,2},{4,3},{5,4},{6,5},{7,6},{8,15},{9,8},{10,9... | collective-permute-start | bytes 1572872 | tf_op jit(solution)/shard_map/ppermute | solution.py:466
  34.2 3.8 %collective-permute-start.10 = (bf16[512,512]{1,0:T(8,128)(2,1)}, bf16[512,512]{1,0:T(8,128)(2,1)S(1)}, u32[]{:S(2)}, u32[]{:S(2)}) collective-permute-start(bf16[512,512]{1,0:T(8,128)(2,1)} %get-tuple-element.55.refs_0_), channel_id=1, source_target_pairs={{0,8},{8,0},{1,9},{9,1},{2,10},{10,2},{3,11},{11,3},{4,12},{12,4},... | collective-permute-start | bytes 1572872 | tf_op jit(solution)/shard_map/ppermute | solution.py:456
  34.2 3.8 %collective-permute-start.12 = (bf16[512,512]{1,0:T(8,128)(2,1)S(1)}, bf16[512,512]{1,0:T(8,128)(2,1)S(1)}, u32[]{:S(2)}, u32[]{:S(2)}) collective-permute-start(bf16[512,512]{1,0:T(8,128)(2,1)S(1)} %get-tuple-element.56.refs_4_.refs_6_), channel_id=1, source_target_pairs={{0,8},{8,0},{1,9},{9,1},{2,10},{10,2},{3,11},{11,3},{4,12},{12,4},... | collective-permute-start | bytes 1572872 | tf_op jit(solution)/shard_map/ppermute | solution.py:456
  34.7 3.3 %collective-permute-start.11 = (bf16[512,512]{1,0:T(8,128)(2,1)}, bf16[512,512]{1,0:T(8,128)(2,1)S(1)}, u32[]{:S(2)}, u32[]{:S(2)}) collective-permute-start(bf16[512,512]{1,0:T(8,128)(2,1)} %gate.12.refs_3_), channel_id=1, source_target_pairs={{0,8},{8,0},{1,9},{9,1},{2,10},{10,2},{3,11},{11,3},{4,12},{12,4},... | collective-permute-start | bytes 1572872 | tf_op jit(solution)/shard_map/ppermute | solution.py:456
  34.7 15.8 %collective-permute-start.7 = (bf16[512,512]{1,0:T(8,128)(2,1)}, bf16[512,512]{1,0:T(8,128)(2,1)S(1)}, u32[]{:S(2)}, u32[]{:S(2)}) collective-permute-start(bf16[512,512]{1,0:T(8,128)(2,1)} %get-tuple-element.55.refs_0_), channel_id=1, source_target_pairs={{0,1},{1,2},{2,3},{3,4},{4,5},{5,6},{6,7},{7,0},{8,9},{9,10},{10,1... | collective-permute-start | bytes 1572872 | tf_op jit(solution)/shard_map/ppermute | solution.py:463
  34.8 15.7 %collective-permute-start.9 = (bf16[512,512]{1,0:T(8,128)(2,1)}, bf16[512,512]{1,0:T(8,128)(2,1)S(1)}, u32[]{:S(2)}, u32[]{:S(2)}) collective-permute-start(bf16[512,512]{1,0:T(8,128)(2,1)} %gate.12.refs_3_), channel_id=1, source_target_pairs={{0,7},{1,0},{2,1},{3,2},{4,3},{5,4},{6,5},{7,6},{8,15},{9,8},{10,9... | collective-permute-start | bytes 1572872 | tf_op jit(solution)/shard_map/ppermute | solution.py:466
  41.7 17.7 %all-to-all-start = ((bf16[16,32,512]{2,1,0:T(8,128)(2,1)}), bf16[16,32,512]{2,1,0:T(8,128)(2,1)S(1)}, u32[]{:S(2)}, u32[]{:S(2)}) async-start(bf16[16,32,512]{2,1,0:T(8,128)(2,1)} %get-tuple-element.66), calls=%async_computation | async-start | bytes 1048576 | tf_op jit(solution)/shard_map/all_to_all | solution.py:504
  52.3 7.1 %collective-permute-start.15 = (bf16[512,512]{1,0:T(8,128)(2,1)}, bf16[512,512]{1,0:T(8,128)(2,1)}, u32[]{:S(2)}, u32[]{:S(2)}) collective-permute-start(bf16[512,512]{1,0:T(8,128)(2,1)} %get-tuple-element.62), channel_id=1, source_target_pairs={{0,8},{8,0},{1,9},{9,1},{2,10},{10,2},{3,11},{11,3},{4,12},{12,4},... | collective-permute-start | bytes 1572872 | tf_op jit(solution)/shard_map/ppermute | solution.py:456
  52.3 7.1 %collective-permute-start.16 = (bf16[512,512]{1,0:T(8,128)(2,1)}, bf16[512,512]{1,0:T(8,128)(2,1)}, u32[]{:S(2)}, u32[]{:S(2)}) collective-permute-start(bf16[512,512]{1,0:T(8,128)(2,1)} %get-tuple-element.63), channel_id=1, source_target_pairs={{0,8},{8,0},{1,9},{9,1},{2,10},{10,2},{3,11},{11,3},{4,12},{12,4},... | collective-permute-start | bytes 1572872 | tf_op jit(solution)/shard_map/ppermute | solution.py:456
  52.9 11.5 %collective-permute-start.13 = (bf16[256,512]{1,0:T(8,128)(2,1)}, bf16[256,512]{1,0:T(8,128)(2,1)S(1)}, u32[]{:S(2)}, u32[]{:S(2)}) collective-permute-start(bf16[256,512]{1,0:T(8,128)(2,1)} %get-tuple-element.60), channel_id=1, source_target_pairs={{0,1},{1,2},{2,3},{3,4},{4,5},{5,6},{6,7},{7,0},{8,9},{9,10},{10,1... | collective-permute-start | bytes 786440 | tf_op jit(solution)/shard_map/ppermute | solution.py:463
  54.5 9.9 %collective-permute-start.14 = (bf16[256,512]{1,0:T(8,128)(2,1)}, bf16[256,512]{1,0:T(8,128)(2,1)}, u32[]{:S(2)}, u32[]{:S(2)}) collective-permute-start(bf16[256,512]{1,0:T(8,128)(2,1)} %get-tuple-element.61), channel_id=1, source_target_pairs={{0,7},{1,0},{2,1},{3,2},{4,3},{5,4},{6,5},{7,6},{8,15},{9,8},{10,9... | collective-permute-start | bytes 786440 | tf_op jit(solution)/shard_map/ppermute | solution.py:466
  64.3 5.9 %copy-start = (bf16[1,512,512]{2,1,0:T(8,128)(2,1)S(1)}, bf16[1,512,512]{2,1,0:T(8,128)(2,1)}, u32[]{:S(2)}) copy-start(bf16[1,512,512]{2,1,0:T(8,128)(2,1)} %param.11) | copy-start | bytes 1572868
  64.4 20.9 %all-to-all-start.2 = ((bf16[16,64,512]{2,1,0:T(8,128)(2,1)}), bf16[16,64,512]{2,1,0:T(8,128)(2,1)S(1)}, u32[]{:S(2)}, u32[]{:S(2)}) async-start(bf16[16,64,512]{2,1,0:T(8,128)(2,1)} %gate.16), calls=%async_computation.2 | async-start | bytes 2097152 | tf_op jit(solution)/shard_map/all_to_all | solution.py:504
  71.3 2.0 %collective-permute-start.17 = (bf16[512,512]{1,0:T(8,128)(2,1)S(1)}, bf16[512,512]{1,0:T(8,128)(2,1)S(1)}, u32[]{:S(2)}, u32[]{:S(2)}) collective-permute-start(bf16[512,512]{1,0:T(8,128)(2,1)S(1)} %pick_other.1), channel_id=1, source_target_pairs={{0,8},{8,0},{1,9},{9,1},{2,10},{10,2},{3,11},{11,3},{4,12},{12,4},... | collective-permute-start | bytes 1572872 | tf_op jit(solution)/shard_map/ppermute | solution.py:456
  71.4 18.8 %collective-permute-start.4 = (bf16[512,512]{1,0:T(8,128)(2,1)}, bf16[512,512]{1,0:T(8,128)(2,1)}, u32[]{:S(2)}, u32[]{:S(2)}) collective-permute-start(bf16[512,512]{1,0:T(8,128)(2,1)} %get-tuple-element.48), channel_id=1, source_target_pairs={{0,8},{8,0},{1,9},{9,1},{2,10},{10,2},{3,11},{11,3},{4,12},{12,4},... | collective-permute-start | bytes 1572872 | tf_op jit(solution)/shard_map/ppermute | solution.py:456
  71.9 18.3 %collective-permute-start.5 = (bf16[512,512]{1,0:T(8,128)(2,1)}, bf16[512,512]{1,0:T(8,128)(2,1)}, u32[]{:S(2)}, u32[]{:S(2)}) collective-permute-start(bf16[512,512]{1,0:T(8,128)(2,1)} %get-tuple-element.50), channel_id=1, source_target_pairs={{0,8},{8,0},{1,9},{9,1},{2,10},{10,2},{3,11},{11,3},{4,12},{12,4},... | collective-permute-start | bytes 1572872 | tf_op jit(solution)/shard_map/ppermute | solution.py:456
  85.3 15.7 %all-to-all-start.1 = ((bf16[16,160,128]{2,1,0:T(8,128)(2,1)}), bf16[16,160,128]{2,1,0:T(8,128)(2,1)S(1)}, u32[]{:S(2)}, u32[]{:S(2)}) async-start(bf16[16,160,128]{2,1,0:T(8,128)(2,1)} %get-tuple-element.69), calls=%async_computation.1 | async-start | bytes 1310720 | tf_op jit(solution)/shard_map/all_to_all | solution.py:504
  90.2 1.0 %copy-start.1 = (bf16[512,512]{1,0:T(8,128)(2,1)S(1)}, bf16[512,512]{1,0:T(8,128)(2,1)}, u32[]{:S(2)}) copy-start(bf16[512,512]{1,0:T(8,128)(2,1)} %get-tuple-element.47.a_ref) | copy-start | bytes 1572868
  91.2 1.0 %copy-start.2 = (bf16[512,512]{1,0:T(8,128)(2,1)S(1)}, bf16[512,512]{1,0:T(8,128)(2,1)}, u32[]{:S(2)}) copy-start(bf16[512,512]{1,0:T(8,128)(2,1)} %get-tuple-element.49.c_ref) | copy-start | bytes 1572868
